TPU v7x, 32 devices: a whole 2x2x4 slice. The times are simulated.
32 devices in a mesh: row: 4 (over y, x), col: 8 (over z, core).
Axes of the slice: x: 2, y: 2, z: 4, core: 2. Of those that a mesh axis runs over, the one named last changes fastest.
Arguments:
- div_blocks: float32 [64, 6, 128, 128], P(('row', 'col')), may hold values from -0.5 to 0.5
- div_owner: int32 [64, 6], P(('row', 'col')), may hold values from 0 to 3, as said below
- div_local: int32 [64, 6], P(('row', 'col')), may hold values from 0 to 1
- div_count: int32 [64], P(('row', 'col')), may hold values from 2 to 6
- inv_blocks: float32 [64, 5, 128, 128], P(('row', 'col')), may hold values from -6 to 6
- inv_cols: int32 [64, 5], P(('row', 'col')), may hold values from 0 to 5, as said below
- inv_count: int32 [64], P(('row', 'col')), may hold values from 3 to 5
- schur_cols: int32 [64, 4], P(('row', 'col')), may hold values from 0 to 63, as said below
- schur_count: int32 [64], P(('row', 'col')), may hold values from 2 to 4
Outputs:
- schur_blocks: float32 [64, 4, 128, 128], P(('row', 'col'))
Inputs may be any that keep to these rules, and one draw needn't show every extreme that they name: `div_owner`: over all 6 slots of the 2 rows of one device, live or not, at most 3 name the same owner, and exactly 3 do for some owner on every device. `inv_cols`: the columns of one row are distinct. `schur_cols`: slot 0 of row p is p itself, slot 1 another row of the same subdomain, slot 2 a row of the subdomain with the same a and c + 1 mod 8, slot 3 one of the subdomain with c - 1 mod 8.
All inputs are finite; a program needn't handle non-finite values.
Results may differ from a plain program's by a relative error of at most 0.0003.
Values sent between devices are 32-bit elements; how exact they have to be, the bound alone decides.
No kernel may reach another device: no remote copies, remote signals or barrier semaphores. Data moves between devices by JAX's collectives and lax.ppermute only.
A program may use at most 128 MiB of HBM per device.

v0:
```python
import jax
import jax.numpy as jnp
from jax import lax
from jax.sharding import PartitionSpec as P


def extended(block, sides, width):
    for axis, dim in sides:
        count = lax.axis_size(axis)
        forward = [(i, i + 1) for i in range(count - 1)]
        forward.append((count - 1, 0))
        backward = [(target, source) for source, target in forward]
        low = lax.ppermute(
            lax.slice_in_dim(block, block.shape[dim] - width, None, axis=dim), axis, forward
        )
        high = lax.ppermute(lax.slice_in_dim(block, 0, width, axis=dim), axis, backward)
        block = jnp.concatenate([low, block, high], axis=dim)
    return block


def local(
    div_blocks,
    div_owner,
    div_local,
    div_count,
    inv_blocks,
    inv_cols,
    inv_count,
    schur_cols,
    schur_count,
):
    rows_here = div_blocks.shape[0]
    slots_row = div_blocks.shape[1]
    block_side = div_blocks.shape[2]
    vel_here = inv_cols.shape[0]
    inv_slots = inv_cols.shape[1]
    pattern = schur_cols.shape[1]
    owner_count = lax.axis_size("row")
    lon_devices = lax.axis_size("col")
    listed = rows_here * slots_row
    capacity = max(2, -(-listed // owner_count))
    spaces = owner_count * capacity
    device = lax.axis_index("row") * lon_devices + lax.axis_index("col")
    press_ids = device * rows_here + jnp.arange(rows_here, dtype=jnp.int32)
    slot_live = jnp.arange(slots_row, dtype=jnp.int32)[None, :] < div_count[:, None]
    live_flat = slot_live.reshape(listed)
    target = div_owner.reshape(listed)
    positions = jnp.arange(listed, dtype=jnp.int32)
    before = (
        (positions[None, :] < positions[:, None])
        & live_flat[None, :]
        & (target[None, :] == target[:, None])
    )
    slot_rank = jnp.sum(before.astype(jnp.int32), axis=1)
    position = target * capacity + slot_rank
    placed = (position[:, None] == jnp.arange(spaces, dtype=jnp.int32)[None, :]) & live_flat[
        :, None
    ]
    placed_int = placed.astype(jnp.int32)
    source_slot = jnp.sum(placed_int * positions[:, None], axis=0)
    filled = jnp.sum(placed_int, axis=0) > 0
    flat_blocks = div_blocks.reshape(listed, block_side, block_side)
    outgoing = jnp.where(filled[:, None, None], jnp.take(flat_blocks, source_slot, axis=0), 0.0)
    pattern_live = jnp.arange(pattern, dtype=jnp.int32)[None, :] < schur_count[:, None]
    targets = jnp.where(pattern_live, schur_cols, -1)
    slot_meta = jnp.concatenate(
        [
            (div_local + 1)[:, :, None],
            jnp.broadcast_to(press_ids[:, None, None], (rows_here, slots_row, 1)),
            jnp.broadcast_to(targets[:, None, :], (rows_here, slots_row, pattern)),
        ],
        axis=2,
    ).reshape(listed, 2 + pattern)
    meta_out = jnp.sum(placed_int[:, :, None] * slot_meta[:, None, :], axis=0)
    arrived, meta_in = (
        lax.all_to_all(outgoing, "row", split_axis=0, concat_axis=0, tiled=True),
        lax.all_to_all(meta_out, "row", split_axis=0, concat_axis=0, tiled=True),
    )
    ext_blocks, ext_meta = (
        extended(arrived, (("col", 0),), spaces),
        extended(meta_in, (("col", 0),), spaces),
    )
    ext_cols = 3 * vel_here
    inv_live = jnp.arange(inv_slots, dtype=jnp.int32)[None, :] < inv_count[:, None]
    select_cols = (
        (inv_cols[:, :, None] == jnp.arange(ext_cols, dtype=jnp.int32)[None, None, :])
        & inv_live[:, :, None]
    ).astype(jnp.float32)
    dense_inv = jnp.einsum(
        "ukv,ukpq->uvpq", select_cols, inv_blocks, precision=lax.Precision.HIGHEST
    )
    own_live = meta_in[:, 0] > 0
    own_vel = meta_in[:, 0] - 1
    own_targets = meta_in[:, 2:]
    pick_rows = (own_vel[:, None] == jnp.arange(vel_here, dtype=jnp.int32)[None, :]) & own_live[
        :, None
    ]
    region_ids = jnp.arange(3 * spaces, dtype=jnp.int32) // spaces
    ext_live = ext_meta[:, 0] > 0
    column_index = region_ids * vel_here + jnp.maximum(ext_meta[:, 0] - 1, 0)
    chosen = jnp.take(dense_inv, column_index, axis=1)
    products = jnp.einsum("ugpq,grq->ugpr", chosen, ext_blocks, precision=lax.Precision.HIGHEST)
    matches = (
        (ext_meta[None, None, :, 1] == own_targets[:, :, None])
        & (own_targets[:, :, None] >= 0)
        & ext_live[None, None, :]
    )
    weight = (pick_rows[:, None, :, None] & matches[:, :, None, :]).astype(jnp.float32)
    factors = jnp.einsum("stug,ugpr->stpr", weight, products, precision=lax.Precision.HIGHEST)
    answer = jnp.einsum("spq,stqr->stpr", arrived, factors, precision=lax.Precision.HIGHEST)
    returned = lax.all_to_all(answer, "row", split_axis=0, concat_axis=0, tiled=True)
    taken = jnp.take(returned, position, axis=0)
    taken = jnp.where(live_flat[:, None, None, None], taken, 0.0)
    schur_blocks = jnp.sum(
        taken.reshape(rows_here, slots_row, pattern, block_side, block_side), axis=1
    )
    return schur_blocks


def solution(mesh):
    placed = (
        P(("row", "col"), None, None, None),
        P(("row", "col"), None),
        P(("row", "col"), None),
        P(("row", "col")),
        P(("row", "col"), None, None, None),
        P(("row", "col"), None),
        P(("row", "col")),
        P(("row", "col"), None),
        P(("row", "col")),
    )
    return jax.shard_map(
        local,
        mesh=mesh,
        in_specs=placed,
        out_specs=P(("row", "col"), None, None, None),
        check_vma=False,
    )
```

profile of v0, /device:TPU:0, one launch (start us, length us, event | category | flops | bytes accessed | tf_op | source)
XLA Modules:
  0.0 125.4 jit_solution(1676557309332054511)
XLA Ops:
  0.0 0.0 copy-start
  0.0 0.8 iota_compare_fusion.4
  0.8 0.1 lt.120
  0.9 0.8 reshape.282
  1.7 0.2 convert_reduce_fusion
  1.8 0.1 broadcast_in_dim.62
  1.9 0.1 broadcast_in_dim.63
  2.0 0.7 broadcast_add_fusion
  2.7 0.1 concatenate.14
  2.8 0.8 compare_select_fusion.5
  3.5 0.1 copy.76
  3.6 0.1 broadcast_in_dim.102
  3.7 0.1 concatenate.15
  3.8 0.1 copy.77
  3.9 0.1 fusion.34
  4.0 0.1 multiply_reduce_fusion
  4.0 0.1 copy.78
  4.1 0.6 all_to_all.14
  4.8 5.2 %all-to-all-start = ((s32[4,3,6]{2,1,0:T(4,128)}), s32[4,3,6]{2,1,0:T(4,128)S(1)}, u32[]{:S(2)}, u32[]{:S(2)}) async-start(s32[4,3,6]{2,1,0:T(4,128)} %all_to_all.14), calls=%async_computation | async-start | bytes 16384 | tf_op jit(solution)/shard_map/all_to_all | solution.py:77
  9.9 0.1 fusion.40
  10.0 0.7 iota_compare_fusion.3
  10.8 0.1 copy.83
  10.8 0.1 fusion.29
  11.0 0.0 copy-done
  11.0 0.6 gather_fusion
  11.6 2.0 %fusion.22 = f32[2,6,128,128]{3,1,2,0:T(8,128)S(1)} fusion(f32[2,5,128,128]{3,2,1,0:T(8,128)} %param.13, s32[2,5]{1,0:T(2,128)} %param.14, pred[2,5]{1,0:T(4,128)(4,1)S(1)} %iota_compare_fusion.3), kind=kOutput, calls=%fused_computation.21 | convolution fusion | flops 11796600 | bytes 1441842 | tf_op jit(solution)/shard_map/ukv,ukpq->uvpq/dot_general | solution.py:89
  13.6 1.0 select_select_fusion
  14.7 0.2 copy.87
  14.8 0.0 all-to-all-done
  14.8 4.2 %all-to-all-start.1 = ((f32[12,128,128]{2,1,0:T(8,128)}), f32[12,128,128]{2,1,0:T(8,128)S(1)}, u32[]{:S(2)}, u32[]{:S(2)}) async-start(f32[12,128,128]{2,1,0:T(8,128)} %select_select_fusion), calls=%async_computation.1 | async-start | bytes 1572864 | tf_op jit(solution)/shard_map/all_to_all | solution.py:76
  19.1 0.1 compare_reduce_fusion
  19.2 0.1 copy.80
  19.3 2.2 %collective-permute-start.1 = (s32[12,6]{1,0:T(8,128)S(1)}, s32[12,6]{1,0:T(8,128)S(1)}, u32[]{:S(2)}, u32[]{:S(2)}) collective-permute-start(s32[12,6]{1,0:T(8,128)S(1)} %all_to_all.16), channel_id=1, source_target_pairs={{1,0},{2,1},{3,2},{4,3},{5,4},{6,5},{7,6},{0,7},{9,8},{10,9},{11,1... | collective-permute-start | bytes 872 | tf_op jit(solution)/shard_map/ppermute | solution.py:16
  21.5 0.0 collective-permute-start
  21.5 0.1 add_reduce_fusion
  21.6 1.2 collective-permute-done.1
  22.8 0.1 copy.81
  22.9 3.4 %collective-permute-done = s32[12,6]{1,0:T(8,128)S(1)} collective-permute-done((s32[12,6]{1,0:T(8,128)S(1)}, s32[12,6]{1,0:T(8,128)S(1)}, u32[]{:S(2)}, u32[]{:S(2)}) %collective-permute-start) | collective-permute-done | bytes 320 | tf_op jit(solution)/shard_map/ppermute | solution.py:13
  26.4 0.1 copy.79
  26.4 2.9 %all-to-all-done.1 = f32[12,128,128]{2,1,0:T(8,128)S(1)} async-done(((f32[12,128,128]{2,1,0:T(8,128)}), f32[12,128,128]{2,1,0:T(8,128)S(1)}, u32[]{:S(2)}, u32[]{:S(2)}) %all-to-all-start.1) | async-done | bytes 786464 | tf_op jit(solution)/shard_map/all_to_all | solution.py:76
  29.3 2.2 %collective-permute-start.3 = (f32[12,128,128]{2,1,0:T(8,128)S(1)}, f32[12,128,128]{2,1,0:T(8,128)S(1)}, u32[]{:S(2)}, u32[]{:S(2)}) collective-permute-start(f32[12,128,128]{2,1,0:T(8,128)S(1)} %all-to-all-done.1), channel_id=1, source_target_pairs={{1,0},{2,1},{3,2},{4,3},{5,4},{6,5},{7,6},{0,7},{9,8},{10,9},{11,1... | collective-permute-start | bytes 2359304 | tf_op jit(solution)/shard_map/ppermute | solution.py:16
  31.5 0.0 collective-permute-start.2
  31.5 0.1 pad_add_fusion
  31.7 3.0 %gather_fusion.1 = f32[36,2,128,128]{3,2,1,0:T(8,128)} fusion(f32[2,6,128,128]{3,2,1,0:T(8,128)S(1)} %copy.87, s32[1024]{0:T(1024)S(1)} %pad_clamp_fusion.1), kind=kCustom, calls=%fused_computation.1 | custom fusion | bytes 9437328 | tf_op jit(solution)/shard_map/jit(_take)/gather | solution.py:101
  34.7 0.1 and_and_fusion
  34.8 13.5 %collective-permute-done.3 = f32[12,128,128]{2,1,0:T(8,128)S(1)} collective-permute-done((f32[12,128,128]{2,1,0:T(8,128)S(1)}, f32[12,128,128]{2,1,0:T(8,128)S(1)}, u32[]{:S(2)}, u32[]{:S(2)}) %collective-permute-start.3) | collective-permute-done | bytes 786464 | tf_op jit(solution)/shard_map/ppermute | solution.py:16
  48.3 3.1 %collective-permute-done.2 = f32[12,128,128]{2,1,0:T(8,128)} collective-permute-done((f32[12,128,128]{2,1,0:T(8,128)S(1)}, f32[12,128,128]{2,1,0:T(8,128)}, u32[]{:S(2)}, u32[]{:S(2)}) %collective-permute-start.2) | collective-permute-done | bytes 786464 | tf_op jit(solution)/shard_map/ppermute | solution.py:13
  51.4 9.1 %fusion.13 = f32[2,36,128,128]{2,3,0,1:T(8,128)} fusion(f32[36,2,128,128]{3,2,1,0:T(8,128)} %gather_fusion.1, pred[36]{0:T(512)(128)(4,1)S(1)} %get-tuple-element.7, f32[12,128,128]{2,1,0:T(8,128)S(1)} %collective-permute-done.3, f32[12,128,128]{2,1,0:T(8,128)S(1)} %all-to-all-done.1, f32[12,128,128]{2,1,0:T(8,128)} %collective-permute-done.2), kind=kOutput, calls=%fused_computation.18 | convolution fusion | flops 1814298624 | bytes 11796516 | tf_op jit(solution)/shard_map/ugpq,grq->ugpr/dot_general | solution.py:102
  60.5 6.3 %copy.88 = f32[2,36,128,128]{3,1,0,2:T(8,128)} copy(f32[2,36,128,128]{2,3,0,1:T(8,128)} %fusion.13) | data formatting | bytes 9437184 | tf_op jit(solution)/shard_map/ugpq,grq->ugpr/transpose | solution.py:102
  66.9 5.3 %fusion.16 = f32[12,4,128,128]{3,0,2,1:T(8,128)S(1)} fusion(f32[2,36,128,128]{3,1,0,2:T(8,128)} %copy.88, pred[12,4,36]{2,0,1:T(8,128)(4,1)S(1)} %and_and_fusion, pred[12,2]{0,1:T(4,128)(4,1)S(1)} %compare_and_fusion.1), kind=kOutput, calls=%fused_computation.19 | convolution fusion | flops 679480704 | bytes 7866072 | tf_op jit(solution)/shard_map/stug,ugpr->stpr/dot_general | solution.py:109
  72.2 7.7 %fusion.19 = f32[12,4,128,128]{2,3,1,0:T(8,128)} fusion(f32[12,4,128,128]{3,0,2,1:T(8,128)S(1)} %fusion.16, f32[12,128,128]{2,1,0:T(8,128)S(1)} %all-to-all-done.1), kind=kOutput, calls=%fused_computation.20 | convolution fusion | flops 1207959552 | bytes 7077888 | tf_op jit(solution)/shard_map/spq,stqr->stpr/dot_general | solution.py:110
  79.9 0.0 copy-start.1
  79.9 4.8 %all-to-all-start.2 = ((f32[12,4,128,128]{2,3,1,0:T(8,128)}), f32[12,4,128,128]{2,3,1,0:T(8,128)}, u32[]{:S(2)}, u32[]{:S(2)}) async-start(f32[12,4,128,128]{2,3,1,0:T(8,128)} %fusion.19), calls=%async_computation.2 | async-start | bytes 6291456 | tf_op jit(solution)/shard_map/all_to_all | solution.py:111
  84.6 0.1 reduce_sum.52
  84.7 0.0 copy-done.1
  84.7 0.1 mul.74
  84.8 0.1 copy.91
  84.9 0.1 fusion.30
  85.0 32.6 %all-to-all-done.2 = f32[12,4,128,128]{2,3,1,0:T(8,128)} async-done(((f32[12,4,128,128]{2,3,1,0:T(8,128)}), f32[12,4,128,128]{2,3,1,0:T(8,128)}, u32[]{:S(2)}, u32[]{:S(2)}) %all-to-all-start.2) | async-done | bytes 3145760 | tf_op jit(solution)/shard_map/all_to_all | solution.py:111
  117.6 4.3 %gather_fusion.2 = f32[12,4,128,128]{2,3,1,0:T(8,128)} fusion(f32[12,4,128,128]{2,3,1,0:T(8,128)} %all-to-all-done.2, s32[1024]{0:T(1024)S(1)} %pad_clamp_fusion), kind=kCustom, calls=%fused_computation.2 | custom fusion | bytes 6291504 | tf_op jit(solution)/shard_map/jit(_take)/gather | solution.py:112
  122.0 2.4 %select_reduce_fusion = f32[2,4,128,128]{2,3,1,0:T(8,128)S(1)} fusion(f32[2,6,4,128,128]{3,4,2,1,0:T(8,128)} %bitcast.55, pred[2,6]{1,0:T(4,128)(4,1)S(1)} %compare_and_fusion.2, pred[2,6]{1,0:T(4,128)(4,1)S(1)} %iota_compare_fusion.4), kind=kLoop, calls=%fused_computation.10 | loop fusion | flops 2228224 | bytes 3670040 | tf_op jit(solution)/shard_map/reduce_sum | solution.py:114
  124.4 1.0 copy.92
  (15 shorter events, 0.1 us)
Async XLA Ops:
  0.0 11.0 %copy-start = (f32[2,6,128,128]{3,2,1,0:T(8,128)S(1)}, f32[2,6,128,128]{3,2,1,0:T(8,128)}, u32[]{:S(2)}) copy-start(f32[2,6,128,128]{3,2,1,0:T(8,128)} %param.9) | copy-start | bytes 2359300
  4.8 10.1 %all-to-all-start = ((s32[4,3,6]{2,1,0:T(4,128)}), s32[4,3,6]{2,1,0:T(4,128)S(1)}, u32[]{:S(2)}, u32[]{:S(2)}) async-start(s32[4,3,6]{2,1,0:T(4,128)} %all_to_all.14), calls=%async_computation | async-start | bytes 16384 | tf_op jit(solution)/shard_map/all_to_all | solution.py:77
  14.8 14.5 %all-to-all-start.1 = ((f32[12,128,128]{2,1,0:T(8,128)}), f32[12,128,128]{2,1,0:T(8,128)S(1)}, u32[]{:S(2)}, u32[]{:S(2)}) async-start(f32[12,128,128]{2,1,0:T(8,128)} %select_select_fusion), calls=%async_computation.1 | async-start | bytes 1572864 | tf_op jit(solution)/shard_map/all_to_all | solution.py:76
  19.3 3.6 %collective-permute-start.1 = (s32[12,6]{1,0:T(8,128)S(1)}, s32[12,6]{1,0:T(8,128)S(1)}, u32[]{:S(2)}, u32[]{:S(2)}) collective-permute-start(s32[12,6]{1,0:T(8,128)S(1)} %all_to_all.16), channel_id=1, source_target_pairs={{1,0},{2,1},{3,2},{4,3},{5,4},{6,5},{7,6},{0,7},{9,8},{10,9},{11,1... | collective-permute-start | bytes 872 | tf_op jit(solution)/shard_map/ppermute | solution.py:16
  21.5 4.9 %collective-permute-start = (s32[12,6]{1,0:T(8,128)S(1)}, s32[12,6]{1,0:T(8,128)S(1)}, u32[]{:S(2)}, u32[]{:S(2)}) collective-permute-start(s32[12,6]{1,0:T(8,128)S(1)} %all_to_all.16), channel_id=1, source_target_pairs={{0,1},{1,2},{2,3},{3,4},{4,5},{5,6},{6,7},{7,0},{8,9},{9,10},{10,1... | collective-permute-start | bytes 872 | tf_op jit(solution)/shard_map/ppermute | solution.py:13
  29.3 19.0 %collective-permute-start.3 = (f32[12,128,128]{2,1,0:T(8,128)S(1)}, f32[12,128,128]{2,1,0:T(8,128)S(1)}, u32[]{:S(2)}, u32[]{:S(2)}) collective-permute-start(f32[12,128,128]{2,1,0:T(8,128)S(1)} %all-to-all-done.1), channel_id=1, source_target_pairs={{1,0},{2,1},{3,2},{4,3},{5,4},{6,5},{7,6},{0,7},{9,8},{10,9},{11,1... | collective-permute-start | bytes 2359304 | tf_op jit(solution)/shard_map/ppermute | solution.py:16
  31.5 19.9 %collective-permute-start.2 = (f32[12,128,128]{2,1,0:T(8,128)S(1)}, f32[12,128,128]{2,1,0:T(8,128)}, u32[]{:S(2)}, u32[]{:S(2)}) collective-permute-start(f32[12,128,128]{2,1,0:T(8,128)S(1)} %all-to-all-done.1), channel_id=1, source_target_pairs={{0,1},{1,2},{2,3},{3,4},{4,5},{5,6},{6,7},{7,0},{8,9},{9,10},{10,1... | collective-permute-start | bytes 2359304 | tf_op jit(solution)/shard_map/ppermute | solution.py:13
  79.9 4.9 %copy-start.1 = (s32[2,6]{1,0:T(2,128)S(1)}, s32[2,6]{1,0:T(2,128)}, u32[]{:S(2)}) copy-start(s32[2,6]{1,0:T(2,128)} %param.10) | copy-start | bytes 148
  79.9 37.8 %all-to-all-start.2 = ((f32[12,4,128,128]{2,3,1,0:T(8,128)}), f32[12,4,128,128]{2,3,1,0:T(8,128)}, u32[]{:S(2)}, u32[]{:S(2)}) async-start(f32[12,4,128,128]{2,3,1,0:T(8,128)} %fusion.19), calls=%async_computation.2 | async-start | bytes 6291456 | tf_op jit(solution)/shard_map/all_to_all | solution.py:111
where the time goes:
time: 126 us; the launch traced here: 125 us
  waiting for transfers between devices  56.7 us (45%)
  matrix products  24.1 us (19%)
  starting transfers between devices  18.6 us (15%)
  local copies, waits for them, and re-layouts  18.2 us (14%)
  other arithmetic  7.57 us (6%)
    all_to_all x1, waiting for transfers between devices, local(): lax.all_to_all(answer, 'row', split_axis=0, concat_axis=0, tiled=True)  32.6 us
    ppermute x2, waiting for transfers between devices, extended(): lax.ppermute(lax.slice_in_dim(block, 0, width, axis=dim), axis, backward)  14.8 us
    dot_general x1, matrix products, local(): jnp.einsum('ugpq,grq->ugpr', chosen, ext_blocks, precision=lax.Precision....  9.11 us
    dot_general x1, matrix products, local(): jnp.einsum('spq,stqr->stpr', arrived, factors, precision=lax.Precision.HI...  7.65 us
    ppermute x2, waiting for transfers between devices, extended(): lax.ppermute(lax.slice_in_dim(block, block.shape[dim] - width, None, axis...  6.53 us
    transpose x1, local copies, waits for them, and re-layouts, local(): jnp.einsum('ugpq,grq->ugpr', chosen, ext_blocks, precision=lax.Precision....  6.34 us
    dot_general x1, matrix products, local(): jnp.einsum('stug,ugpr->stpr', weight, products, precision=lax.Precision.H...  5.33 us
    all_to_all x1, starting transfers between devices, local(): lax.all_to_all(meta_out, 'row', split_axis=0, concat_axis=0, tiled=True)  5.17 us
  transfers between devices with their start and end apart: 7, of which 6 were waited for; matrix products, arithmetic and copies ran while one was open for 7% of the time, Pallas kernels for 0%

commit v1 on v0

v1 whole, which is shorter than its diff:
```python
import functools

import jax
import jax.numpy as jnp
from jax import lax
from jax.experimental import pallas as pl
from jax.experimental.pallas import tpu as pltpu
from jax.sharding import PartitionSpec as P

F32 = jnp.float32
BF16 = jnp.bfloat16
VMEM = pl.BlockSpec(memory_space=pltpu.VMEM)
SMEM = pl.BlockSpec(memory_space=pltpu.SMEM)
HALO, TARGETS = 32, 64


def halves(value):
    high = value.astype(BF16)
    return high, (value - high.astype(F32)).astype(BF16)


def product(left, right, transposed=False):
    dims = (((1,), (1 if transposed else 0,)), ((), ()))
    dot = functools.partial(lax.dot_general, dimension_numbers=dims, preferred_element_type=F32)
    return dot(left[0], right[0]) + (dot(left[0], right[1]) + dot(left[1], right[0]))


def clear(ref):
    ref[...] = jnp.zeros(ref.shape, ref.dtype)


def place_div(codes, blocks, sizes, dense):
    rows, slots, _, _, side = sizes
    for row in range(rows):
        for slot in range(slots):
            code = codes[row * slots + slot]

            @pl.when(code >= 0)
            def _():
                dense[code, pl.ds(row * side, side), :] += blocks[pl.ds((row * slots + slot) * side, side), :]


def place_inv(codes, blocks, sizes, high, low, first=0):
    _, _, width, slots, side = sizes
    for row in range(width):
        for slot in range(slots):
            code = codes[first + row * slots + slot]

            @pl.when(code >= 0)
            def _():
                spot = (pl.ds(row * side, side), pl.ds(pl.multiple_of(code * side, side), side))
                high[spot], low[spot] = halves(blocks[pl.ds((row * slots + slot) * side, side), :])


def owner_part(dense, owner, width):
    return halves(jnp.concatenate([dense[owner * width + i] for i in range(width)], axis=1))


def write(out, region_sums, meta):
    rows, pattern, side, _ = out.shape
    for row in range(rows):
        for slot in range(pattern):
            code = meta[row * pattern + slot]
            values = region_sums[(1, 1, 2, 0)[slot]][row * side : (row + 1) * side, :]
            result = jnp.zeros((side, side), F32)
            for other in range(rows):
                result = jnp.where(code == other, values[:, other * side : (other + 1) * side], result)
            out[row, slot] = result


def kernel_pack(row_axis, div, inv, owner, velocity, d_count, cols, m_count, targets, s_count, d_out, m_out, *scratch):
    tables, (m_sem, d_sem, sems) = scratch[:-3], scratch[-3:]
    d_rows, m_rows = div.shape[0], inv.shape[0]
    big = [
        pltpu.make_async_copy(inv, m_out.at[pl.ds(0, m_rows)], m_sem),
        pltpu.make_async_copy(div, d_out.at[pl.ds(0, d_rows)], d_sem),
    ]
    small = [
        pltpu.make_async_copy(source, table, sems.at[i])
        for i, (source, table) in enumerate(zip((owner, velocity, d_count, cols, m_count, targets, s_count), tables))
    ]
    for copy in big + small:
        copy.start()
    for copy in small:
        copy.wait()
    owner, velocity, d_count, cols, m_count, targets, s_count = tables
    row, col = (lax.axis_index(name) for name in row_axis)
    rows, slots = owner.shape
    width, inv_slots = cols.shape
    pattern = targets.shape[1]
    lane = lax.broadcasted_iota(jnp.int32, (8, 128), 1)

    def tile(codes):
        values = jnp.full((8, 128), -1, jnp.int32)
        for spot, code in codes:
            values = jnp.where(lane == spot, code, values)
        return values.astype(F32)

    codes = []
    for i in range(rows):
        for k in range(slots):
            apart = owner[i, k] ^ row
            swapped = ((apart & 1) << 1) | (apart >> 1)
            live = k < d_count[i]
            even, odd = (jnp.where(live, x * width + velocity[i, k], -1) for x in (apart, swapped))
            here = jnp.where(col % 2 == 0, even, odd)
            there = jnp.where(col % 2 == 0, odd, even)
            codes += [(i * slots + k, here), (HALO + i * slots + k, there)]
        for t in range(pattern):
            codes.append((TARGETS + i * pattern + t, jnp.where(t < s_count[i], targets[i, t] % rows, -1)))
    d_out[pl.ds(d_rows, 8), :] = tile(codes)
    m_out[pl.ds(m_rows, 8), :] = tile(
        (u * inv_slots + m, jnp.where(m < m_count[u], cols[u, m], -1)) for u in range(width) for m in range(inv_slots)
    )
    for copy in big:
        copy.wait()


def integers(packed, table, sem):
    copy = pltpu.make_async_copy(packed.at[pl.ds(packed.shape[0] - 8, 8)], table, sem)
    copy.start()
    return copy


class Row:
    def __init__(self, table, first=0):
        self.table, self.first = table, first

    def __getitem__(self, i):
        return self.table[0, self.first + i].astype(jnp.int32)


def kernel_own(sizes, div, inv, b_high, b_low, y_high, y_low, s_own, dense, m_high, m_low, d_table, m_table, sems):
    rows, slots, width, inv_slots, side = sizes
    copies = [integers(div, d_table, sems.at[0]), integers(inv, m_table, sems.at[1])]
    clear(dense)
    clear(m_high)
    clear(m_low)
    for copy in copies:
        copy.wait()
    place_div(Row(d_table), div, sizes, dense)
    for owner in range(dense.shape[0] // width):
        b_high[owner], b_low[owner] = owner_part(dense, owner, width)
    place_inv(Row(m_table), inv, sizes, m_high, m_low)
    own = (b_high[0], b_low[0])
    y_high[...], y_low[...] = halves(product(own, (m_high[...], m_low[...])))
    size = own[0].shape[1]
    s_own[...] = product((y_high[:, size : 2 * size], y_low[:, size : 2 * size]), own, True)


def kernel_side(which, sizes, inv, b_high, b_low, s_in, y_high, y_low, s_out, m_high, m_low, m_table, sem):
    copy = integers(inv, m_table, sem)
    clear(m_high)
    clear(m_low)
    copy.wait()
    place_inv(Row(m_table), inv, sizes, m_high, m_low)
    part = (b_high[which], b_low[which])
    y_high[...], y_low[...] = halves(product(part, (m_high[...], m_low[...])))
    size = part[0].shape[1]
    s_out[...] = s_in[...] + product((y_high[:, size : 2 * size], y_low[:, size : 2 * size]), part, True)


def kernel_halo(sizes, prev, follow, *refs):
    ys, (s_prev, s_next, p_high, p_low, n_high, n_low, dense, p_table, n_table, sems) = refs[:6], refs[6:]
    width = sizes[2]
    size = p_high.shape[1]
    copies = [integers(prev, p_table, sems.at[0]), integers(follow, n_table, sems.at[1])]
    clear(dense)
    for copy in copies:
        copy.wait()
    place_div(Row(p_table, HALO), prev, sizes, dense.at[0])
    place_div(Row(n_table, HALO), follow, sizes, dense.at[1])
    for i, (total, high, low, start) in enumerate(((s_prev, p_high, p_low, 0), (s_next, n_high, n_low, 2 * size))):
        for owner in range(3):
            part = owner_part(dense.at[i], owner, width)
            left = (ys[2 * owner][:, start : start + size], ys[2 * owner + 1][:, start : start + size])
            term = product(left, part, True)
            total[...] = term if owner == 0 else total[...] + term
        high[...], low[...] = owner_part(dense.at[i], 3, width)


def kernel_last(sizes, inv, div, b_high, b_low, p_high, p_low, n_high, n_low, s_own, s_prev, s_next, out, *scratch):
    m_high, m_low, m_table, d_table, sems = scratch
    copies = [integers(inv, m_table, sems.at[0]), integers(div, d_table, sems.at[1])]
    clear(m_high)
    clear(m_low)
    for copy in copies:
        copy.wait()
    place_inv(Row(m_table), inv, sizes, m_high, m_low)
    own = (b_high[3], b_low[3])
    y_high, y_low = halves(product(own, (m_high[...], m_low[...])))
    size = own[0].shape[1]
    sums = []
    for region, (part, total) in enumerate(
        (((p_high[...], p_low[...]), s_prev), (own, s_own), ((n_high[...], n_low[...]), s_next))
    ):
        cut = slice(region * size, (region + 1) * size)
        sums.append(total[...] + product((y_high[:, cut], y_low[:, cut]), part, True))
    write(out, sums, Row(d_table, TARGETS))


def kernel_all(sizes, d_meta, p_meta, n_meta, m_meta, s_meta, div, prev, follow, inv, out, dense, sums, m_high, m_low):
    _, _, width, slots, _ = sizes
    clear(dense)
    clear(sums)
    for region, (meta, blocks) in enumerate(((p_meta, prev), (d_meta, div), (n_meta, follow))):
        place_div(meta, blocks, sizes, dense.at[region])

    @pl.loop(0, inv.shape[0])
    def _(owner):
        clear(m_high)
        clear(m_low)
        place_inv(m_meta, inv.at[owner], sizes, m_high, m_low, owner * width * slots)
        size = m_high.shape[0]
        own = owner_part(dense.at[1], owner, width)
        y_high, y_low = halves(product(own, (m_high[...], m_low[...])))
        for region in range(3):
            cut = slice(region * size, (region + 1) * size)
            sums[region] += product((y_high[:, cut], y_low[:, cut]), owner_part(dense.at[region], owner, width), True)

    write(out, [sums[region] for region in range(3)], s_meta)


def call(kernel, operands, outs, scratch, flops, scalars=0, specs=None, limit=24 << 20):
    moved = sum(x.size * x.dtype.itemsize for x in operands[scalars:] + outs)
    return pl.pallas_call(
        kernel,
        out_shape=outs if len(outs) > 1 else outs[0],
        in_specs=specs or [SMEM] * scalars + [VMEM] * (len(operands) - scalars),
        out_specs=[VMEM] * len(outs) if len(outs) > 1 else VMEM,
        scratch_shapes=scratch,
        compiler_params=pltpu.CompilerParams(vmem_limit_bytes=limit),
        cost_estimate=pl.CostEstimate(flops=flops, bytes_accessed=moved, transcendentals=0),
    )(*operands)


def local(div_blocks, div_owner, div_local, div_count, inv_blocks, inv_cols, inv_count, schur_cols, schur_count):
    rows, slots, side, _ = div_blocks.shape
    width, inv_slots = inv_cols.shape
    pattern = schur_cols.shape[1]
    owners = lax.axis_size("row")
    count = lax.axis_size("col")
    size, wide = width * side, 3 * width * side
    sizes = (rows, slots, width, inv_slots, side)
    forward = [(i, (i + 1) % count) for i in range(count)]
    backward = [(i, (i - 1) % count) for i in range(count)]
    div_flat = div_blocks.reshape(rows * slots * side, side)
    inv_flat = inv_blocks.reshape(width * inv_slots * side, side)

    square = jax.ShapeDtypeStruct((rows * side, rows * side), F32)
    half = jax.ShapeDtypeStruct((rows * side, size), BF16)
    every = jax.ShapeDtypeStruct((owners, rows * side, size), BF16)
    y_half = jax.ShapeDtypeStruct((rows * side, wide), BF16)
    result = jax.ShapeDtypeStruct((rows, pattern, side, side), F32)
    m_half = pltpu.VMEM((size, wide), BF16)
    one = 2 * 3 * rows * side * size * wide

    if owners != 4 or count % 2 or side != 128:

        def order(length):
            return jnp.arange(length, dtype=jnp.int32)[None, :]

        d_meta = jnp.where(order(slots) < div_count[:, None], div_owner * width + div_local, -1).reshape(-1)
        m_meta = jnp.where(order(inv_slots) < inv_count[:, None], inv_cols, -1).reshape(-1)
        s_meta = jnp.where(order(pattern) < schur_count[:, None], schur_cols % rows, -1).reshape(-1)
        prev = lax.ppermute(div_flat, "col", forward)
        follow = lax.ppermute(div_flat, "col", backward)
        p_meta = lax.ppermute(d_meta, "col", forward)
        n_meta = lax.ppermute(d_meta, "col", backward)
        inv = lax.all_gather(inv_flat, "row")
        all_meta = lax.all_gather(m_meta, "row", tiled=True)
        return call(
            functools.partial(kernel_all, sizes),
            [d_meta, p_meta, n_meta, all_meta, s_meta, div_flat, prev, follow, inv],
            [result],
            [
                pltpu.VMEM((3, owners * width, rows * side, side), F32),
                pltpu.VMEM((3, rows * side, rows * side), F32),
                m_half,
                m_half,
            ],
            owners * one * 2,
            scalars=5,
            limit=56 << 20,
        )

    def swap(first):
        def partner(r, c):
            return r ^ (1 if (c % 2 == 0) == first else 2)

        return [(r * count + c, partner(r, c) * count + c) for r in range(owners) for c in range(count)]

    table = pltpu.SMEM((8, 128), F32)
    tables = (div_owner, div_local, div_count, inv_cols, inv_count, schur_cols, schur_count)
    div, inv = call(
        functools.partial(kernel_pack, ("row", "col")),
        [div_flat, inv_flat, *tables],
        [jax.ShapeDtypeStruct((x.shape[0] + 8, side), F32) for x in (div_flat, inv_flat)],
        [pltpu.SMEM(x.shape, x.dtype) for x in tables]
        + [pltpu.SemaphoreType.DMA, pltpu.SemaphoreType.DMA, pltpu.SemaphoreType.DMA((len(tables),))],
        0,
        specs=[pl.BlockSpec(memory_space=pl.ANY)] * (2 + len(tables)),
        limit=60 << 20,
    )
    inv_1 = lax.ppermute(inv, ("row", "col"), swap(True))
    inv_2 = lax.ppermute(inv, ("row", "col"), swap(False))
    prev = lax.ppermute(div, "col", forward)
    follow = lax.ppermute(div, "col", backward)
    inv_3 = lax.ppermute(inv_1, ("row", "col"), swap(False))

    pair = pltpu.SemaphoreType.DMA((2,))
    b_high, b_low, y0_high, y0_low, s_own = call(
        functools.partial(kernel_own, sizes),
        [div, inv],
        [every, every, y_half, y_half, square],
        [pltpu.VMEM((owners * width, rows * side, side), F32), m_half, m_half, table, table, pair],
        one * 4 // 3,
    )
    y1_high, y1_low, s_own = call(
        functools.partial(kernel_side, 1, sizes),
        [inv_1, b_high, b_low, s_own],
        [y_half, y_half, square],
        [m_half, m_half, table, pltpu.SemaphoreType.DMA],
        one * 4 // 3,
    )
    y2_high, y2_low, s_own = call(
        functools.partial(kernel_side, 2, sizes),
        [inv_2, b_high, b_low, s_own],
        [y_half, y_half, square],
        [m_half, m_half, table, pltpu.SemaphoreType.DMA],
        one * 4 // 3,
    )
    s_prev, s_next, p_high, p_low, n_high, n_low = call(
        functools.partial(kernel_halo, sizes),
        [prev, follow, y0_high, y0_low, y1_high, y1_low, y2_high, y2_low],
        [square, square, half, half, half, half],
        [pltpu.VMEM((2, owners * width, rows * side, side), F32), table, table, pair],
        one * 2,
    )
    return call(
        functools.partial(kernel_last, sizes),
        [inv_3, div, b_high, b_low, p_high, p_low, n_high, n_low, s_own, s_prev, s_next],
        [result],
        [m_half, m_half, table, table, pair],
        one * 2,
    )


def solution(mesh):
    blocks = P(("row", "col"), None, None, None)
    table = P(("row", "col"), None)
    line = P(("row", "col"))
    return jax.shard_map(
        local,
        mesh=mesh,
        in_specs=(blocks, table, table, line, blocks, table, line, table, line),
        out_specs=blocks,
        check_vma=False,
    )
```

time: 126 us -> 33.1 us (0.26)
  waiting for transfers between devices: 56.7 us -> 10.3 us
  matrix products: 24.1 us -> 0 us
  local copies, waits for them, and re-layouts: 18.2 us -> 2.23 us
  Pallas kernels: 0 us -> 11.8 us
  starting transfers between devices: 18.6 us -> 8.45 us
  other arithmetic: 7.57 us -> 0 us
    all_to_all x3 -> x0, waiting for transfers between devices: 35.4 us -> none  [the longest x1 32.6 us: local(): lax.all_to_all(answer, 'row', split_axis=0, concat_axis=0, tiled=True)]
    dot_general x4 -> x0, matrix products: 24.1 us -> none  [the longest x1 9.11 us: local(): jnp.einsum('ugpq,grq->ugpr', chosen, ext_blocks, precision=lax.Precision....]
    all_to_all x3 -> x0, starting transfers between devices: 14.1 us -> none  [the longest x1 5.17 us: local(): lax.all_to_all(meta_out, 'row', split_axis=0, concat_axis=0, tiled=True)]
    pallas_call x0 -> x6, Pallas kernels: none -> 11.8 us  [call(): pl.pallas_call(kernel, out_shape=outs if len(outs) > 1 else outs[0], in_s...]
    ppermute x4 -> x5, waiting for transfers between devices: 21.3 us -> 10.3 us  [the longest x1 10.3 us: local(): inv_1 = lax.ppermute(inv, ('row', 'col'), swap(True))]
    gather x3 -> x0, local copies, waits for them, and re-layouts: 7.96 us -> none  [the longest x1 4.34 us: local(): taken = jnp.take(returned, position, axis=0)]
    transpose x1 -> x0, local copies, waits for them, and re-layouts: 6.34 us -> none  [local(): jnp.einsum('ugpq,grq->ugpr', chosen, ext_blocks, precision=lax.Precision....]
    ppermute x4 -> x5, starting transfers between devices: 4.43 us -> 8.45 us  [the longest x1 3 us: local(): inv_1 = lax.ppermute(inv, ('row', 'col'), swap(True))]
  transfers between devices with their start and end apart: 7 -> 5, of which waited for: 6 -> 1; matrix products, arithmetic and copies ran while one was open for 7% -> 0% of each run, Pallas kernels for 0% -> 20%
where the time goes in v1:
time: 33.1 us; the launch traced here: 32.9 us
  Pallas kernels  11.8 us (36%)
  waiting for transfers between devices  10.3 us (31%)
  starting transfers between devices  8.45 us (26%)
  local copies, waits for them, and re-layouts  2.23 us (7%)
    pallas_call x6, Pallas kernels, call(): pl.pallas_call(kernel, out_shape=outs if len(outs) > 1 else outs[0], in_s...  11.8 us
    ppermute x1, waiting for transfers between devices, local(): inv_1 = lax.ppermute(inv, ('row', 'col'), swap(True))  10.3 us
    ppermute x1, starting transfers between devices, local(): inv_1 = lax.ppermute(inv, ('row', 'col'), swap(True))  3 us
    ppermute x1, starting transfers between devices, local(): follow = lax.ppermute(div, 'col', backward)  2.79 us
    unnamed x6, local copies, waits for them, and re-layouts  2.23 us
    ppermute x1, starting transfers between devices, local(): inv_3 = lax.ppermute(inv_1, ('row', 'col'), swap(False))  2.14 us
  transfers between devices with their start and end apart: 5, of which 1 were waited for; matrix products, arithmetic and copies ran while one was open for 0% of the time, Pallas kernels for 20%

profile of v1, /device:TPU:0, one launch (start us, length us, event | category | flops | bytes accessed | tf_op | source)
XLA Modules:
  0.0 32.9 jit_solution(18030048169378516464)
XLA Ops:
  0.0 2.5 %shard_map.91 = (f32[1544,128]{1,0:T(8,128)}, f32[1288,128]{1,0:T(8,128)}) custom-call(f32[1536,128]{1,0:T(8,128)} %bitcast.2, f32[1280,128]{1,0:T(8,128)} %bitcast.3, s32[2,6]{1,0:T(2,128)} %owner.1, s32[2,6]{1,0:T(2,128)} %velocity.1, s32[2]{0:T(128)} %d_count.1, s32[2,5]{1,0:T(2,128)} %cols.1, s32[2]{0:T(128)} %m_count.1, s32[2,4]{1,0:T(2,128)} %targets.1, ...), custom_call_target="tpu_custom_call" | custom-call | bytes 2891968 | tf_op jit(solution)/shard_map/pallas_call | solution.py:226
  2.5 3.0 %collective-permute-start = (f32[1288,128]{1,0:T(8,128)}, f32[1288,128]{1,0:T(8,128)S(1)}, u32[]{:S(2)}, u32[]{:S(2)}) collective-permute-start(f32[1288,128]{1,0:T(8,128)} %get-tuple-element.24.inv), channel_id=1, source_target_pairs={{0,8},{1,17},{2,10},{3,19},{4,12},{5,21},{6,14},{7,23},{8,0},{9,25... | collective-permute-start | bytes 1978376 | tf_op jit(solution)/shard_map/ppermute | solution.py:305
  5.5 2.8 %collective-permute-start.3 = (f32[1544,128]{1,0:T(8,128)}, f32[1544,128]{1,0:T(8,128)S(1)}, u32[]{:S(2)}, u32[]{:S(2)}) collective-permute-start(f32[1544,128]{1,0:T(8,128)} %get-tuple-element.25.div), channel_id=1, source_target_pairs={{0,7},{1,0},{2,1},{3,2},{4,3},{5,4},{6,5},{7,6},{8,15},{9,8},{10,9... | collective-permute-start | bytes 2371592 | tf_op jit(solution)/shard_map/ppermute | solution.py:308
  8.3 0.0 collective-permute-start.2
  8.3 0.5 %collective-permute-start.4 = (f32[1288,128]{1,0:T(8,128)}, f32[1288,128]{1,0:T(8,128)S(1)}, u32[]{:S(2)}, u32[]{:S(2)}) collective-permute-start(f32[1288,128]{1,0:T(8,128)} %get-tuple-element.24.inv), channel_id=1, source_target_pairs={{0,16},{1,9},{2,18},{3,11},{4,20},{5,13},{6,22},{7,15},{8,24},{9,1... | collective-permute-start | bytes 1978376 | tf_op jit(solution)/shard_map/ppermute | solution.py:306
  8.8 10.3 %collective-permute-done.inv = f32[1288,128]{1,0:T(8,128)S(1)} collective-permute-done((f32[1288,128]{1,0:T(8,128)}, f32[1288,128]{1,0:T(8,128)S(1)}, u32[]{:S(2)}, u32[]{:S(2)}) %collective-permute-start) | collective-permute-done | bytes 659488 | tf_op jit(solution)/shard_map/ppermute | solution.py:305
  19.1 2.1 %collective-permute-start.1 = (f32[1288,128]{1,0:T(8,128)S(1)}, f32[1288,128]{1,0:T(8,128)S(1)}, u32[]{:S(2)}, u32[]{:S(2)}) collective-permute-start(f32[1288,128]{1,0:T(8,128)S(1)} %collective-permute-done.inv), channel_id=1, source_target_pairs={{0,16},{1,9},{2,18},{3,11},{4,20},{5,13},{6,22},{7,15},{8,24},{9,1... | collective-permute-start | bytes 1978376 | tf_op jit(solution)/shard_map/ppermute | solution.py:309
  21.3 0.0 copy-start
  21.3 1.1 %copy-done = f32[1544,128]{1,0:T(8,128)S(1)} copy-done((f32[1544,128]{1,0:T(8,128)S(1)}, f32[1544,128]{1,0:T(8,128)}, u32[]{:S(2)}) %copy-start) | copy-done | bytes 790552
  22.4 0.0 copy-start.2
  22.4 1.1 %copy-done.2 = f32[1288,128]{1,0:T(8,128)S(1)} copy-done((f32[1288,128]{1,0:T(8,128)S(1)}, f32[1288,128]{1,0:T(8,128)}, u32[]{:S(2)}) %copy-start.2) | copy-done | bytes 659480
  23.5 1.8 %shard_map.92 = (bf16[4,256,256]{2,1,0:T(8,128)(2,1)S(1)}, bf16[4,256,256]{2,1,0:T(8,128)(2,1)S(1)}, bf16[256,768]{1,0:T(8,128)(2,1)S(1)}, bf16[256,768]{1,0:T(8,128)(2,1)S(1)}, f32[256,256]{1,0:T(8,128)S(1)}) custom-call(f32[1544,128]{1,0:T(8,128)S(1)} %copy-done, f32[1288,128]{1,0:T(8,128)S(1)} %copy-done.2), custom_call_target="tpu_custom_call" | custom-call | flops 402653184 | bytes 3547136 | tf_op jit(solution)/shard_map/pallas_call | solution.py:226
  25.4 1.4 %shard_map.93 = (bf16[256,768]{1,0:T(8,128)(2,1)S(1)}, bf16[256,768]{1,0:T(8,128)(2,1)S(1)}, f32[256,256]{1,0:T(8,128)S(1)}) custom-call(f32[1288,128]{1,0:T(8,128)S(1)} %collective-permute-done.inv, bf16[4,256,256]{2,1,0:T(8,128)(2,1)S(1)} %get-tuple-element.26.b_high, bf16[4,256,256]{2,1,0:T(8,128)(2,1)S(1)} %get-tuple-element.27.b_low, ...), custom_call_target="tpu_custom_call" | custom-call | flops 402653184 | bytes 3018752 | tf_op jit(solution)/shard_map/pallas_call | solution.py:226
  26.8 0.0 collective-permute-done.4.inv
  26.8 1.5 %shard_map.94 = (bf16[256,768]{1,0:T(8,128)(2,1)S(1)}, bf16[256,768]{1,0:T(8,128)(2,1)S(1)}, f32[256,256]{1,0:T(8,128)S(1)}) custom-call(f32[1288,128]{1,0:T(8,128)S(1)} %collective-permute-done.4.inv, bf16[4,256,256]{2,1,0:T(8,128)(2,1)S(1)} %get-tuple-element.26.b_high, bf16[4,256,256]{2,1,0:T(8,128)(2,1)S(1)} %get-tuple-element.27.b_low, ...), custom_call_target="tpu_custom_call" | custom-call | flops 402653184 | bytes 3018752 | tf_op jit(solution)/shard_map/pallas_call | solution.py:226
  28.3 0.0 collective-permute-done.3.follow
  28.3 0.0 collective-permute-done.2.prev
  28.3 0.0 copy-start.1
  28.3 1.9 %shard_map.95 = (f32[256,256]{1,0:T(8,128)S(1)}, f32[256,256]{1,0:T(8,128)S(1)}, bf16[256,256]{1,0:T(8,128)(2,1)S(1)}, bf16[256,256]{1,0:T(8,128)(2,1)S(1)}, bf1...) custom-call(f32[1544,128]{1,0:T(8,128)S(1)} %collective-permute-done.2.prev, ...), custom_call_target="tpu_custom_call" | custom-call | flops 603979776 | bytes 4988928 | tf_op jit(solution)/shard_map/pallas_call | solution.py:226
  30.2 0.0 collective-permute-done.1.inv
  30.2 0.0 copy-done.1
  30.3 2.6 %shard_map.96 = f32[2,4,128,128]{3,2,1,0:T(8,128)} custom-call(f32[1288,128]{1,0:T(8,128)S(1)} %collective-permute-done.1.inv, f32[1544,128]{1,0:T(8,128)S(1)} %copy-done.1, bf16[4,256,256]{2,1,0:T(8,128)(2,1)S(1)} %get-tuple-element.26.b_high, bf16[4,256,256]{2,1,0:T(8,128)(2,1)S(1)} %get-tuple-element.27.b_low, ...), custom_call_target="tpu_custom_call" | custom-call | flops 603979776 | bytes 4333568 | tf_op jit(solution)/shard_map/pallas_call | solution.py:226
Async XLA Ops:
  2.5 16.6 %collective-permute-start = (f32[1288,128]{1,0:T(8,128)}, f32[1288,128]{1,0:T(8,128)S(1)}, u32[]{:S(2)}, u32[]{:S(2)}) collective-permute-start(f32[1288,128]{1,0:T(8,128)} %get-tuple-element.24.inv), channel_id=1, source_target_pairs={{0,8},{1,17},{2,10},{3,19},{4,12},{5,21},{6,14},{7,23},{8,0},{9,25... | collective-permute-start | bytes 1978376 | tf_op jit(solution)/shard_map/ppermute | solution.py:305
  5.5 22.8 %collective-permute-start.3 = (f32[1544,128]{1,0:T(8,128)}, f32[1544,128]{1,0:T(8,128)S(1)}, u32[]{:S(2)}, u32[]{:S(2)}) collective-permute-start(f32[1544,128]{1,0:T(8,128)} %get-tuple-element.25.div), channel_id=1, source_target_pairs={{0,7},{1,0},{2,1},{3,2},{4,3},{5,4},{6,5},{7,6},{8,15},{9,8},{10,9... | collective-permute-start | bytes 2371592 | tf_op jit(solution)/shard_map/ppermute | solution.py:308
  8.3 20.0 %collective-permute-start.2 = (f32[1544,128]{1,0:T(8,128)}, f32[1544,128]{1,0:T(8,128)S(1)}, u32[]{:S(2)}, u32[]{:S(2)}) collective-permute-start(f32[1544,128]{1,0:T(8,128)} %get-tuple-element.25.div), channel_id=1, source_target_pairs={{0,1},{1,2},{2,3},{3,4},{4,5},{5,6},{6,7},{7,0},{8,9},{9,10},{10,1... | collective-permute-start | bytes 2371592 | tf_op jit(solution)/shard_map/ppermute | solution.py:307
  8.3 18.5 %collective-permute-start.4 = (f32[1288,128]{1,0:T(8,128)}, f32[1288,128]{1,0:T(8,128)S(1)}, u32[]{:S(2)}, u32[]{:S(2)}) collective-permute-start(f32[1288,128]{1,0:T(8,128)} %get-tuple-element.24.inv), channel_id=1, source_target_pairs={{0,16},{1,9},{2,18},{3,11},{4,20},{5,13},{6,22},{7,15},{8,24},{9,1... | collective-permute-start | bytes 1978376 | tf_op jit(solution)/shard_map/ppermute | solution.py:306
  19.1 11.1 %collective-permute-start.1 = (f32[1288,128]{1,0:T(8,128)S(1)}, f32[1288,128]{1,0:T(8,128)S(1)}, u32[]{:S(2)}, u32[]{:S(2)}) collective-permute-start(f32[1288,128]{1,0:T(8,128)S(1)} %collective-permute-done.inv), channel_id=1, source_target_pairs={{0,16},{1,9},{2,18},{3,11},{4,20},{5,13},{6,22},{7,15},{8,24},{9,1... | collective-permute-start | bytes 1978376 | tf_op jit(solution)/shard_map/ppermute | solution.py:309
  21.3 1.1 %copy-start = (f32[1544,128]{1,0:T(8,128)S(1)}, f32[1544,128]{1,0:T(8,128)}, u32[]{:S(2)}) copy-start(f32[1544,128]{1,0:T(8,128)} %get-tuple-element.25.div) | copy-start | bytes 2371588
  22.4 1.1 %copy-start.2 = (f32[1288,128]{1,0:T(8,128)S(1)}, f32[1288,128]{1,0:T(8,128)}, u32[]{:S(2)}) copy-start(f32[1288,128]{1,0:T(8,128)} %get-tuple-element.24.inv) | copy-start | bytes 1978372
  28.3 1.9 %copy-start.1 = (f32[1544,128]{1,0:T(8,128)S(1)}, f32[1544,128]{1,0:T(8,128)}, u32[]{:S(2)}) copy-start(f32[1544,128]{1,0:T(8,128)} %get-tuple-element.25.div) | copy-start | bytes 2371588

commit v2 on v1

v2 whole, which is shorter than its diff:
```python
import functools

import jax
import jax.numpy as jnp
from jax import lax
from jax.experimental import pallas as pl
from jax.experimental.pallas import tpu as pltpu
from jax.sharding import PartitionSpec as P

F32 = jnp.float32
BF16 = jnp.bfloat16
VMEM = pl.BlockSpec(memory_space=pltpu.VMEM)
SMEM = pl.BlockSpec(memory_space=pltpu.SMEM)
PACK_LIMIT = 60 << 20
PARTS = 4


def halves(value):
    high = value.astype(BF16)
    return high, (value - high.astype(F32)).astype(BF16)


def product(left, right, transposed=False):
    dims = (((1,), (1 if transposed else 0,)), ((), ()))
    dot = functools.partial(lax.dot_general, dimension_numbers=dims, preferred_element_type=F32)
    return dot(left[0], right[0]) + (dot(left[0], right[1]) + dot(left[1], right[0]))


def clear(ref):
    ref[...] = jnp.zeros(ref.shape, ref.dtype)


def place_div(codes, blocks, sizes, dense):
    rows, slots, _, _, side = sizes
    for row in range(rows):
        for slot in range(slots):
            code = codes[row * slots + slot]

            @pl.when(code >= 0)
            def _():
                dense[code, pl.ds(row * side, side), :] += blocks[pl.ds((row * slots + slot) * side, side), :]


def place_inv(codes, blocks, sizes, high, low):
    _, _, width, slots, side = sizes
    for row in range(width):
        for slot in range(slots):
            code = codes[row * slots + slot]

            @pl.when(code >= 0)
            def _():
                spot = (pl.ds(row * side, side), pl.ds(pl.multiple_of(code * side, side), side))
                high[spot], low[spot] = halves(blocks[pl.ds((row * slots + slot) * side, side), :])


def owner_part(dense, owner, width):
    return halves(jnp.concatenate([dense[owner * width + i] for i in range(width)], axis=1))


def write(out, buf, sums, slots, codes, sems):
    rows, pattern, side, _ = out.shape
    copies = []
    for row in range(rows):
        for slot in slots:
            code = codes[row * pattern + slot]
            result = jnp.zeros((side, side), F32)
            for other in range(rows):
                block = sums[row * side : (row + 1) * side, other * side : (other + 1) * side]
                result = jnp.where(code == other, block, result)
            buf[row, slot] = result
            copies.append(pltpu.make_async_copy(buf.at[row, slot], out.at[row, slot], sems.at[row, slot]))
            copies[-1].start()
    return copies


def fetch(sources, targets, sems):
    copies = [pltpu.make_async_copy(x, y, sems.at[i]) for i, (x, y) in enumerate(zip(sources, targets))]
    for copy in copies:
        copy.start()
    return copies


def kernel_pack(inv, div, *refs):
    tables, (inv_out, div_out, tile_out), scratch = refs[:7], refs[7:10], refs[10:]
    small_refs, (inv_buf, div_buf, small_sem, in_sem, out_sem) = scratch[:7], scratch[7:]
    small = fetch(tables, small_refs, small_sem)
    parts = in_sem.shape[1]
    arrays = ((inv, inv_buf, inv_out), (div, div_buf, div_out))
    cuts = [[pl.ds(j * (x.shape[0] // parts), x.shape[0] // parts) for j in range(parts)] for x in (inv, div)]
    reads, writes = [], []
    for i, (blocks, buf, out) in enumerate(arrays):
        reads += fetch([blocks.at[cut] for cut in cuts[i]], [buf.at[cut] for cut in cuts[i]], in_sem.at[i])
    for copy in small:
        copy.wait()
    for i, tables in enumerate((small_refs[:2], small_refs[2:])):
        _, buf, out = arrays[i]
        at = rows = buf.shape[0] - 8
        buf[pl.ds(rows, 8), :] = jnp.zeros((8, buf.shape[1]), F32)
        for table in tables:
            values = table[...].astype(F32)
            height, length = (1, *values.shape)[-2:]
            buf[pl.ds(at, height), pl.ds(0, length)] = values.reshape(height, length)
            at += height
        cuts[i].append(pl.ds(rows, 8))
    tile = pltpu.make_async_copy(inv_buf.at[cuts[0][-1]], tile_out, small_sem.at[0])
    tile.start()
    writes.append(tile)
    for i, (_, buf, out) in enumerate(arrays):
        for j, cut in enumerate(cuts[i]):
            if j < parts:
                reads[i * parts + j].wait()
            copy = pltpu.make_async_copy(buf.at[cut], out.at[cut], out_sem.at[i, j])
            copy.start()
            writes.append(copy)
    for copy in writes:
        copy.wait()


def integers(packed):
    return packed[pl.ds(packed.shape[0] - 8, 8), :].astype(jnp.int32)


def inv_codes(table, sizes):
    _, _, width, slots, _ = sizes
    codes = []
    for u in range(width):
        count = table[width, u]
        codes += [jnp.where(m < count, table[u, m], -1) for m in range(slots)]
    return codes


def div_codes(table, sizes):
    rows, slots, width, _, _ = sizes
    mine = lax.axis_index("row")
    odd = lax.axis_index("col") % 2
    codes = []
    for i in range(rows):
        count = table[3 * rows, i]
        for k in range(slots):
            apart = table[i, k] ^ mine
            apart = jnp.where(odd == 1, ((apart & 1) << 1) | (apart >> 1), apart)
            code = apart * width + table[rows + i, k]
            codes.append(jnp.where(k < count, code, -1))
    return codes


def target_codes(table, rows, pattern):
    codes = []
    for i in range(rows):
        count = table[3 * rows + 1, i]
        codes += [jnp.where(t < count, table[2 * rows + i, t] % rows, -1) for t in range(pattern)]
    return codes


def read_inv(inv, tile, sizes, m_high, m_low):
    clear(m_high)
    clear(m_low)
    place_inv(inv_codes(integers(tile), sizes), inv, sizes, m_high, m_low)


def kernel_own(sizes, div, inv, b_high, b_low, y_high, y_low, s_own, dense, m_high, m_low):
    clear(dense)
    read_inv(inv, inv, sizes, m_high, m_low)
    place_div(div_codes(integers(div), sizes), div, sizes, dense)
    for owner in range(b_high.shape[0]):
        b_high[owner], b_low[owner] = owner_part(dense, owner, sizes[2])
    own = (b_high[0], b_low[0])
    y_high[...], y_low[...] = halves(product(own, (m_high[...], m_low[...])))
    size = own[0].shape[1]
    s_own[...] = product((y_high[:, size : 2 * size], y_low[:, size : 2 * size]), own, True)


def kernel_side(which, sizes, inv, tile, b_high, b_low, s_in, y_high, y_low, s_out, m_high, m_low):
    read_inv(inv, tile, sizes, m_high, m_low)
    part = (b_high[which], b_low[which])
    y_high[...], y_low[...] = halves(product(part, (m_high[...], m_low[...])))
    size = part[0].shape[1]
    s_out[...] = s_in[...] + product((y_high[:, size : 2 * size], y_low[:, size : 2 * size]), part, True)


def kernel_next(sizes, y0_high, y0_low, y1_high, y1_low, y2_high, y2_low, div, s_next, n_high, n_low, dense):
    clear(dense)
    place_div(div_codes(integers(div), sizes), div, sizes, dense)
    size = n_high.shape[1]
    cut = slice(2 * size, 3 * size)
    for owner, (high, low) in enumerate(((y0_high, y0_low), (y1_high, y1_low), (y2_high, y2_low))):
        term = product((high[:, cut], low[:, cut]), owner_part(dense, owner, sizes[2]), True)
        s_next[...] = term if owner == 0 else s_next[...] + term
    n_high[...], n_low[...] = owner_part(dense, 3, sizes[2])


def kernel_far(
    sizes, inv, tile, div, b_high, b_low, n_high, n_low, s_own, s_next, out, y3_high, y3_low, m_high, m_low, buf, out_sem
):
    read_inv(inv, tile, sizes, m_high, m_low)
    codes = target_codes(integers(div), *out.shape[:2])
    own = (b_high[3], b_low[3])
    y_high, y_low = halves(product(own, (m_high[...], m_low[...])))
    size = own[0].shape[1]
    y3_high[...], y3_low[...] = y_high[:, :size], y_low[:, :size]
    cut = slice(size, 2 * size)
    own_sum = s_own[...] + product((y_high[:, cut], y_low[:, cut]), own, True)
    copies = write(out, buf, own_sum, (0, 1), codes, out_sem)
    cut = slice(2 * size, 3 * size)
    next_sum = s_next[...] + product((y_high[:, cut], y_low[:, cut]), (n_high[...], n_low[...]), True)
    copies += write(out, buf, next_sum, (2,), codes, out_sem)
    for copy in copies:
        copy.wait()


def kernel_prev(sizes, ready, div, own, *refs):
    ys, (out, buf, dense, out_sem) = refs[:8], refs[8:]
    clear(dense)
    place_div(div_codes(integers(div), sizes), div, sizes, dense)
    size = dense.shape[1]
    total = None
    for owner in range(4):
        term = product((ys[2 * owner][:, :size], ys[2 * owner + 1][:, :size]), owner_part(dense, owner, sizes[2]), True)
        total = term if owner == 0 else total + term
    for copy in write(out, buf, total, (3,), target_codes(integers(own), *out.shape[:2]), out_sem):
        copy.wait()


def kernel_all(sizes, d_meta, p_meta, n_meta, m_meta, s_meta, div, prev, follow, inv, out, dense, sums, m_high, m_low, buf, out_sem):
    _, _, width, slots, _ = sizes
    clear(dense)
    clear(sums)
    for region, (meta, blocks) in enumerate(((p_meta, prev), (d_meta, div), (n_meta, follow))):
        place_div(meta, blocks, sizes, dense.at[region])

    @pl.loop(0, inv.shape[0])
    def _(owner):
        clear(m_high)
        clear(m_low)
        codes = [m_meta[owner * width * slots + i] for i in range(width * slots)]
        place_inv(codes, inv.at[owner], sizes, m_high, m_low)
        size = m_high.shape[0]
        own = owner_part(dense.at[1], owner, width)
        y_high, y_low = halves(product(own, (m_high[...], m_low[...])))
        for region in range(3):
            cut = slice(region * size, (region + 1) * size)
            sums[region] += product((y_high[:, cut], y_low[:, cut]), owner_part(dense.at[region], owner, width), True)

    codes = [s_meta[i] for i in range(out.shape[0] * out.shape[1])]
    for slots, region in (((0, 1), 1), ((2,), 2), ((3,), 0)):
        for copy in write(out, buf, sums[region], slots, codes, out_sem):
            copy.wait()


def call(kernel, operands, outs, scratch, flops, scalars=0, specs=None, out_specs=None, aliases=None, limit=24 << 20):
    moved = sum(x.size * x.dtype.itemsize for x in operands[scalars:] + outs)
    return pl.pallas_call(
        kernel,
        out_shape=outs if len(outs) > 1 else outs[0],
        in_specs=specs or [SMEM] * scalars + [VMEM] * (len(operands) - scalars),
        out_specs=out_specs or ([VMEM] * len(outs) if len(outs) > 1 else VMEM),
        scratch_shapes=scratch,
        input_output_aliases=aliases or {},
        compiler_params=pltpu.CompilerParams(vmem_limit_bytes=limit),
        cost_estimate=pl.CostEstimate(flops=flops, bytes_accessed=moved, transcendentals=0),
    )(*operands)


def local(div_blocks, div_owner, div_local, div_count, inv_blocks, inv_cols, inv_count, schur_cols, schur_count):
    rows, slots, side, _ = div_blocks.shape
    width, inv_slots = inv_cols.shape
    pattern = schur_cols.shape[1]
    owners = lax.axis_size("row")
    count = lax.axis_size("col")
    size, wide = width * side, 3 * width * side
    sizes = (rows, slots, width, inv_slots, side)
    forward = [(i, (i + 1) % count) for i in range(count)]
    backward = [(i, (i - 1) % count) for i in range(count)]
    div_flat = div_blocks.reshape(rows * slots * side, side)
    inv_flat = inv_blocks.reshape(width * inv_slots * side, side)

    square = jax.ShapeDtypeStruct((rows * side, rows * side), F32)
    half = jax.ShapeDtypeStruct((rows * side, size), BF16)
    every = jax.ShapeDtypeStruct((owners, rows * side, size), BF16)
    y_half = jax.ShapeDtypeStruct((rows * side, wide), BF16)
    result = jax.ShapeDtypeStruct((rows, pattern, side, side), F32)
    m_half = pltpu.VMEM((size, wide), BF16)
    one = 2 * 3 * rows * side * size * wide

    if owners != 4 or count % 2 or rows != 2 or side != 128:

        def order(length):
            return jnp.arange(length, dtype=jnp.int32)[None, :]

        d_meta = jnp.where(order(slots) < div_count[:, None], div_owner * width + div_local, -1).reshape(-1)
        m_meta = jnp.where(order(inv_slots) < inv_count[:, None], inv_cols, -1).reshape(-1)
        s_meta = jnp.where(order(pattern) < schur_count[:, None], schur_cols % rows, -1).reshape(-1)
        prev = lax.ppermute(div_flat, "col", forward)
        follow = lax.ppermute(div_flat, "col", backward)
        p_meta = lax.ppermute(d_meta, "col", forward)
        n_meta = lax.ppermute(d_meta, "col", backward)
        inv = lax.all_gather(inv_flat, "row")
        all_meta = lax.all_gather(m_meta, "row", tiled=True)
        return call(
            functools.partial(kernel_all, sizes),
            [d_meta, p_meta, n_meta, all_meta, s_meta, div_flat, prev, follow, inv],
            [result],
            [
                pltpu.VMEM((3, owners * width, rows * side, side), F32),
                pltpu.VMEM((3, rows * side, rows * side), F32),
                m_half,
                m_half,
                pltpu.VMEM(result.shape, F32),
                pltpu.SemaphoreType.DMA((rows, pattern)),
            ],
            owners * one * 2,
            scalars=5,
            out_specs=pl.BlockSpec(memory_space=pl.ANY),
            limit=56 << 20,
        )

    anywhere = pl.BlockSpec(memory_space=pl.ANY)

    tables = (inv_cols, inv_count, div_owner, div_local, schur_cols, div_count, schur_count)
    packed = [jax.ShapeDtypeStruct((x.shape[0] + 8, side), F32) for x in (inv_flat, div_flat)]
    inv, div, tile = call(
        kernel_pack,
        [inv_flat, div_flat, *tables],
        [*packed, jax.ShapeDtypeStruct((8, side), F32)],
        [pltpu.VMEM(x.shape, x.dtype) for x in (*tables, *packed)]
        + [pltpu.SemaphoreType.DMA(shape) for shape in ((len(tables),), (2, PARTS), (2, PARTS + 1))],
        0,
        specs=[anywhere] * (2 + len(tables)),
        out_specs=[anywhere] * 3,
        limit=PACK_LIMIT,
    )

    def swap(first):
        def partner(r, c):
            return r ^ (1 if (c % 2 == 0) == first else 2)

        return [(r * count + c, partner(r, c) * count + c) for r in range(owners) for c in range(count)]

    inv_1 = lax.ppermute(inv_flat, ("row", "col"), swap(True))
    inv_2 = lax.ppermute(inv, ("row", "col"), swap(False))
    follow = lax.ppermute(div, "col", backward)
    prev = lax.ppermute(div, "col", forward)

    m_scratch = [m_half, m_half]
    b_high, b_low, y0_high, y0_low, s_own = call(
        functools.partial(kernel_own, sizes),
        [div, inv],
        [every, every, y_half, y_half, square],
        [pltpu.VMEM((owners * width, rows * side, side), F32), *m_scratch],
        one * 4 // 3,
    )
    inv_1, s_own = lax.optimization_barrier((inv_1, s_own))
    inv_3 = lax.ppermute(inv_1, ("row", "col"), swap(False))
    tile_1 = lax.ppermute(tile, ("row", "col"), swap(True))
    tile_3 = lax.ppermute(tile_1, ("row", "col"), swap(False))
    y1_high, y1_low, s_own = call(
        functools.partial(kernel_side, 1, sizes), [inv_1, tile_1, b_high, b_low, s_own], [y_half, y_half, square], m_scratch, one * 4 // 3
    )
    y2_high, y2_low, s_own = call(
        functools.partial(kernel_side, 2, sizes), [inv_2, inv_2, b_high, b_low, s_own], [y_half, y_half, square], m_scratch, one * 4 // 3
    )
    s_next, n_high, n_low = call(
        functools.partial(kernel_next, sizes),
        [y0_high, y0_low, y1_high, y1_low, y2_high, y2_low, follow],
        [square, half, half],
        [pltpu.VMEM((owners * width, rows * side, side), F32)],
        one,
    )
    out_scratch = [pltpu.VMEM(result.shape, F32)]
    out_sems = pltpu.SemaphoreType.DMA((rows, pattern))
    ready, y3_high, y3_low = call(
        functools.partial(kernel_far, sizes),
        [inv_3, tile_3, div, b_high, b_low, n_high, n_low, s_own, s_next],
        [result, half, half],
        [*m_scratch, *out_scratch, out_sems],
        one * 5 // 3,
        out_specs=[anywhere, VMEM, VMEM],
    )
    return call(
        functools.partial(kernel_prev, sizes),
        [ready, prev, div, y0_high, y0_low, y1_high, y1_low, y2_high, y2_low, y3_high, y3_low],
        [result],
        [*out_scratch, pltpu.VMEM((owners * width, rows * side, side), F32), out_sems],
        one,
        specs=[anywhere] + [VMEM] * 10,
        out_specs=anywhere,
        aliases={0: 0},
    )


def solution(mesh):
    blocks = P(("row", "col"), None, None, None)
    table = P(("row", "col"), None)
    line = P(("row", "col"))
    return jax.shard_map(
        local,
        mesh=mesh,
        in_specs=(blocks, table, table, line, blocks, table, line, table, line),
        out_specs=blocks,
        check_vma=False,
    )
```

time: 33.1 us -> 29.9 us (0.903)
  waiting for transfers between devices: 10.3 us -> 6.95 us
  starting transfers between devices: 8.45 us -> 10.7 us
  Pallas kernels: 11.8 us -> 9.71 us
    ppermute x1 -> x3, waiting for transfers between devices: 10.3 us -> 3.74 us  [the longest x1 1.69 us: local(): tile_1 = lax.ppermute(tile, ('row', 'col'), swap(True))]
    ppermute x1, waiting for transfers between devices: 0.01 us -> 3.2 us  [local(): follow = lax.ppermute(div, 'col', backward)]
    ppermute x1 -> x3, starting transfers between devices: 3 us -> 5.32 us  [the longest x1 2.94 us: local(): inv_1 = lax.ppermute(inv_flat, ('row', 'col'), swap(True))]
    pallas_call x6 -> x7, Pallas kernels: 11.8 us -> 9.71 us  [call(): pl.pallas_call(kernel, out_shape=outs if len(outs) > 1 else outs[0], in_s...]
    unnamed x6 -> x8, local copies, waits for them, and re-layouts: 2.23 us -> 2.23 us
  transfers between devices with their start and end apart: 5 -> 7, of which waited for: 1 -> 4; matrix products, arithmetic and copies ran while one was open for 0% -> 0% of each run, Pallas kernels for 20% -> 27%
where the time goes in v2:
time: 29.9 us; the launch traced here: 29.7 us
  starting transfers between devices  10.7 us (36%)
  Pallas kernels  9.71 us (32%)
  waiting for transfers between devices  6.95 us (23%)
  local copies, waits for them, and re-layouts  2.23 us (7%)
    pallas_call x7, Pallas kernels, call(): pl.pallas_call(kernel, out_shape=outs if len(outs) > 1 else outs[0], in_s...  9.71 us
    ppermute x1, waiting for transfers between devices, local(): follow = lax.ppermute(div, 'col', backward)  3.2 us
    ppermute x1, starting transfers between devices, local(): inv_1 = lax.ppermute(inv_flat, ('row', 'col'), swap(True))  2.94 us
    ppermute x1, starting transfers between devices, local(): follow = lax.ppermute(div, 'col', backward)  2.84 us
    ppermute x1, starting transfers between devices, local(): tile_1 = lax.ppermute(tile, ('row', 'col'), swap(True))  2.38 us
    unnamed x8, local copies, waits for them, and re-layouts  2.23 us
    ppermute x1, starting transfers between devices, local(): inv_3 = lax.ppermute(inv_1, ('row', 'col'), swap(False))  2.05 us
    ppermute x1, waiting for transfers between devices, local(): tile_1 = lax.ppermute(tile, ('row', 'col'), swap(True))  1.69 us
  transfers between devices with their start and end apart: 7, of which 4 were waited for; matrix products, arithmetic and copies ran while one was open for 0% of the time, Pallas kernels for 27%

profile of v2, /device:TPU:0, one launch (start us, length us, event | category | flops | bytes accessed | tf_op | source)
XLA Modules:
  0.0 29.7 jit_solution(9468266918773425211)
XLA Ops:
  0.0 2.9 %collective-permute-start = (f32[1280,128]{1,0:T(8,128)}, f32[1280,128]{1,0:T(8,128)S(1)}, u32[]{:S(2)}, u32[]{:S(2)}) collective-permute-start(f32[1280,128]{1,0:T(8,128)} %bitcast.3), channel_id=1, source_target_pairs={{0,8},{1,17},{2,10},{3,19},{4,12},{5,21},{6,14},{7,23},{8,0},{9,25... | collective-permute-start | bytes 1966088 | tf_op jit(solution)/shard_map/ppermute | solution.py:339
  2.9 2.5 %shard_map.91 = (f32[1288,128]{1,0:T(8,128)}, f32[1544,128]{1,0:T(8,128)}, f32[8,128]{1,0:T(8,128)}) custom-call(f32[1280,128]{1,0:T(8,128)} %bitcast.4, f32[1536,128]{1,0:T(8,128)} %bitcast.2, s32[2,5]{1,0:T(2,128)} %refs_0_.1, s32[2]{0:T(128)} %refs_1_.1, s32[2,6]{1,0:T(2,128)} %refs_2_.1, s32[2,6]{1,0:T(2,128)} %refs_3_.1, s32[2,4]{1,0:T(2,128)} %refs_4_.1, ...), custom_call_target="tpu_custom_call" | custom-call | bytes 2896064 | tf_op jit(solution)/shard_map/pallas_call | solution.py:252
  5.5 2.8 %collective-permute-start.5 = (f32[1544,128]{1,0:T(8,128)}, f32[1544,128]{1,0:T(8,128)S(1)}, u32[]{:S(2)}, u32[]{:S(2)}) collective-permute-start(f32[1544,128]{1,0:T(8,128)} %get-tuple-element.27.div.own), channel_id=1, source_target_pairs={{0,7},{1,0},{2,1},{3,2},{4,3},{5,4},{6,5},{7,6},{8,15},{9,8},{10,9... | collective-permute-start | bytes 2371592 | tf_op jit(solution)/shard_map/ppermute | solution.py:341
  8.3 0.0 collective-permute-start.6
  8.3 0.5 %collective-permute-start.4 = (f32[1288,128]{1,0:T(8,128)}, f32[1288,128]{1,0:T(8,128)S(1)}, u32[]{:S(2)}, u32[]{:S(2)}) collective-permute-start(f32[1288,128]{1,0:T(8,128)} %get-tuple-element.28.inv), channel_id=1, source_target_pairs={{0,16},{1,9},{2,18},{3,11},{4,20},{5,13},{6,22},{7,15},{8,24},{9,1... | collective-permute-start | bytes 1978376 | tf_op jit(solution)/shard_map/ppermute | solution.py:340
  8.8 0.0 copy-start
  8.8 1.1 %copy-done = f32[1544,128]{1,0:T(8,128)S(1)} copy-done((f32[1544,128]{1,0:T(8,128)S(1)}, f32[1544,128]{1,0:T(8,128)}, u32[]{:S(2)}) %copy-start) | copy-done | bytes 790552
  10.0 0.0 copy-start.2
  10.0 1.1 %copy-done.2 = f32[1288,128]{1,0:T(8,128)S(1)} copy-done((f32[1288,128]{1,0:T(8,128)S(1)}, f32[1288,128]{1,0:T(8,128)}, u32[]{:S(2)}) %copy-start.2) | copy-done | bytes 659480
  11.1 0.0 copy-start.3
  11.1 1.3 %shard_map.92 = (bf16[4,256,256]{2,1,0:T(8,128)(2,1)S(1)}, bf16[4,256,256]{2,1,0:T(8,128)(2,1)S(1)}, bf16[256,768]{1,0:T(8,128)(2,1)S(1)}, bf16[256,768]{1,0:T(8,128)(2,1)S(1)}, f32[256,256]{1,0:T(8,128)S(1)}) custom-call(f32[1544,128]{1,0:T(8,128)S(1)} %copy-done, f32[1288,128]{1,0:T(8,128)S(1)} %copy-done.2), custom_call_target="tpu_custom_call" | custom-call | flops 402653184 | bytes 3547136 | tf_op jit(solution)/shard_map/pallas_call | solution.py:252
  12.4 1.5 %collective-permute-done.inv = f32[1280,128]{1,0:T(8,128)S(1)} collective-permute-done((f32[1280,128]{1,0:T(8,128)}, f32[1280,128]{1,0:T(8,128)S(1)}, u32[]{:S(2)}, u32[]{:S(2)}) %collective-permute-start) | collective-permute-done | bytes 655392 | tf_op jit(solution)/shard_map/ppermute | solution.py:339
  13.9 2.0 %collective-permute-start.1 = (f32[1280,128]{1,0:T(8,128)S(1)}, f32[1280,128]{1,0:T(8,128)S(1)}, u32[]{:S(2)}, u32[]{:S(2)}) collective-permute-start(f32[1280,128]{1,0:T(8,128)S(1)} %collective-permute-done.inv), channel_id=1, source_target_pairs={{0,16},{1,9},{2,18},{3,11},{4,20},{5,13},{6,22},{7,15},{8,24},{9,1... | collective-permute-start | bytes 1966088 | tf_op jit(solution)/shard_map/ppermute | solution.py:353
  15.9 0.0 copy-done.3
  15.9 2.4 %collective-permute-start.2 = (f32[8,128]{1,0:T(8,128)S(1)}, f32[8,128]{1,0:T(8,128)S(1)}, u32[]{:S(2)}, u32[]{:S(2)}) collective-permute-start(f32[8,128]{1,0:T(8,128)S(1)} %copy-done.3), channel_id=1, source_target_pairs={{0,8},{1,17},{2,10},{3,19},{4,12},{5,21},{6,14},{7,23},{8,0},{9,25... | collective-permute-start | bytes 12296 | tf_op jit(solution)/shard_map/ppermute | solution.py:354
  18.3 1.7 %collective-permute-done.2.tile = f32[8,128]{1,0:T(8,128)S(1)} collective-permute-done((f32[8,128]{1,0:T(8,128)S(1)}, f32[8,128]{1,0:T(8,128)S(1)}, u32[]{:S(2)}, u32[]{:S(2)}) %collective-permute-start.2) | collective-permute-done | bytes 4128 | tf_op jit(solution)/shard_map/ppermute | solution.py:354
  20.0 0.0 collective-permute-start.3
  20.0 0.9 %shard_map.93 = (bf16[256,768]{1,0:T(8,128)(2,1)S(1)}, bf16[256,768]{1,0:T(8,128)(2,1)S(1)}, f32[256,256]{1,0:T(8,128)S(1)}) custom-call(f32[1280,128]{1,0:T(8,128)S(1)} %collective-permute-done.inv, f32[8,128]{1,0:T(8,128)S(1)} %collective-permute-done.2.tile, bf16[4,256,256]{2,1,0:T(8,128)(2,1)S(1)} %get-tuple-element.32.b_high, ...), custom_call_target="tpu_custom_call" | custom-call | flops 402653184 | bytes 3018752 | tf_op jit(solution)/shard_map/pallas_call | solution.py:252
  20.9 0.0 collective-permute-done.4.inv.tile
  20.9 0.9 %shard_map.94 = (bf16[256,768]{1,0:T(8,128)(2,1)S(1)}, bf16[256,768]{1,0:T(8,128)(2,1)S(1)}, f32[256,256]{1,0:T(8,128)S(1)}) custom-call(f32[1288,128]{1,0:T(8,128)S(1)} %collective-permute-done.4.inv.tile, f32[1288,128]{1,0:T(8,128)S(1)} %collective-permute-done.4.inv.tile, bf16[4,256,256]{2,1,0:T(8,128)(2,1)S(1)} %get-tuple-element.32.b_high, ...), custom_call_target="tpu_custom_call" | custom-call | flops 402653184 | bytes 3678208 | tf_op jit(solution)/shard_map/pallas_call | solution.py:252
  21.8 3.2 %collective-permute-done.5.div = f32[1544,128]{1,0:T(8,128)S(1)} collective-permute-done((f32[1544,128]{1,0:T(8,128)}, f32[1544,128]{1,0:T(8,128)S(1)}, u32[]{:S(2)}, u32[]{:S(2)}) %collective-permute-start.5) | collective-permute-done | bytes 790560 | tf_op jit(solution)/shard_map/ppermute | solution.py:341
  25.0 0.0 copy-start.1
  25.0 0.7 %shard_map.95 = (f32[256,256]{1,0:T(8,128)S(1)}, bf16[256,256]{1,0:T(8,128)(2,1)S(1)}, bf16[256,256]{1,0:T(8,128)(2,1)S(1)}) custom-call(bf16[256,768]{1,0:T(8,128)(2,1)S(1)} %get-tuple-element.34.y0_high.refs_0_, bf16[256,768]{1,0:T(8,128)(2,1)S(1)} %get-tuple-element.35.y0_low.refs_1_, bf16[256,768]{1,0:T(8,128)(2,1)S(1)} %get-tuple-element.37.y1_high.refs_2_, ...), custom_call_target="tpu_custom_call" | custom-call | flops 301989888 | bytes 3674112 | tf_op jit(solution)/shard_map/pallas_call | solution.py:252
  25.7 0.5 %collective-permute-done.3.tile = f32[8,128]{1,0:T(8,128)S(1)} collective-permute-done((f32[8,128]{1,0:T(8,128)S(1)}, f32[8,128]{1,0:T(8,128)S(1)}, u32[]{:S(2)}, u32[]{:S(2)}) %collective-permute-start.3) | collective-permute-done | bytes 4128 | tf_op jit(solution)/shard_map/ppermute | solution.py:355
  26.3 0.0 collective-permute-done.1.inv
  26.3 0.0 copy-done.1
  26.3 1.8 %shard_map.96 = (f32[2,4,128,128]{3,2,1,0:T(8,128)}, bf16[256,256]{1,0:T(8,128)(2,1)S(1)}, bf16[256,256]{1,0:T(8,128)(2,1)S(1)}) custom-call(f32[1280,128]{1,0:T(8,128)S(1)} %collective-permute-done.1.inv, f32[8,128]{1,0:T(8,128)S(1)} %collective-permute-done.3.tile, f32[1544,128]{1,0:T(8,128)S(1)} %copy-done.1, ...), custom_call_target="tpu_custom_call" | custom-call | flops 503316480 | bytes 4071424 | tf_op jit(solution)/shard_map/pallas_call | solution.py:252
  28.1 0.0 collective-permute-done.6.div
  28.1 1.6 %shard_map.97 = f32[2,4,128,128]{3,2,1,0:T(8,128)} custom-call(f32[2,4,128,128]{3,2,1,0:T(8,128)} %get-tuple-element.46.ready, f32[1544,128]{1,0:T(8,128)S(1)} %collective-permute-done.6.div, f32[1544,128]{1,0:T(8,128)S(1)} %copy-done.1, bf16[256,768]{1,0:T(8,128)(2,1)S(1)} %get-tuple-element.34.y0_high.refs_0_, ...), custom_call_target="tpu_custom_call", output_to_operand_aliasing={{}: (0, {})} | custom-call | flops 301989888 | bytes 5251072 | tf_op jit(solution)/shard_map/pallas_call | solution.py:252
Async XLA Ops:
  0.0 13.9 %collective-permute-start = (f32[1280,128]{1,0:T(8,128)}, f32[1280,128]{1,0:T(8,128)S(1)}, u32[]{:S(2)}, u32[]{:S(2)}) collective-permute-start(f32[1280,128]{1,0:T(8,128)} %bitcast.3), channel_id=1, source_target_pairs={{0,8},{1,17},{2,10},{3,19},{4,12},{5,21},{6,14},{7,23},{8,0},{9,25... | collective-permute-start | bytes 1966088 | tf_op jit(solution)/shard_map/ppermute | solution.py:339
  5.5 19.5 %collective-permute-start.5 = (f32[1544,128]{1,0:T(8,128)}, f32[1544,128]{1,0:T(8,128)S(1)}, u32[]{:S(2)}, u32[]{:S(2)}) collective-permute-start(f32[1544,128]{1,0:T(8,128)} %get-tuple-element.27.div.own), channel_id=1, source_target_pairs={{0,7},{1,0},{2,1},{3,2},{4,3},{5,4},{6,5},{7,6},{8,15},{9,8},{10,9... | collective-permute-start | bytes 2371592 | tf_op jit(solution)/shard_map/ppermute | solution.py:341
  8.3 19.8 %collective-permute-start.6 = (f32[1544,128]{1,0:T(8,128)}, f32[1544,128]{1,0:T(8,128)S(1)}, u32[]{:S(2)}, u32[]{:S(2)}) collective-permute-start(f32[1544,128]{1,0:T(8,128)} %get-tuple-element.27.div.own), channel_id=1, source_target_pairs={{0,1},{1,2},{2,3},{3,4},{4,5},{5,6},{6,7},{7,0},{8,9},{9,10},{10,1... | collective-permute-start | bytes 2371592 | tf_op jit(solution)/shard_map/ppermute | solution.py:342
  8.3 12.6 %collective-permute-start.4 = (f32[1288,128]{1,0:T(8,128)}, f32[1288,128]{1,0:T(8,128)S(1)}, u32[]{:S(2)}, u32[]{:S(2)}) collective-permute-start(f32[1288,128]{1,0:T(8,128)} %get-tuple-element.28.inv), channel_id=1, source_target_pairs={{0,16},{1,9},{2,18},{3,11},{4,20},{5,13},{6,22},{7,15},{8,24},{9,1... | collective-permute-start | bytes 1978376 | tf_op jit(solution)/shard_map/ppermute | solution.py:340
  8.8 1.1 %copy-start = (f32[1544,128]{1,0:T(8,128)S(1)}, f32[1544,128]{1,0:T(8,128)}, u32[]{:S(2)}) copy-start(f32[1544,128]{1,0:T(8,128)} %get-tuple-element.27.div.own) | copy-start | bytes 2371588
  10.0 1.1 %copy-start.2 = (f32[1288,128]{1,0:T(8,128)S(1)}, f32[1288,128]{1,0:T(8,128)}, u32[]{:S(2)}) copy-start(f32[1288,128]{1,0:T(8,128)} %get-tuple-element.28.inv) | copy-start | bytes 1978372
  11.1 4.9 %copy-start.3 = (f32[8,128]{1,0:T(8,128)S(1)}, f32[8,128]{1,0:T(8,128)}, u32[]{:S(2)}) copy-start(f32[8,128]{1,0:T(8,128)} %get-tuple-element.31) | copy-start | bytes 12292
  13.9 12.4 %collective-permute-start.1 = (f32[1280,128]{1,0:T(8,128)S(1)}, f32[1280,128]{1,0:T(8,128)S(1)}, u32[]{:S(2)}, u32[]{:S(2)}) collective-permute-start(f32[1280,128]{1,0:T(8,128)S(1)} %collective-permute-done.inv), channel_id=1, source_target_pairs={{0,16},{1,9},{2,18},{3,11},{4,20},{5,13},{6,22},{7,15},{8,24},{9,1... | collective-permute-start | bytes 1966088 | tf_op jit(solution)/shard_map/ppermute | solution.py:353
  15.9 4.1 %collective-permute-start.2 = (f32[8,128]{1,0:T(8,128)S(1)}, f32[8,128]{1,0:T(8,128)S(1)}, u32[]{:S(2)}, u32[]{:S(2)}) collective-permute-start(f32[8,128]{1,0:T(8,128)S(1)} %copy-done.3), channel_id=1, source_target_pairs={{0,8},{1,17},{2,10},{3,19},{4,12},{5,21},{6,14},{7,23},{8,0},{9,25... | collective-permute-start | bytes 12296 | tf_op jit(solution)/shard_map/ppermute | solution.py:354
  20.0 6.3 %collective-permute-start.3 = (f32[8,128]{1,0:T(8,128)S(1)}, f32[8,128]{1,0:T(8,128)S(1)}, u32[]{:S(2)}, u32[]{:S(2)}) collective-permute-start(f32[8,128]{1,0:T(8,128)S(1)} %collective-permute-done.2.tile), channel_id=1, source_target_pairs={{0,16},{1,9},{2,18},{3,11},{4,20},{5,13},{6,22},{7,15},{8,24},{9,1... | collective-permute-start | bytes 12296 | tf_op jit(solution)/shard_map/ppermute | solution.py:355
  25.0 1.3 %copy-start.1 = (f32[1544,128]{1,0:T(8,128)S(1)}, f32[1544,128]{1,0:T(8,128)}, u32[]{:S(2)}) copy-start(f32[1544,128]{1,0:T(8,128)} %get-tuple-element.27.div.own) | copy-start | bytes 2371588

commit v3 on v2

--- a/solution.py
+++ b/solution.py
@@ -57,9 +57,9 @@
     return halves(jnp.concatenate([dense[owner * width + i] for i in range(width)], axis=1))
 
 
-def write(out, buf, sums, slots, codes, sems):
-    rows, pattern, side, _ = out.shape
-    copies = []
+def pick(out, sums, slots, codes):
+    rows, _, side, _ = out.shape
+    pattern = len(codes) // rows
     for row in range(rows):
         for slot in slots:
             code = codes[row * pattern + slot]
@@ -67,10 +67,7 @@
             for other in range(rows):
                 block = sums[row * side : (row + 1) * side, other * side : (other + 1) * side]
                 result = jnp.where(code == other, block, result)
-            buf[row, slot] = result
-            copies.append(pltpu.make_async_copy(buf.at[row, slot], out.at[row, slot], sems.at[row, slot]))
-            copies[-1].start()
-    return copies
+            out[row, slot] = result
 
 
 def fetch(sources, targets, sems):
@@ -135,7 +132,7 @@
     odd = lax.axis_index("col") % 2
     codes = []
     for i in range(rows):
-        count = table[3 * rows, i]
+        count = table[2 * rows, i]
         for k in range(slots):
             apart = table[i, k] ^ mine
             apart = jnp.where(odd == 1, ((apart & 1) << 1) | (apart >> 1), apart)
@@ -147,8 +144,8 @@
 def target_codes(table, rows, pattern):
     codes = []
     for i in range(rows):
-        count = table[3 * rows + 1, i]
-        codes += [jnp.where(t < count, table[2 * rows + i, t] % rows, -1) for t in range(pattern)]
+        count = table[rows, i]
+        codes += [jnp.where(t < count, table[i, t] % rows, -1) for t in range(pattern)]
     return codes
 
 
@@ -178,50 +175,73 @@
     s_out[...] = s_in[...] + product((y_high[:, size : 2 * size], y_low[:, size : 2 * size]), part, True)
 
 
-def kernel_next(sizes, y0_high, y0_low, y1_high, y1_low, y2_high, y2_low, div, s_next, n_high, n_low, dense):
+def kernel_next(sizes, y0_high, y0_low, y1_high, y1_low, y2_high, y2_low, div, s_next, n_high, n_low, p_high, p_low, dense):
+    width, side = sizes[2], sizes[4]
     clear(dense)
     place_div(div_codes(integers(div), sizes), div, sizes, dense)
     size = n_high.shape[1]
     cut = slice(2 * size, 3 * size)
     for owner, (high, low) in enumerate(((y0_high, y0_low), (y1_high, y1_low), (y2_high, y2_low))):
-        term = product((high[:, cut], low[:, cut]), owner_part(dense, owner, sizes[2]), True)
+        term = product((high[:, cut], low[:, cut]), owner_part(dense, owner, width), True)
         s_next[...] = term if owner == 0 else s_next[...] + term
-    n_high[...], n_low[...] = owner_part(dense, 3, sizes[2])
+        for u in range(width):
+            block = slice(u * side, (u + 1) * side)
+            p_high[owner * width + u], p_low[owner * width + u] = high[:, block], low[:, block]
+    n_high[...], n_low[...] = owner_part(dense, 3, width)
 
 
 def kernel_far(
-    sizes, inv, tile, div, b_high, b_low, n_high, n_low, s_own, s_next, out, y3_high, y3_low, m_high, m_low, buf, out_sem
+    sizes, inv, tile, div, b_high, b_low, n_high, n_low, s_own, s_next, p_in_high, p_in_low, blocks, p_high, p_low, m_high, m_low
 ):
+    rows, _, width, _, side = sizes
     read_inv(inv, tile, sizes, m_high, m_low)
-    codes = target_codes(integers(div), *out.shape[:2])
+    codes = target_codes(integers(div), rows, blocks.shape[1] + 1)
     own = (b_high[3], b_low[3])
     y_high, y_low = halves(product(own, (m_high[...], m_low[...])))
     size = own[0].shape[1]
-    y3_high[...], y3_low[...] = y_high[:, :size], y_low[:, :size]
+    for u in range(width):
+        cut = slice(u * side, (u + 1) * side)
+        p_high[3 * width + u], p_low[3 * width + u] = y_high[:, cut], y_low[:, cut]
     cut = slice(size, 2 * size)
     own_sum = s_own[...] + product((y_high[:, cut], y_low[:, cut]), own, True)
-    copies = write(out, buf, own_sum, (0, 1), codes, out_sem)
+    pick(blocks, own_sum, (0, 1), codes)
     cut = slice(2 * size, 3 * size)
     next_sum = s_next[...] + product((y_high[:, cut], y_low[:, cut]), (n_high[...], n_low[...]), True)
-    copies += write(out, buf, next_sum, (2,), codes, out_sem)
+    pick(blocks, next_sum, (2,), codes)
+
+
+def kernel_prev(sizes, div, own, p_high, p_low, blocks, out, buf, left_high, left_low, sems):
+    rows, slots, _, _, side = sizes
+    pattern = out.shape[1]
+    copies = []
+    for row in range(rows):
+        copies.append(pltpu.make_async_copy(blocks.at[row], out.at[row, pl.ds(0, pattern - 1)], sems.at[0, row]))
+        copies[-1].start()
+    codes = div_codes(integers(div), sizes)
+    targets = target_codes(integers(own), rows, pattern)
+    for row in range(rows):
+        target = targets[row * pattern + pattern - 1]
+        place = pl.ds(row * side, side)
+        other = jnp.maximum(target, 0)
+        right = []
+        for slot in range(slots):
+            code = codes[slot]
+            for i in range(1, rows):
+                code = jnp.where(other == i, codes[i * slots + slot], code)
+            cut = pl.ds(slot * side, side)
+            source = pl.multiple_of((other * slots + slot) * side, side)
+            live = jnp.where((code >= 0) & (target >= 0), 1.0, 0.0)
+            right.append(div[pl.ds(source, side), :] * live)
+            code = jnp.maximum(code, 0)
+            left_high[:, cut], left_low[:, cut] = p_high[code, place, :], p_low[code, place, :]
+        buf[row] = product((left_high[...], left_low[...]), halves(jnp.concatenate(right, axis=1)), True)
+        copies.append(pltpu.make_async_copy(buf.at[row], out.at[row, pattern - 1], sems.at[1, row]))
+        copies[-1].start()
     for copy in copies:
         copy.wait()
 
 
-def kernel_prev(sizes, ready, div, own, *refs):
-    ys, (out, buf, dense, out_sem) = refs[:8], refs[8:]
-    clear(dense)
-    place_div(div_codes(integers(div), sizes), div, sizes, dense)
-    size = dense.shape[1]
-    total = None
-    for owner in range(4):
-        term = product((ys[2 * owner][:, :size], ys[2 * owner + 1][:, :size]), owner_part(dense, owner, sizes[2]), True)
-        total = term if owner == 0 else total + term
-    for copy in write(out, buf, total, (3,), target_codes(integers(own), *out.shape[:2]), out_sem):
-        copy.wait()
-
-
-def kernel_all(sizes, d_meta, p_meta, n_meta, m_meta, s_meta, div, prev, follow, inv, out, dense, sums, m_high, m_low, buf, out_sem):
+def kernel_all(sizes, d_meta, p_meta, n_meta, m_meta, s_meta, div, prev, follow, inv, out, dense, sums, m_high, m_low):
     _, _, width, slots, _ = sizes
     clear(dense)
     clear(sums)
@@ -243,8 +263,7 @@
 
     codes = [s_meta[i] for i in range(out.shape[0] * out.shape[1])]
     for slots, region in (((0, 1), 1), ((2,), 2), ((3,), 0)):
-        for copy in write(out, buf, sums[region], slots, codes, out_sem):
-            copy.wait()
+        pick(out, sums[region], slots, codes)
 
 
 def call(kernel, operands, outs, scratch, flops, scalars=0, specs=None, out_specs=None, aliases=None, limit=24 << 20):
@@ -282,7 +301,7 @@
     m_half = pltpu.VMEM((size, wide), BF16)
     one = 2 * 3 * rows * side * size * wide
 
-    if owners != 4 or count % 2 or rows != 2 or side != 128:
+    if owners != 4 or count % 2 or rows != 2 or side != 128 or pattern != 4:
 
         def order(length):
             return jnp.arange(length, dtype=jnp.int32)[None, :]
@@ -305,30 +324,29 @@
                 pltpu.VMEM((3, rows * side, rows * side), F32),
                 m_half,
                 m_half,
-                pltpu.VMEM(result.shape, F32),
-                pltpu.SemaphoreType.DMA((rows, pattern)),
             ],
             owners * one * 2,
             scalars=5,
-            out_specs=pl.BlockSpec(memory_space=pl.ANY),
             limit=56 << 20,
         )
 
     anywhere = pl.BlockSpec(memory_space=pl.ANY)
 
-    tables = (inv_cols, inv_count, div_owner, div_local, schur_cols, div_count, schur_count)
-    packed = [jax.ShapeDtypeStruct((x.shape[0] + 8, side), F32) for x in (inv_flat, div_flat)]
-    inv, div, tile = call(
-        kernel_pack,
-        [inv_flat, div_flat, *tables],
-        [*packed, jax.ShapeDtypeStruct((8, side), F32)],
-        [pltpu.VMEM(x.shape, x.dtype) for x in (*tables, *packed)]
-        + [pltpu.SemaphoreType.DMA(shape) for shape in ((len(tables),), (2, PARTS), (2, PARTS + 1))],
-        0,
-        specs=[anywhere] * (2 + len(tables)),
-        out_specs=[anywhere] * 3,
-        limit=PACK_LIMIT,
-    )
+    def noted(blocks, tables):
+        height = blocks.shape[0] + 8
+        out, at = jnp.pad(blocks, ((0, 8), (0, 0))), blocks.shape[0]
+        for table in tables:
+            lines, length = table.shape
+            out = out + jnp.pad(table.astype(F32), ((at, height - at - lines), (0, side - length)))
+            at += lines
+        return out
+
+    inv_tables = (inv_cols, inv_count[None, :])
+    div = noted(div_flat, (div_owner, div_local, div_count[None, :]))
+    inv = noted(inv_flat, inv_tables)
+    nothing = jnp.zeros((0, side), F32)
+    tile = noted(nothing, inv_tables)
+    pattern_tile = noted(nothing, (schur_cols, schur_count[None, :]))
 
     def swap(first):
         def partner(r, c):
@@ -359,32 +377,30 @@
     y2_high, y2_low, s_own = call(
         functools.partial(kernel_side, 2, sizes), [inv_2, inv_2, b_high, b_low, s_own], [y_half, y_half, square], m_scratch, one * 4 // 3
     )
-    s_next, n_high, n_low = call(
+    p_half = jax.ShapeDtypeStruct((owners * width, rows * side, side), BF16)
+    s_next, n_high, n_low, p_high, p_low = call(
         functools.partial(kernel_next, sizes),
         [y0_high, y0_low, y1_high, y1_low, y2_high, y2_low, follow],
-        [square, half, half],
+        [square, half, half, p_half, p_half],
         [pltpu.VMEM((owners * width, rows * side, side), F32)],
         one,
     )
-    out_scratch = [pltpu.VMEM(result.shape, F32)]
-    out_sems = pltpu.SemaphoreType.DMA((rows, pattern))
-    ready, y3_high, y3_low = call(
+    three, p_high, p_low = call(
         functools.partial(kernel_far, sizes),
-        [inv_3, tile_3, div, b_high, b_low, n_high, n_low, s_own, s_next],
-        [result, half, half],
-        [*m_scratch, *out_scratch, out_sems],
+        [inv_3, tile_3, pattern_tile, b_high, b_low, n_high, n_low, s_own, s_next, p_high, p_low],
+        [jax.ShapeDtypeStruct((rows, pattern - 1, side, side), F32), p_half, p_half],
+        m_scratch,
         one * 5 // 3,
-        out_specs=[anywhere, VMEM, VMEM],
-    )
+        aliases={9: 1, 10: 2},
+    )
+    left = pltpu.VMEM((side, slots * side), BF16)
     return call(
         functools.partial(kernel_prev, sizes),
-        [ready, prev, div, y0_high, y0_low, y1_high, y1_low, y2_high, y2_low, y3_high, y3_low],
+        [prev, pattern_tile, p_high, p_low, three],
         [result],
-        [*out_scratch, pltpu.VMEM((owners * width, rows * side, side), F32), out_sems],
+        [pltpu.VMEM((rows, side, side), F32), left, left, pltpu.SemaphoreType.DMA((2, rows))],
         one,
-        specs=[anywhere] + [VMEM] * 10,
         out_specs=anywhere,
-        aliases={0: 0},
     )
 
 

time: 29.9 us -> 28.6 us (0.957)
  Pallas kernels: 9.71 us -> 6.3 us
  waiting for transfers between devices: 6.95 us -> 8.75 us
  local copies, waits for them, and re-layouts: 2.23 us -> 0.67 us
  other arithmetic: 0 us -> 1.34 us
  starting transfers between devices: 10.7 us -> 11.3 us
    pallas_call x7 -> x6, Pallas kernels: 9.71 us -> 6.3 us  [call(): pl.pallas_call(kernel, out_shape=outs if len(outs) > 1 else outs[0], in_s...]
    ppermute x1, waiting for transfers between devices: 1.51 us -> 4.37 us  [local(): inv_1 = lax.ppermute(inv_flat, ('row', 'col'), swap(True))]
    ppermute x1, waiting for transfers between devices: 3.2 us -> 1.58 us  [local(): follow = lax.ppermute(div, 'col', backward)]
    unnamed x8 -> x16, local copies, waits for them, and re-layouts: 2.23 us -> 0.67 us
    add x0 -> x4, other arithmetic: none -> 1.32 us  [noted(): out + jnp.pad(table.astype(F32), ((at, height - at - lines), (0, side - l...]
    ppermute x1, starting transfers between devices: 0.51 us -> 1.03 us  [local(): inv_2 = lax.ppermute(inv, ('row', 'col'), swap(False))]
    ppermute x1, waiting for transfers between devices: 0.01 us -> 0.35 us  [local(): prev = lax.ppermute(div, 'col', forward)]
  transfers between devices with their start and end apart: 7 -> 7, of which waited for: 4 -> 5; matrix products, arithmetic and copies ran while one was open for 0% -> 5% of each run, Pallas kernels for 27% -> 17%
where the time goes in v3:
time: 28.6 us; the launch traced here: 28.4 us
  starting transfers between devices  11.3 us (40%)
  waiting for transfers between devices  8.75 us (31%)
  Pallas kernels  6.3 us (22%)
  other arithmetic  1.34 us (5%)
  local copies, waits for them, and re-layouts  0.67 us (2%)
    pallas_call x6, Pallas kernels, call(): pl.pallas_call(kernel, out_shape=outs if len(outs) > 1 else outs[0], in_s...  6.3 us
    ppermute x1, waiting for transfers between devices, local(): inv_1 = lax.ppermute(inv_flat, ('row', 'col'), swap(True))  4.37 us
    ppermute x1, starting transfers between devices, local(): inv_1 = lax.ppermute(inv_flat, ('row', 'col'), swap(True))  2.94 us
    ppermute x1, starting transfers between devices, local(): follow = lax.ppermute(div, 'col', backward)  2.84 us
    ppermute x1, starting transfers between devices, local(): tile_1 = lax.ppermute(tile, ('row', 'col'), swap(True))  2.37 us
    ppermute x1, starting transfers between devices, local(): inv_3 = lax.ppermute(inv_1, ('row', 'col'), swap(False))  1.98 us
    ppermute x1, waiting for transfers between devices, local(): tile_1 = lax.ppermute(tile, ('row', 'col'), swap(True))  1.67 us
    ppermute x1, waiting for transfers between devices, local(): follow = lax.ppermute(div, 'col', backward)  1.58 us
  transfers between devices with their start and end apart: 7, of which 5 were waited for; matrix products, arithmetic and copies ran while one was open for 5% of the time, Pallas kernels for 17%

profile of v3, /device:TPU:0, one launch (start us, length us, event | category | flops | bytes accessed | tf_op | source)
XLA Modules:
  0.0 28.4 jit_solution(5711993999084106622)
XLA Ops:
  0.0 0.0 copy-start.1
  0.0 0.0 copy-start.2
  0.0 2.9 %collective-permute-start.1 = (f32[1280,128]{1,0:T(8,128)}, f32[1280,128]{1,0:T(8,128)S(1)}, u32[]{:S(2)}, u32[]{:S(2)}) collective-permute-start(f32[1280,128]{1,0:T(8,128)} %bitcast.9), channel_id=1, source_target_pairs={{0,8},{1,17},{2,10},{3,19},{4,12},{5,21},{6,14},{7,23},{8,0},{9,25... | collective-permute-start | bytes 1966088 | tf_op jit(solution)/shard_map/ppermute | solution.py:357
  2.9 0.0 copy-done.1
  2.9 0.0 copy-done.2
  3.0 0.0 copy-start.5
  3.0 0.6 %copy-done.5 = s32[2]{0:T(128)S(1)} copy-done((s32[2]{0:T(128)S(1)}, s32[2]{0:T(128)}, u32[]{:S(2)}) %copy-start.5) | copy-done | bytes 32
  3.6 0.0 copy-start.3
  3.6 0.0 copy-start
  3.6 1.3 %pad_add_fusion.div = f32[1544,128]{1,0:T(8,128)S(1)} fusion(f32[1,2]{1,0:T(1,128)S(1)} %convert_bitcast_fusion.2, f32[2,6]{1,0:T(2,128)S(1)} %convert_element_type.57, f32[2,6]{1,0:T(2,128)S(1)} %convert_element_type.56, f32[1536,128]{1,0:T(8,128)} %bitcast.8), kind=kLoop, calls=%fused_computation | loop fusion | flops 592896 | bytes 1577064 | tf_op jit(solution)/shard_map/add | solution.py:340
  4.9 0.0 copy-start.6
  4.9 2.8 %collective-permute-start.6 = (f32[1544,128]{1,0:T(8,128)S(1)}, f32[1544,128]{1,0:T(8,128)S(1)}, u32[]{:S(2)}, u32[]{:S(2)}) collective-permute-start(f32[1544,128]{1,0:T(8,128)S(1)} %pad_add_fusion.div), channel_id=1, source_target_pairs={{0,7},{1,0},{2,1},{3,2},{4,3},{5,4},{6,5},{7,6},{8,15},{9,8},{10,9... | collective-permute-start | bytes 2371592 | tf_op jit(solution)/shard_map/ppermute | solution.py:359
  7.7 0.0 collective-permute-start
  7.7 0.0 copy-done.3
  7.7 0.0 copy-done.6
  7.8 0.0 copy-done
  7.8 1.0 %collective-permute-start.5 = (f32[1288,128]{1,0:T(8,128)S(1)}, f32[1288,128]{1,0:T(8,128)S(1)}, u32[]{:S(2)}, u32[]{:S(2)}) collective-permute-start(f32[1288,128]{1,0:T(8,128)S(1)} %pad_add_fusion.1.inv), channel_id=1, source_target_pairs={{0,16},{1,9},{2,18},{3,11},{4,20},{5,13},{6,22},{7,15},{8,24},{9,1... | collective-permute-start | bytes 1978376 | tf_op jit(solution)/shard_map/ppermute | solution.py:358
  8.8 1.3 %shard_map.91 = (bf16[4,256,256]{2,1,0:T(8,128)(2,1)S(1)}, bf16[4,256,256]{2,1,0:T(8,128)(2,1)S(1)}, bf16[256,768]{1,0:T(8,128)(2,1)S(1)}, bf16[256,768]{1,0:T(8,128)(2,1)S(1)}, f32[256,256]{1,0:T(8,128)S(1)}) custom-call(f32[1544,128]{1,0:T(8,128)S(1)} %pad_add_fusion.div, f32[1288,128]{1,0:T(8,128)S(1)} %pad_add_fusion.1.inv), custom_call_target="tpu_custom_call" | custom-call | flops 402653184 | bytes 3547136 | tf_op jit(solution)/shard_map/pallas_call | solution.py:271
  10.2 4.4 %collective-permute-done.1.inv = f32[1280,128]{1,0:T(8,128)S(1)} collective-permute-done((f32[1280,128]{1,0:T(8,128)}, f32[1280,128]{1,0:T(8,128)S(1)}, u32[]{:S(2)}, u32[]{:S(2)}) %collective-permute-start.1) | collective-permute-done | bytes 655392 | tf_op jit(solution)/shard_map/ppermute | solution.py:357
  14.5 0.0 copy-start.4
  14.5 2.0 %collective-permute-start.2 = (f32[1280,128]{1,0:T(8,128)S(1)}, f32[1280,128]{1,0:T(8,128)S(1)}, u32[]{:S(2)}, u32[]{:S(2)}) collective-permute-start(f32[1280,128]{1,0:T(8,128)S(1)} %collective-permute-done.1.inv), channel_id=1, source_target_pairs={{0,16},{1,9},{2,18},{3,11},{4,20},{5,13},{6,22},{7,15},{8,24},{9,1... | collective-permute-start | bytes 1966088 | tf_op jit(solution)/shard_map/ppermute | solution.py:371
  16.5 0.0 copy-start.7
  16.5 2.4 %collective-permute-start.3 = (f32[8,128]{1,0:T(8,128)S(1)}, f32[8,128]{1,0:T(8,128)S(1)}, u32[]{:S(2)}, u32[]{:S(2)}) collective-permute-start(f32[8,128]{1,0:T(8,128)S(1)} %pad_add_fusion.2), channel_id=1, source_target_pairs={{0,8},{1,17},{2,10},{3,19},{4,12},{5,21},{6,14},{7,23},{8,0},{9,25... | collective-permute-start | bytes 12296 | tf_op jit(solution)/shard_map/ppermute | solution.py:372
  18.9 0.0 copy-done.4
  18.9 0.0 copy-done.7
  18.9 1.7 %collective-permute-done.3.tile = f32[8,128]{1,0:T(8,128)S(1)} collective-permute-done((f32[8,128]{1,0:T(8,128)S(1)}, f32[8,128]{1,0:T(8,128)S(1)}, u32[]{:S(2)}, u32[]{:S(2)}) %collective-permute-start.3) | collective-permute-done | bytes 4128 | tf_op jit(solution)/shard_map/ppermute | solution.py:372
  20.6 0.1 collective-permute-start.4
  20.7 0.9 %shard_map.92 = (bf16[256,768]{1,0:T(8,128)(2,1)S(1)}, bf16[256,768]{1,0:T(8,128)(2,1)S(1)}, f32[256,256]{1,0:T(8,128)S(1)}) custom-call(f32[1280,128]{1,0:T(8,128)S(1)} %collective-permute-done.1.inv, f32[8,128]{1,0:T(8,128)S(1)} %collective-permute-done.3.tile, bf16[4,256,256]{2,1,0:T(8,128)(2,1)S(1)} %get-tuple-element.28.b_high, ...), custom_call_target="tpu_custom_call" | custom-call | flops 402653184 | bytes 3018752 | tf_op jit(solution)/shard_map/pallas_call | solution.py:271
  21.6 0.0 collective-permute-done.5.inv.tile
  21.6 0.9 %shard_map.93 = (bf16[256,768]{1,0:T(8,128)(2,1)S(1)}, bf16[256,768]{1,0:T(8,128)(2,1)S(1)}, f32[256,256]{1,0:T(8,128)S(1)}) custom-call(f32[1288,128]{1,0:T(8,128)S(1)} %collective-permute-done.5.inv.tile, f32[1288,128]{1,0:T(8,128)S(1)} %collective-permute-done.5.inv.tile, bf16[4,256,256]{2,1,0:T(8,128)(2,1)S(1)} %get-tuple-element.28.b_high, ...), custom_call_target="tpu_custom_call" | custom-call | flops 402653184 | bytes 3678208 | tf_op jit(solution)/shard_map/pallas_call | solution.py:271
  22.5 1.6 %collective-permute-done.6.div = f32[1544,128]{1,0:T(8,128)S(1)} collective-permute-done((f32[1544,128]{1,0:T(8,128)S(1)}, f32[1544,128]{1,0:T(8,128)S(1)}, u32[]{:S(2)}, u32[]{:S(2)}) %collective-permute-start.6) | collective-permute-done | bytes 790560 | tf_op jit(solution)/shard_map/ppermute | solution.py:359
  24.1 0.8 %shard_map.94 = (f32[256,256]{1,0:T(8,128)S(1)}, bf16[256,256]{1,0:T(8,128)(2,1)S(1)}, bf16[256,256]{1,0:T(8,128)(2,1)S(1)}, bf16[8,256,128]{2,1,0:T(8,128)(2,1)S(1)}, bf16[8,256,128]{2,1,0:T(8,128)(2,1)S(1)}) custom-call(bf16[256,768]{1,0:T(8,128)(2,1)S(1)} %get-tuple-element.30.y0_high, bf16[256,768]{1,0:T(8,128)(2,1)S(1)} %get-tuple-element.31.y0_low, ...), custom_call_target="tpu_custom_call" | custom-call | flops 301989888 | bytes 4722688 | tf_op jit(solution)/shard_map/pallas_call | solution.py:271
  24.9 0.8 %collective-permute-done.4.tile = f32[8,128]{1,0:T(8,128)S(1)} collective-permute-done((f32[8,128]{1,0:T(8,128)S(1)}, f32[8,128]{1,0:T(8,128)S(1)}, u32[]{:S(2)}, u32[]{:S(2)}) %collective-permute-start.4) | collective-permute-done | bytes 4128 | tf_op jit(solution)/shard_map/ppermute | solution.py:373
  25.6 0.0 collective-permute-done.2.inv
  25.6 1.0 %shard_map.95 = (f32[2,3,128,128]{3,2,1,0:T(8,128)S(1)}, bf16[8,256,128]{2,1,0:T(8,128)(2,1)S(1)}, bf16[8,256,128]{2,1,0:T(8,128)(2,1)S(1)}) custom-call(f32[1280,128]{1,0:T(8,128)S(1)} %collective-permute-done.2.inv, f32[8,128]{1,0:T(8,128)S(1)} %collective-permute-done.4.tile, ...), custom_call_target="tpu_custom_call", output_to_operand_aliasing={{1}: (9, {}), {2}: (10, {})} | custom-call | flops 503316480 | bytes 4988928 | tf_op jit(solution)/shard_map/pallas_call | solution.py:271
  26.7 0.3 %collective-permute-done.div = f32[1544,128]{1,0:T(8,128)S(1)} collective-permute-done((f32[1544,128]{1,0:T(8,128)S(1)}, f32[1544,128]{1,0:T(8,128)S(1)}, u32[]{:S(2)}, u32[]{:S(2)}) %collective-permute-start) | collective-permute-done | bytes 790560 | tf_op jit(solution)/shard_map/ppermute | solution.py:360
  27.0 1.4 %shard_map.96 = f32[2,4,128,128]{3,2,1,0:T(8,128)} custom-call(f32[1544,128]{1,0:T(8,128)S(1)} %collective-permute-done.div, f32[8,128]{1,0:T(8,128)S(1)} %pad_add_fusion.3.div.own, bf16[8,256,128]{2,1,0:T(8,128)(2,1)S(1)} %get-tuple-element.44.p_high, bf16[8,256,128]{2,1,0:T(8,128)(2,1)S(1)} %get-tuple-element.45.p_low, ...), custom_call_target="tpu_custom_call" | custom-call | flops 301989888 | bytes 2760704 | tf_op jit(solution)/shard_map/pallas_call | solution.py:271
  (10 shorter events, 0.1 us)
Async XLA Ops:
  0.0 2.9 %copy-start.1 = (s32[2,6]{1,0:T(2,128)S(1)}, s32[2,6]{1,0:T(2,128)}, u32[]{:S(2)}) copy-start(s32[2,6]{1,0:T(2,128)} %param.10) | copy-start | bytes 148
  0.0 2.9 %copy-start.2 = (s32[2,6]{1,0:T(2,128)S(1)}, s32[2,6]{1,0:T(2,128)}, u32[]{:S(2)}) copy-start(s32[2,6]{1,0:T(2,128)} %param.11) | copy-start | bytes 148
  0.0 14.5 %collective-permute-start.1 = (f32[1280,128]{1,0:T(8,128)}, f32[1280,128]{1,0:T(8,128)S(1)}, u32[]{:S(2)}, u32[]{:S(2)}) collective-permute-start(f32[1280,128]{1,0:T(8,128)} %bitcast.9), channel_id=1, source_target_pairs={{0,8},{1,17},{2,10},{3,19},{4,12},{5,21},{6,14},{7,23},{8,0},{9,25... | collective-permute-start | bytes 1966088 | tf_op jit(solution)/shard_map/ppermute | solution.py:357
  3.0 0.7 %copy-start.5 = (s32[2]{0:T(128)S(1)}, s32[2]{0:T(128)}, u32[]{:S(2)}) copy-start(s32[2]{0:T(128)} %param.12) | copy-start | bytes 28
  3.6 4.1 %copy-start.3 = (s32[2,5]{1,0:T(2,128)S(1)}, s32[2,5]{1,0:T(2,128)}, u32[]{:S(2)}) copy-start(s32[2,5]{1,0:T(2,128)} %param.14) | copy-start | bytes 124
  3.6 4.1 %copy-start = (f32[2,5,128,128]{3,2,1,0:T(8,128)S(1)}, f32[2,5,128,128]{3,2,1,0:T(8,128)}, u32[]{:S(2)}) copy-start(f32[2,5,128,128]{3,2,1,0:T(8,128)} %param.13) | copy-start | bytes 1966084
  4.9 2.9 %copy-start.6 = (s32[2]{0:T(128)S(1)}, s32[2]{0:T(128)}, u32[]{:S(2)}) copy-start(s32[2]{0:T(128)} %param.15) | copy-start | bytes 28
  4.9 19.2 %collective-permute-start.6 = (f32[1544,128]{1,0:T(8,128)S(1)}, f32[1544,128]{1,0:T(8,128)S(1)}, u32[]{:S(2)}, u32[]{:S(2)}) collective-permute-start(f32[1544,128]{1,0:T(8,128)S(1)} %pad_add_fusion.div), channel_id=1, source_target_pairs={{0,7},{1,0},{2,1},{3,2},{4,3},{5,4},{6,5},{7,6},{8,15},{9,8},{10,9... | collective-permute-start | bytes 2371592 | tf_op jit(solution)/shard_map/ppermute | solution.py:359
  7.7 19.3 %collective-permute-start = (f32[1544,128]{1,0:T(8,128)S(1)}, f32[1544,128]{1,0:T(8,128)S(1)}, u32[]{:S(2)}, u32[]{:S(2)}) collective-permute-start(f32[1544,128]{1,0:T(8,128)S(1)} %pad_add_fusion.div), channel_id=1, source_target_pairs={{0,1},{1,2},{2,3},{3,4},{4,5},{5,6},{6,7},{7,0},{8,9},{9,10},{10,1... | collective-permute-start | bytes 2371592 | tf_op jit(solution)/shard_map/ppermute | solution.py:360
  7.8 13.8 %collective-permute-start.5 = (f32[1288,128]{1,0:T(8,128)S(1)}, f32[1288,128]{1,0:T(8,128)S(1)}, u32[]{:S(2)}, u32[]{:S(2)}) collective-permute-start(f32[1288,128]{1,0:T(8,128)S(1)} %pad_add_fusion.1.inv), channel_id=1, source_target_pairs={{0,16},{1,9},{2,18},{3,11},{4,20},{5,13},{6,22},{7,15},{8,24},{9,1... | collective-permute-start | bytes 1978376 | tf_op jit(solution)/shard_map/ppermute | solution.py:358
  14.5 4.4 %copy-start.4 = (s32[2,4]{1,0:T(2,128)S(1)}, s32[2,4]{1,0:T(2,128)}, u32[]{:S(2)}) copy-start(s32[2,4]{1,0:T(2,128)} %param.16) | copy-start | bytes 100
  14.5 11.1 %collective-permute-start.2 = (f32[1280,128]{1,0:T(8,128)S(1)}, f32[1280,128]{1,0:T(8,128)S(1)}, u32[]{:S(2)}, u32[]{:S(2)}) collective-permute-start(f32[1280,128]{1,0:T(8,128)S(1)} %collective-permute-done.1.inv), channel_id=1, source_target_pairs={{0,16},{1,9},{2,18},{3,11},{4,20},{5,13},{6,22},{7,15},{8,24},{9,1... | collective-permute-start | bytes 1966088 | tf_op jit(solution)/shard_map/ppermute | solution.py:371
  16.5 2.4 %copy-start.7 = (s32[2]{0:T(128)S(1)}, s32[2]{0:T(128)}, u32[]{:S(2)}) copy-start(s32[2]{0:T(128)} %param.17) | copy-start | bytes 28
  16.5 4.1 %collective-permute-start.3 = (f32[8,128]{1,0:T(8,128)S(1)}, f32[8,128]{1,0:T(8,128)S(1)}, u32[]{:S(2)}, u32[]{:S(2)}) collective-permute-start(f32[8,128]{1,0:T(8,128)S(1)} %pad_add_fusion.2), channel_id=1, source_target_pairs={{0,8},{1,17},{2,10},{3,19},{4,12},{5,21},{6,14},{7,23},{8,0},{9,25... | collective-permute-start | bytes 12296 | tf_op jit(solution)/shard_map/ppermute | solution.py:372
  20.6 5.0 %collective-permute-start.4 = (f32[8,128]{1,0:T(8,128)S(1)}, f32[8,128]{1,0:T(8,128)S(1)}, u32[]{:S(2)}, u32[]{:S(2)}) collective-permute-start(f32[8,128]{1,0:T(8,128)S(1)} %collective-permute-done.3.tile), channel_id=1, source_target_pairs={{0,16},{1,9},{2,18},{3,11},{4,20},{5,13},{6,22},{7,15},{8,24},{9,1... | collective-permute-start | bytes 12296 | tf_op jit(solution)/shard_map/ppermute | solution.py:373

commit v4 on v3

--- a/solution.py
+++ b/solution.py
@@ -342,7 +342,8 @@
         return out
 
     inv_tables = (inv_cols, inv_count[None, :])
-    div = noted(div_flat, (div_owner, div_local, div_count[None, :]))
+    div = lax.optimization_barrier(noted(div_flat, (div_owner, div_local)))
+    div = lax.dynamic_update_slice(div, div_count[None, :].astype(F32), (div_flat.shape[0] + 2 * rows, 0))
     inv = noted(inv_flat, inv_tables)
     nothing = jnp.zeros((0, side), F32)
     tile = noted(nothing, inv_tables)

time: 28.6 us -> 28.2 us (0.986)
  local copies, waits for them, and re-layouts: 0.67 us -> 0.23 us
    ppermute x1, waiting for transfers between devices: 1.58 us -> 0.76 us  [local(): follow = lax.ppermute(div, 'col', backward)]
    ppermute x1, waiting for transfers between devices: 4.37 us -> 5.19 us  [local(): inv_1 = lax.ppermute(inv_flat, ('row', 'col'), swap(True))]
    unnamed x16, local copies, waits for them, and re-layouts: 0.67 us -> 0.04 us
    ppermute x1, waiting for transfers between devices: 0.35 us -> 0.01 us  [local(): prev = lax.ppermute(div, 'col', forward)]
    ppermute x1, waiting for transfers between devices: 0.77 us -> 1.11 us  [local(): tile_3 = lax.ppermute(tile_1, ('row', 'col'), swap(False))]
  transfers between devices with their start and end apart: 7 -> 7, of which waited for: 5 -> 4; matrix products, arithmetic and copies ran while one was open for 5% -> 5% of each run, Pallas kernels for 17% -> 18%
where the time goes in v4:
time: 28.2 us; the launch traced here: 28 us
  starting transfers between devices  11.3 us (40%)
  waiting for transfers between devices  8.74 us (31%)
  Pallas kernels  6.32 us (22%)
  other arithmetic  1.34 us (5%)
    pallas_call x6, Pallas kernels, call(): pl.pallas_call(kernel, out_shape=outs if len(outs) > 1 else outs[0], in_s...  6.32 us
    ppermute x1, waiting for transfers between devices, local(): inv_1 = lax.ppermute(inv_flat, ('row', 'col'), swap(True))  5.19 us
    ppermute x1, starting transfers between devices, local(): inv_1 = lax.ppermute(inv_flat, ('row', 'col'), swap(True))  2.94 us
    ppermute x1, starting transfers between devices, local(): follow = lax.ppermute(div, 'col', backward)  2.84 us
    ppermute x1, starting transfers between devices, local(): tile_1 = lax.ppermute(tile, ('row', 'col'), swap(True))  2.38 us
    ppermute x1, starting transfers between devices, local(): inv_3 = lax.ppermute(inv_1, ('row', 'col'), swap(False))  1.98 us
    ppermute x1, waiting for transfers between devices, local(): tile_1 = lax.ppermute(tile, ('row', 'col'), swap(True))  1.67 us
    add x4, other arithmetic, noted(): out + jnp.pad(table.astype(F32), ((at, height - at - lines), (0, side - l...  1.32 us
  transfers between devices with their start and end apart: 7, of which 4 were waited for; matrix products, arithmetic and copies ran while one was open for 5% of the time, Pallas kernels for 18%

profile of v4, /device:TPU:0, one launch (start us, length us, event | category | flops | bytes accessed | tf_op | source)
XLA Modules:
  0.0 28.0 jit_solution(11608522930075864232)
XLA Ops:
  0.0 0.0 copy-start.1
  0.0 0.0 copy-start.2
  0.0 2.9 %collective-permute-start.1 = (f32[1280,128]{1,0:T(8,128)}, f32[1280,128]{1,0:T(8,128)S(1)}, u32[]{:S(2)}, u32[]{:S(2)}) collective-permute-start(f32[1280,128]{1,0:T(8,128)} %bitcast.9), channel_id=1, source_target_pairs={{0,8},{1,17},{2,10},{3,19},{4,12},{5,21},{6,14},{7,23},{8,0},{9,25... | collective-permute-start | bytes 1966088 | tf_op jit(solution)/shard_map/ppermute | solution.py:358
  2.9 0.0 copy-done.1
  2.9 0.0 copy-done.2
  3.0 0.0 copy-start.5
  3.0 0.0 copy-start
  3.0 1.3 %pad_add_fusion = f32[1544,128]{1,0:T(8,128)S(1)} fusion(f32[2,6]{1,0:T(2,128)S(1)} %convert_element_type.55, f32[2,6]{1,0:T(2,128)S(1)} %convert_element_type.54, f32[1536,128]{1,0:T(8,128)} %bitcast.8), kind=kLoop, calls=%fused_computation | loop fusion | flops 395264 | bytes 1577056 | tf_op jit(solution)/shard_map/add | solution.py:340
  4.2 0.0 copy-done.5
  4.3 0.0 copy-start.3
  4.3 0.2 dynamic_update_slice.3.div
  4.5 0.0 copy-start.6
  4.5 2.8 %collective-permute-start.6 = (f32[1544,128]{1,0:T(8,128)S(1)}, f32[1544,128]{1,0:T(8,128)S(1)}, u32[]{:S(2)}, u32[]{:S(2)}) collective-permute-start(f32[1544,128]{1,0:T(8,128)S(1)} %dynamic_update_slice.3.div), channel_id=1, source_target_pairs={{0,7},{1,0},{2,1},{3,2},{4,3},{5,4},{6,5},{7,6},{8,15},{9,8},{10,9... | collective-permute-start | bytes 2371592 | tf_op jit(solution)/shard_map/ppermute | solution.py:360
  7.3 0.0 collective-permute-start
  7.3 0.0 copy-done.3
  7.3 0.0 copy-done.6
  7.4 0.0 copy-done
  7.4 1.0 %collective-permute-start.5 = (f32[1288,128]{1,0:T(8,128)S(1)}, f32[1288,128]{1,0:T(8,128)S(1)}, u32[]{:S(2)}, u32[]{:S(2)}) collective-permute-start(f32[1288,128]{1,0:T(8,128)S(1)} %pad_add_fusion.1.inv), channel_id=1, source_target_pairs={{0,16},{1,9},{2,18},{3,11},{4,20},{5,13},{6,22},{7,15},{8,24},{9,1... | collective-permute-start | bytes 1978376 | tf_op jit(solution)/shard_map/ppermute | solution.py:359
  8.4 1.3 %shard_map.91 = (bf16[4,256,256]{2,1,0:T(8,128)(2,1)S(1)}, bf16[4,256,256]{2,1,0:T(8,128)(2,1)S(1)}, bf16[256,768]{1,0:T(8,128)(2,1)S(1)}, bf16[256,768]{1,0:T(8,128)(2,1)S(1)}, f32[256,256]{1,0:T(8,128)S(1)}) custom-call(f32[1544,128]{1,0:T(8,128)S(1)} %dynamic_update_slice.3.div, f32[1288,128]{1,0:T(8,128)S(1)} %pad_add_fusion.1.inv), custom_call_target="tpu_custom_call" | custom-call | flops 402653184 | bytes 3547136 | tf_op jit(solution)/shard_map/pallas_call | solution.py:271
  9.8 5.2 %collective-permute-done.1.inv = f32[1280,128]{1,0:T(8,128)S(1)} collective-permute-done((f32[1280,128]{1,0:T(8,128)}, f32[1280,128]{1,0:T(8,128)S(1)}, u32[]{:S(2)}, u32[]{:S(2)}) %collective-permute-start.1) | collective-permute-done | bytes 655392 | tf_op jit(solution)/shard_map/ppermute | solution.py:358
  14.9 0.0 copy-start.4
  14.9 2.0 %collective-permute-start.2 = (f32[1280,128]{1,0:T(8,128)S(1)}, f32[1280,128]{1,0:T(8,128)S(1)}, u32[]{:S(2)}, u32[]{:S(2)}) collective-permute-start(f32[1280,128]{1,0:T(8,128)S(1)} %collective-permute-done.1.inv), channel_id=1, source_target_pairs={{0,16},{1,9},{2,18},{3,11},{4,20},{5,13},{6,22},{7,15},{8,24},{9,1... | collective-permute-start | bytes 1966088 | tf_op jit(solution)/shard_map/ppermute | solution.py:372
  16.9 0.0 copy-start.7
  16.9 2.4 %collective-permute-start.3 = (f32[8,128]{1,0:T(8,128)S(1)}, f32[8,128]{1,0:T(8,128)S(1)}, u32[]{:S(2)}, u32[]{:S(2)}) collective-permute-start(f32[8,128]{1,0:T(8,128)S(1)} %pad_add_fusion.2), channel_id=1, source_target_pairs={{0,8},{1,17},{2,10},{3,19},{4,12},{5,21},{6,14},{7,23},{8,0},{9,25... | collective-permute-start | bytes 12296 | tf_op jit(solution)/shard_map/ppermute | solution.py:373
  19.3 0.0 copy-done.4
  19.3 0.0 copy-done.7
  19.3 1.7 %collective-permute-done.3.tile = f32[8,128]{1,0:T(8,128)S(1)} collective-permute-done((f32[8,128]{1,0:T(8,128)S(1)}, f32[8,128]{1,0:T(8,128)S(1)}, u32[]{:S(2)}, u32[]{:S(2)}) %collective-permute-start.3) | collective-permute-done | bytes 4128 | tf_op jit(solution)/shard_map/ppermute | solution.py:373
  21.0 0.1 collective-permute-start.4
  21.1 0.9 %shard_map.92 = (bf16[256,768]{1,0:T(8,128)(2,1)S(1)}, bf16[256,768]{1,0:T(8,128)(2,1)S(1)}, f32[256,256]{1,0:T(8,128)S(1)}) custom-call(f32[1280,128]{1,0:T(8,128)S(1)} %collective-permute-done.1.inv, f32[8,128]{1,0:T(8,128)S(1)} %collective-permute-done.3.tile, bf16[4,256,256]{2,1,0:T(8,128)(2,1)S(1)} %get-tuple-element.28.b_high, ...), custom_call_target="tpu_custom_call" | custom-call | flops 402653184 | bytes 3018752 | tf_op jit(solution)/shard_map/pallas_call | solution.py:271
  22.0 0.0 collective-permute-done.5.inv.tile
  22.0 0.9 %shard_map.93 = (bf16[256,768]{1,0:T(8,128)(2,1)S(1)}, bf16[256,768]{1,0:T(8,128)(2,1)S(1)}, f32[256,256]{1,0:T(8,128)S(1)}) custom-call(f32[1288,128]{1,0:T(8,128)S(1)} %collective-permute-done.5.inv.tile, f32[1288,128]{1,0:T(8,128)S(1)} %collective-permute-done.5.inv.tile, bf16[4,256,256]{2,1,0:T(8,128)(2,1)S(1)} %get-tuple-element.28.b_high, ...), custom_call_target="tpu_custom_call" | custom-call | flops 402653184 | bytes 3678208 | tf_op jit(solution)/shard_map/pallas_call | solution.py:271
  22.9 0.8 %collective-permute-done.6.div = f32[1544,128]{1,0:T(8,128)S(1)} collective-permute-done((f32[1544,128]{1,0:T(8,128)S(1)}, f32[1544,128]{1,0:T(8,128)S(1)}, u32[]{:S(2)}, u32[]{:S(2)}) %collective-permute-start.6) | collective-permute-done | bytes 790560 | tf_op jit(solution)/shard_map/ppermute | solution.py:360
  23.7 0.8 %shard_map.94 = (f32[256,256]{1,0:T(8,128)S(1)}, bf16[256,256]{1,0:T(8,128)(2,1)S(1)}, bf16[256,256]{1,0:T(8,128)(2,1)S(1)}, bf16[8,256,128]{2,1,0:T(8,128)(2,1)S(1)}, bf16[8,256,128]{2,1,0:T(8,128)(2,1)S(1)}) custom-call(bf16[256,768]{1,0:T(8,128)(2,1)S(1)} %get-tuple-element.30.y0_high, bf16[256,768]{1,0:T(8,128)(2,1)S(1)} %get-tuple-element.31.y0_low, ...), custom_call_target="tpu_custom_call" | custom-call | flops 301989888 | bytes 4722688 | tf_op jit(solution)/shard_map/pallas_call | solution.py:271
  24.5 1.1 %collective-permute-done.4.tile = f32[8,128]{1,0:T(8,128)S(1)} collective-permute-done((f32[8,128]{1,0:T(8,128)S(1)}, f32[8,128]{1,0:T(8,128)S(1)}, u32[]{:S(2)}, u32[]{:S(2)}) %collective-permute-start.4) | collective-permute-done | bytes 4128 | tf_op jit(solution)/shard_map/ppermute | solution.py:374
  25.6 0.0 collective-permute-done.2.inv
  25.6 1.0 %shard_map.95 = (f32[2,3,128,128]{3,2,1,0:T(8,128)S(1)}, bf16[8,256,128]{2,1,0:T(8,128)(2,1)S(1)}, bf16[8,256,128]{2,1,0:T(8,128)(2,1)S(1)}) custom-call(f32[1280,128]{1,0:T(8,128)S(1)} %collective-permute-done.2.inv, f32[8,128]{1,0:T(8,128)S(1)} %collective-permute-done.4.tile, ...), custom_call_target="tpu_custom_call", output_to_operand_aliasing={{1}: (9, {}), {2}: (10, {})} | custom-call | flops 503316480 | bytes 4988928 | tf_op jit(solution)/shard_map/pallas_call | solution.py:271
  26.6 0.0 collective-permute-done.div
  26.6 1.4 %shard_map.96 = f32[2,4,128,128]{3,2,1,0:T(8,128)} custom-call(f32[1544,128]{1,0:T(8,128)S(1)} %collective-permute-done.div, f32[8,128]{1,0:T(8,128)S(1)} %pad_add_fusion.3.div.own, bf16[8,256,128]{2,1,0:T(8,128)(2,1)S(1)} %get-tuple-element.44.p_high, bf16[8,256,128]{2,1,0:T(8,128)(2,1)S(1)} %get-tuple-element.45.p_low, ...), custom_call_target="tpu_custom_call" | custom-call | flops 301989888 | bytes 2760704 | tf_op jit(solution)/shard_map/pallas_call | solution.py:271
  (10 shorter events, 0.1 us)
Async XLA Ops:
  0.0 2.9 %copy-start.1 = (s32[2,6]{1,0:T(2,128)S(1)}, s32[2,6]{1,0:T(2,128)}, u32[]{:S(2)}) copy-start(s32[2,6]{1,0:T(2,128)} %param.10) | copy-start | bytes 148
  0.0 2.9 %copy-start.2 = (s32[2,6]{1,0:T(2,128)S(1)}, s32[2,6]{1,0:T(2,128)}, u32[]{:S(2)}) copy-start(s32[2,6]{1,0:T(2,128)} %param.11) | copy-start | bytes 148
  0.0 14.9 %collective-permute-start.1 = (f32[1280,128]{1,0:T(8,128)}, f32[1280,128]{1,0:T(8,128)S(1)}, u32[]{:S(2)}, u32[]{:S(2)}) collective-permute-start(f32[1280,128]{1,0:T(8,128)} %bitcast.9), channel_id=1, source_target_pairs={{0,8},{1,17},{2,10},{3,19},{4,12},{5,21},{6,14},{7,23},{8,0},{9,25... | collective-permute-start | bytes 1966088 | tf_op jit(solution)/shard_map/ppermute | solution.py:358
  3.0 1.3 %copy-start.5 = (s32[2]{0:T(128)S(1)}, s32[2]{0:T(128)}, u32[]{:S(2)}) copy-start(s32[2]{0:T(128)} %param.12) | copy-start | bytes 28
  3.0 4.4 %copy-start = (f32[2,5,128,128]{3,2,1,0:T(8,128)S(1)}, f32[2,5,128,128]{3,2,1,0:T(8,128)}, u32[]{:S(2)}) copy-start(f32[2,5,128,128]{3,2,1,0:T(8,128)} %param.13) | copy-start | bytes 1966084
  4.3 3.1 %copy-start.3 = (s32[2,5]{1,0:T(2,128)S(1)}, s32[2,5]{1,0:T(2,128)}, u32[]{:S(2)}) copy-start(s32[2,5]{1,0:T(2,128)} %param.14) | copy-start | bytes 124
  4.5 2.9 %copy-start.6 = (s32[2]{0:T(128)S(1)}, s32[2]{0:T(128)}, u32[]{:S(2)}) copy-start(s32[2]{0:T(128)} %param.15) | copy-start | bytes 28
  4.5 19.2 %collective-permute-start.6 = (f32[1544,128]{1,0:T(8,128)S(1)}, f32[1544,128]{1,0:T(8,128)S(1)}, u32[]{:S(2)}, u32[]{:S(2)}) collective-permute-start(f32[1544,128]{1,0:T(8,128)S(1)} %dynamic_update_slice.3.div), channel_id=1, source_target_pairs={{0,7},{1,0},{2,1},{3,2},{4,3},{5,4},{6,5},{7,6},{8,15},{9,8},{10,9... | collective-permute-start | bytes 2371592 | tf_op jit(solution)/shard_map/ppermute | solution.py:360
  7.3 19.3 %collective-permute-start = (f32[1544,128]{1,0:T(8,128)S(1)}, f32[1544,128]{1,0:T(8,128)S(1)}, u32[]{:S(2)}, u32[]{:S(2)}) collective-permute-start(f32[1544,128]{1,0:T(8,128)S(1)} %dynamic_update_slice.3.div), channel_id=1, source_target_pairs={{0,1},{1,2},{2,3},{3,4},{4,5},{5,6},{6,7},{7,0},{8,9},{9,10},{10,1... | collective-permute-start | bytes 2371592 | tf_op jit(solution)/shard_map/ppermute | solution.py:361
  7.4 14.6 %collective-permute-start.5 = (f32[1288,128]{1,0:T(8,128)S(1)}, f32[1288,128]{1,0:T(8,128)S(1)}, u32[]{:S(2)}, u32[]{:S(2)}) collective-permute-start(f32[1288,128]{1,0:T(8,128)S(1)} %pad_add_fusion.1.inv), channel_id=1, source_target_pairs={{0,16},{1,9},{2,18},{3,11},{4,20},{5,13},{6,22},{7,15},{8,24},{9,1... | collective-permute-start | bytes 1978376 | tf_op jit(solution)/shard_map/ppermute | solution.py:359
  14.9 4.4 %copy-start.4 = (s32[2,4]{1,0:T(2,128)S(1)}, s32[2,4]{1,0:T(2,128)}, u32[]{:S(2)}) copy-start(s32[2,4]{1,0:T(2,128)} %param.16) | copy-start | bytes 100
  14.9 10.6 %collective-permute-start.2 = (f32[1280,128]{1,0:T(8,128)S(1)}, f32[1280,128]{1,0:T(8,128)S(1)}, u32[]{:S(2)}, u32[]{:S(2)}) collective-permute-start(f32[1280,128]{1,0:T(8,128)S(1)} %collective-permute-done.1.inv), channel_id=1, source_target_pairs={{0,16},{1,9},{2,18},{3,11},{4,20},{5,13},{6,22},{7,15},{8,24},{9,1... | collective-permute-start | bytes 1966088 | tf_op jit(solution)/shard_map/ppermute | solution.py:372
  16.9 2.4 %copy-start.7 = (s32[2]{0:T(128)S(1)}, s32[2]{0:T(128)}, u32[]{:S(2)}) copy-start(s32[2]{0:T(128)} %param.17) | copy-start | bytes 28
  16.9 4.1 %collective-permute-start.3 = (f32[8,128]{1,0:T(8,128)S(1)}, f32[8,128]{1,0:T(8,128)S(1)}, u32[]{:S(2)}, u32[]{:S(2)}) collective-permute-start(f32[8,128]{1,0:T(8,128)S(1)} %pad_add_fusion.2), channel_id=1, source_target_pairs={{0,8},{1,17},{2,10},{3,19},{4,12},{5,21},{6,14},{7,23},{8,0},{9,25... | collective-permute-start | bytes 12296 | tf_op jit(solution)/shard_map/ppermute | solution.py:373
  21.0 4.6 %collective-permute-start.4 = (f32[8,128]{1,0:T(8,128)S(1)}, f32[8,128]{1,0:T(8,128)S(1)}, u32[]{:S(2)}, u32[]{:S(2)}) collective-permute-start(f32[8,128]{1,0:T(8,128)S(1)} %collective-permute-done.3.tile), channel_id=1, source_target_pairs={{0,16},{1,9},{2,18},{3,11},{4,20},{5,13},{6,22},{7,15},{8,24},{9,1... | collective-permute-start | bytes 12296 | tf_op jit(solution)/shard_map/ppermute | solution.py:374

commit v5 on v4

--- a/solution.py
+++ b/solution.py
@@ -191,7 +191,7 @@
 
 
 def kernel_far(
-    sizes, inv, tile, div, b_high, b_low, n_high, n_low, s_own, s_next, p_in_high, p_in_low, blocks, p_high, p_low, m_high, m_low
+    sizes, inv, tile, div, b_high, b_low, n_high, n_low, s_own, s_next, blocks, q_high, q_low, m_high, m_low
 ):
     rows, _, width, _, side = sizes
     read_inv(inv, tile, sizes, m_high, m_low)
@@ -201,7 +201,7 @@
     size = own[0].shape[1]
     for u in range(width):
         cut = slice(u * side, (u + 1) * side)
-        p_high[3 * width + u], p_low[3 * width + u] = y_high[:, cut], y_low[:, cut]
+        q_high[u], q_low[u] = y_high[:, cut], y_low[:, cut]
     cut = slice(size, 2 * size)
     own_sum = s_own[...] + product((y_high[:, cut], y_low[:, cut]), own, True)
     pick(blocks, own_sum, (0, 1), codes)
@@ -210,9 +210,10 @@
     pick(blocks, next_sum, (2,), codes)
 
 
-def kernel_prev(sizes, div, own, p_high, p_low, blocks, out, buf, left_high, left_low, sems):
+def kernel_prev(sizes, div, own, p_high, p_low, q_high, q_low, blocks, out, buf, sems):
     rows, slots, _, _, side = sizes
     pattern = out.shape[1]
+    known = p_high.shape[0]
     copies = []
     for row in range(rows):
         copies.append(pltpu.make_async_copy(blocks.at[row], out.at[row, pl.ds(0, pattern - 1)], sems.at[0, row]))
@@ -223,18 +224,18 @@
         target = targets[row * pattern + pattern - 1]
         place = pl.ds(row * side, side)
         other = jnp.maximum(target, 0)
-        right = []
+        left, right = ([], []), []
         for slot in range(slots):
             code = codes[slot]
             for i in range(1, rows):
                 code = jnp.where(other == i, codes[i * slots + slot], code)
-            cut = pl.ds(slot * side, side)
             source = pl.multiple_of((other * slots + slot) * side, side)
             live = jnp.where((code >= 0) & (target >= 0), 1.0, 0.0)
             right.append(div[pl.ds(source, side), :] * live)
-            code = jnp.maximum(code, 0)
-            left_high[:, cut], left_low[:, cut] = p_high[code, place, :], p_low[code, place, :]
-        buf[row] = product((left_high[...], left_low[...]), halves(jnp.concatenate(right, axis=1)), True)
+            at, late = jnp.clip(code, 0, known - 1), jnp.maximum(code - known, 0)
+            for part, early, last in zip(left, (p_high, p_low), (q_high, q_low)):
+                part.append(jnp.where(code < known, early[at, place, :], last[late, place, :]))
+        buf[row] = product([jnp.concatenate(x, axis=1) for x in left], halves(jnp.concatenate(right, axis=1)), True)
         copies.append(pltpu.make_async_copy(buf.at[row], out.at[row, pattern - 1], sems.at[1, row]))
         copies[-1].start()
     for copy in copies:
@@ -266,7 +267,7 @@
         pick(out, sums[region], slots, codes)
 
 
-def call(kernel, operands, outs, scratch, flops, scalars=0, specs=None, out_specs=None, aliases=None, limit=24 << 20):
+def call(kernel, operands, outs, scratch, flops, scalars=0, specs=None, out_specs=None, limit=24 << 20):
     moved = sum(x.size * x.dtype.itemsize for x in operands[scalars:] + outs)
     return pl.pallas_call(
         kernel,
@@ -274,7 +275,6 @@
         in_specs=specs or [SMEM] * scalars + [VMEM] * (len(operands) - scalars),
         out_specs=out_specs or ([VMEM] * len(outs) if len(outs) > 1 else VMEM),
         scratch_shapes=scratch,
-        input_output_aliases=aliases or {},
         compiler_params=pltpu.CompilerParams(vmem_limit_bytes=limit),
         cost_estimate=pl.CostEstimate(flops=flops, bytes_accessed=moved, transcendentals=0),
     )(*operands)
@@ -378,7 +378,7 @@
     y2_high, y2_low, s_own = call(
         functools.partial(kernel_side, 2, sizes), [inv_2, inv_2, b_high, b_low, s_own], [y_half, y_half, square], m_scratch, one * 4 // 3
     )
-    p_half = jax.ShapeDtypeStruct((owners * width, rows * side, side), BF16)
+    p_half, q_half = (jax.ShapeDtypeStruct((n * width, rows * side, side), BF16) for n in (owners - 1, 1))
     s_next, n_high, n_low, p_high, p_low = call(
         functools.partial(kernel_next, sizes),
         [y0_high, y0_low, y1_high, y1_low, y2_high, y2_low, follow],
@@ -386,20 +386,18 @@
         [pltpu.VMEM((owners * width, rows * side, side), F32)],
         one,
     )
-    three, p_high, p_low = call(
+    three, q_high, q_low = call(
         functools.partial(kernel_far, sizes),
-        [inv_3, tile_3, pattern_tile, b_high, b_low, n_high, n_low, s_own, s_next, p_high, p_low],
-        [jax.ShapeDtypeStruct((rows, pattern - 1, side, side), F32), p_half, p_half],
+        [inv_3, tile_3, pattern_tile, b_high, b_low, n_high, n_low, s_own, s_next],
+        [jax.ShapeDtypeStruct((rows, pattern - 1, side, side), F32), q_half, q_half],
         m_scratch,
         one * 5 // 3,
-        aliases={9: 1, 10: 2},
-    )
-    left = pltpu.VMEM((side, slots * side), BF16)
+    )
     return call(
         functools.partial(kernel_prev, sizes),
-        [prev, pattern_tile, p_high, p_low, three],
+        [prev, pattern_tile, p_high, p_low, q_high, q_low, three],
         [result],
-        [pltpu.VMEM((rows, side, side), F32), left, left, pltpu.SemaphoreType.DMA((2, rows))],
+        [pltpu.VMEM((rows, side, side), F32), pltpu.SemaphoreType.DMA((2, rows))],
         one,
         out_specs=anywhere,
     )

time: 28.2 us -> 28.2 us (level)
  transfers between devices with their start and end apart: 7 -> 7, of which waited for: 4 -> 4; matrix products, arithmetic and copies ran while one was open for 5% -> 5% of each run, Pallas kernels for 18% -> 17%
where the time goes in v5:
time: 28.2 us; the launch traced here: 28.1 us
  starting transfers between devices  11.3 us (40%)
  waiting for transfers between devices  8.76 us (31%)
  Pallas kernels  6.35 us (23%)
  other arithmetic  1.34 us (5%)
    pallas_call x6, Pallas kernels, call(): pl.pallas_call(kernel, out_shape=outs if len(outs) > 1 else outs[0], in_s...  6.35 us
    ppermute x1, waiting for transfers between devices, local(): inv_1 = lax.ppermute(inv_flat, ('row', 'col'), swap(True))  5.18 us
    ppermute x1, starting transfers between devices, local(): inv_1 = lax.ppermute(inv_flat, ('row', 'col'), swap(True))  2.94 us
    ppermute x1, starting transfers between devices, local(): follow = lax.ppermute(div, 'col', backward)  2.84 us
    ppermute x1, starting transfers between devices, local(): tile_1 = lax.ppermute(tile, ('row', 'col'), swap(True))  2.38 us
    ppermute x1, starting transfers between devices, local(): inv_3 = lax.ppermute(inv_1, ('row', 'col'), swap(False))  1.98 us
    ppermute x1, waiting for transfers between devices, local(): tile_1 = lax.ppermute(tile, ('row', 'col'), swap(True))  1.67 us
    add x4, other arithmetic, noted(): out + jnp.pad(table.astype(F32), ((at, height - at - lines), (0, side - l...  1.32 us
  transfers between devices with their start and end apart: 7, of which 4 were waited for; matrix products, arithmetic and copies ran while one was open for 5% of the time, Pallas kernels for 17%

profile of v5, /device:TPU:0, one launch (start us, length us, event | category | flops | bytes accessed | tf_op | source)
XLA Modules:
  0.0 28.1 jit_solution(11871646442386593565)
XLA Ops:
  0.0 0.0 copy-start.1
  0.0 0.0 copy-start.2
  0.0 2.9 %collective-permute-start.1 = (f32[1280,128]{1,0:T(8,128)}, f32[1280,128]{1,0:T(8,128)S(1)}, u32[]{:S(2)}, u32[]{:S(2)}) collective-permute-start(f32[1280,128]{1,0:T(8,128)} %bitcast.9), channel_id=1, source_target_pairs={{0,8},{1,17},{2,10},{3,19},{4,12},{5,21},{6,14},{7,23},{8,0},{9,25... | collective-permute-start | bytes 1966088 | tf_op jit(solution)/shard_map/ppermute | solution.py:358
  2.9 0.0 copy-done.1
  2.9 0.0 copy-done.2
  3.0 0.0 copy-start.5
  3.0 0.0 copy-start
  3.0 1.3 %pad_add_fusion = f32[1544,128]{1,0:T(8,128)S(1)} fusion(f32[2,6]{1,0:T(2,128)S(1)} %convert_element_type.55, f32[2,6]{1,0:T(2,128)S(1)} %convert_element_type.54, f32[1536,128]{1,0:T(8,128)} %bitcast.8), kind=kLoop, calls=%fused_computation | loop fusion | flops 395264 | bytes 1577056 | tf_op jit(solution)/shard_map/add | solution.py:340
  4.2 0.0 copy-done.5
  4.3 0.0 copy-start.3
  4.3 0.2 dynamic_update_slice.3.div
  4.5 0.0 copy-start.6
  4.5 2.8 %collective-permute-start.4 = (f32[1544,128]{1,0:T(8,128)S(1)}, f32[1544,128]{1,0:T(8,128)S(1)}, u32[]{:S(2)}, u32[]{:S(2)}) collective-permute-start(f32[1544,128]{1,0:T(8,128)S(1)} %dynamic_update_slice.3.div), channel_id=1, source_target_pairs={{0,7},{1,0},{2,1},{3,2},{4,3},{5,4},{6,5},{7,6},{8,15},{9,8},{10,9... | collective-permute-start | bytes 2371592 | tf_op jit(solution)/shard_map/ppermute | solution.py:360
  7.3 0.0 collective-permute-start
  7.3 0.0 copy-done.3
  7.3 0.0 copy-done.6
  7.4 0.0 copy-done
  7.4 1.0 %collective-permute-start.3 = (f32[1288,128]{1,0:T(8,128)S(1)}, f32[1288,128]{1,0:T(8,128)S(1)}, u32[]{:S(2)}, u32[]{:S(2)}) collective-permute-start(f32[1288,128]{1,0:T(8,128)S(1)} %pad_add_fusion.1.inv), channel_id=1, source_target_pairs={{0,16},{1,9},{2,18},{3,11},{4,20},{5,13},{6,22},{7,15},{8,24},{9,1... | collective-permute-start | bytes 1978376 | tf_op jit(solution)/shard_map/ppermute | solution.py:359
  8.4 1.3 %shard_map.91 = (bf16[4,256,256]{2,1,0:T(8,128)(2,1)S(1)}, bf16[4,256,256]{2,1,0:T(8,128)(2,1)S(1)}, bf16[256,768]{1,0:T(8,128)(2,1)S(1)}, bf16[256,768]{1,0:T(8,128)(2,1)S(1)}, f32[256,256]{1,0:T(8,128)S(1)}) custom-call(f32[1544,128]{1,0:T(8,128)S(1)} %dynamic_update_slice.3.div, f32[1288,128]{1,0:T(8,128)S(1)} %pad_add_fusion.1.inv), custom_call_target="tpu_custom_call" | custom-call | flops 402653184 | bytes 3547136 | tf_op jit(solution)/shard_map/pallas_call | solution.py:272
  9.8 5.2 %collective-permute-done.1.inv = f32[1280,128]{1,0:T(8,128)S(1)} collective-permute-done((f32[1280,128]{1,0:T(8,128)}, f32[1280,128]{1,0:T(8,128)S(1)}, u32[]{:S(2)}, u32[]{:S(2)}) %collective-permute-start.1) | collective-permute-done | bytes 655392 | tf_op jit(solution)/shard_map/ppermute | solution.py:358
  14.9 0.0 copy-start.4
  14.9 2.0 %collective-permute-start.5 = (f32[1280,128]{1,0:T(8,128)S(1)}, f32[1280,128]{1,0:T(8,128)S(1)}, u32[]{:S(2)}, u32[]{:S(2)}) collective-permute-start(f32[1280,128]{1,0:T(8,128)S(1)} %collective-permute-done.1.inv), channel_id=1, source_target_pairs={{0,16},{1,9},{2,18},{3,11},{4,20},{5,13},{6,22},{7,15},{8,24},{9,1... | collective-permute-start | bytes 1966088 | tf_op jit(solution)/shard_map/ppermute | solution.py:372
  16.9 0.0 copy-start.7
  16.9 2.4 %collective-permute-start.2 = (f32[8,128]{1,0:T(8,128)S(1)}, f32[8,128]{1,0:T(8,128)S(1)}, u32[]{:S(2)}, u32[]{:S(2)}) collective-permute-start(f32[8,128]{1,0:T(8,128)S(1)} %pad_add_fusion.2), channel_id=1, source_target_pairs={{0,8},{1,17},{2,10},{3,19},{4,12},{5,21},{6,14},{7,23},{8,0},{9,25... | collective-permute-start | bytes 12296 | tf_op jit(solution)/shard_map/ppermute | solution.py:373
  19.3 0.0 copy-done.4
  19.3 0.0 copy-done.7
  19.3 1.7 %collective-permute-done.2.tile = f32[8,128]{1,0:T(8,128)S(1)} collective-permute-done((f32[8,128]{1,0:T(8,128)S(1)}, f32[8,128]{1,0:T(8,128)S(1)}, u32[]{:S(2)}, u32[]{:S(2)}) %collective-permute-start.2) | collective-permute-done | bytes 4128 | tf_op jit(solution)/shard_map/ppermute | solution.py:373
  21.0 0.1 collective-permute-start.6
  21.1 0.9 %shard_map.92 = (bf16[256,768]{1,0:T(8,128)(2,1)S(1)}, bf16[256,768]{1,0:T(8,128)(2,1)S(1)}, f32[256,256]{1,0:T(8,128)S(1)}) custom-call(f32[1280,128]{1,0:T(8,128)S(1)} %collective-permute-done.1.inv, f32[8,128]{1,0:T(8,128)S(1)} %collective-permute-done.2.tile, bf16[4,256,256]{2,1,0:T(8,128)(2,1)S(1)} %get-tuple-element.30.b_high, ...), custom_call_target="tpu_custom_call" | custom-call | flops 402653184 | bytes 3018752 | tf_op jit(solution)/shard_map/pallas_call | solution.py:272
  22.0 0.0 collective-permute-done.3.inv.tile
  22.0 0.9 %shard_map.93 = (bf16[256,768]{1,0:T(8,128)(2,1)S(1)}, bf16[256,768]{1,0:T(8,128)(2,1)S(1)}, f32[256,256]{1,0:T(8,128)S(1)}) custom-call(f32[1288,128]{1,0:T(8,128)S(1)} %collective-permute-done.3.inv.tile, f32[1288,128]{1,0:T(8,128)S(1)} %collective-permute-done.3.inv.tile, bf16[4,256,256]{2,1,0:T(8,128)(2,1)S(1)} %get-tuple-element.30.b_high, ...), custom_call_target="tpu_custom_call" | custom-call | flops 402653184 | bytes 3678208 | tf_op jit(solution)/shard_map/pallas_call | solution.py:272
  22.9 0.8 %collective-permute-done.4.div = f32[1544,128]{1,0:T(8,128)S(1)} collective-permute-done((f32[1544,128]{1,0:T(8,128)S(1)}, f32[1544,128]{1,0:T(8,128)S(1)}, u32[]{:S(2)}, u32[]{:S(2)}) %collective-permute-start.4) | collective-permute-done | bytes 790560 | tf_op jit(solution)/shard_map/ppermute | solution.py:360
  23.7 0.8 %shard_map.94 = (f32[256,256]{1,0:T(8,128)S(1)}, bf16[256,256]{1,0:T(8,128)(2,1)S(1)}, bf16[256,256]{1,0:T(8,128)(2,1)S(1)}, bf16[6,256,128]{2,1,0:T(8,128)(2,1)S(1)}, bf16[6,256,128]{2,1,0:T(8,128)(2,1)S(1)}) custom-call(bf16[256,768]{1,0:T(8,128)(2,1)S(1)} %get-tuple-element.26.y0_high, bf16[256,768]{1,0:T(8,128)(2,1)S(1)} %get-tuple-element.27.y0_low, ...), custom_call_target="tpu_custom_call" | custom-call | flops 301989888 | bytes 4460544 | tf_op jit(solution)/shard_map/pallas_call | solution.py:272
  24.5 1.1 %collective-permute-done.6.tile = f32[8,128]{1,0:T(8,128)S(1)} collective-permute-done((f32[8,128]{1,0:T(8,128)S(1)}, f32[8,128]{1,0:T(8,128)S(1)}, u32[]{:S(2)}, u32[]{:S(2)}) %collective-permute-start.6) | collective-permute-done | bytes 4128 | tf_op jit(solution)/shard_map/ppermute | solution.py:374
  25.6 0.0 collective-permute-done.5.inv
  25.6 1.0 %shard_map.95 = (f32[2,3,128,128]{3,2,1,0:T(8,128)S(1)}, bf16[2,256,128]{2,1,0:T(8,128)(2,1)S(1)}, bf16[2,256,128]{2,1,0:T(8,128)(2,1)S(1)}) custom-call(f32[1280,128]{1,0:T(8,128)S(1)} %collective-permute-done.5.inv, f32[8,128]{1,0:T(8,128)S(1)} %collective-permute-done.6.tile, f32[8,128]{1,0:T(8,128)S(1)} %pad_add_fusion.3.div.own, ...), custom_call_target="tpu_custom_call" | custom-call | flops 503316480 | bytes 3153920 | tf_op jit(solution)/shard_map/pallas_call | solution.py:272
  26.6 0.0 collective-permute-done.div
  26.6 1.5 %shard_map.96 = f32[2,4,128,128]{3,2,1,0:T(8,128)} custom-call(f32[1544,128]{1,0:T(8,128)S(1)} %collective-permute-done.div, f32[8,128]{1,0:T(8,128)S(1)} %pad_add_fusion.3.div.own, bf16[6,256,128]{2,1,0:T(8,128)(2,1)S(1)} %get-tuple-element.38.p_high, bf16[6,256,128]{2,1,0:T(8,128)(2,1)S(1)} %get-tuple-element.39.p_low, ...), custom_call_target="tpu_custom_call" | custom-call | flops 301989888 | bytes 2760704 | tf_op jit(solution)/shard_map/pallas_call | solution.py:272
  (10 shorter events, 0.1 us)
Async XLA Ops:
  0.0 2.9 %copy-start.1 = (s32[2,6]{1,0:T(2,128)S(1)}, s32[2,6]{1,0:T(2,128)}, u32[]{:S(2)}) copy-start(s32[2,6]{1,0:T(2,128)} %param.10) | copy-start | bytes 148
  0.0 2.9 %copy-start.2 = (s32[2,6]{1,0:T(2,128)S(1)}, s32[2,6]{1,0:T(2,128)}, u32[]{:S(2)}) copy-start(s32[2,6]{1,0:T(2,128)} %param.11) | copy-start | bytes 148
  0.0 14.9 %collective-permute-start.1 = (f32[1280,128]{1,0:T(8,128)}, f32[1280,128]{1,0:T(8,128)S(1)}, u32[]{:S(2)}, u32[]{:S(2)}) collective-permute-start(f32[1280,128]{1,0:T(8,128)} %bitcast.9), channel_id=1, source_target_pairs={{0,8},{1,17},{2,10},{3,19},{4,12},{5,21},{6,14},{7,23},{8,0},{9,25... | collective-permute-start | bytes 1966088 | tf_op jit(solution)/shard_map/ppermute | solution.py:358
  3.0 1.3 %copy-start.5 = (s32[2]{0:T(128)S(1)}, s32[2]{0:T(128)}, u32[]{:S(2)}) copy-start(s32[2]{0:T(128)} %param.12) | copy-start | bytes 28
  3.0 4.4 %copy-start = (f32[2,5,128,128]{3,2,1,0:T(8,128)S(1)}, f32[2,5,128,128]{3,2,1,0:T(8,128)}, u32[]{:S(2)}) copy-start(f32[2,5,128,128]{3,2,1,0:T(8,128)} %param.13) | copy-start | bytes 1966084
  4.3 3.1 %copy-start.3 = (s32[2,5]{1,0:T(2,128)S(1)}, s32[2,5]{1,0:T(2,128)}, u32[]{:S(2)}) copy-start(s32[2,5]{1,0:T(2,128)} %param.14) | copy-start | bytes 124
  4.5 2.9 %copy-start.6 = (s32[2]{0:T(128)S(1)}, s32[2]{0:T(128)}, u32[]{:S(2)}) copy-start(s32[2]{0:T(128)} %param.15) | copy-start | bytes 28
  4.5 19.2 %collective-permute-start.4 = (f32[1544,128]{1,0:T(8,128)S(1)}, f32[1544,128]{1,0:T(8,128)S(1)}, u32[]{:S(2)}, u32[]{:S(2)}) collective-permute-start(f32[1544,128]{1,0:T(8,128)S(1)} %dynamic_update_slice.3.div), channel_id=1, source_target_pairs={{0,7},{1,0},{2,1},{3,2},{4,3},{5,4},{6,5},{7,6},{8,15},{9,8},{10,9... | collective-permute-start | bytes 2371592 | tf_op jit(solution)/shard_map/ppermute | solution.py:360
  7.3 19.3 %collective-permute-start = (f32[1544,128]{1,0:T(8,128)S(1)}, f32[1544,128]{1,0:T(8,128)S(1)}, u32[]{:S(2)}, u32[]{:S(2)}) collective-permute-start(f32[1544,128]{1,0:T(8,128)S(1)} %dynamic_update_slice.3.div), channel_id=1, source_target_pairs={{0,1},{1,2},{2,3},{3,4},{4,5},{5,6},{6,7},{7,0},{8,9},{9,10},{10,1... | collective-permute-start | bytes 2371592 | tf_op jit(solution)/shard_map/ppermute | solution.py:361
  7.4 14.6 %collective-permute-start.3 = (f32[1288,128]{1,0:T(8,128)S(1)}, f32[1288,128]{1,0:T(8,128)S(1)}, u32[]{:S(2)}, u32[]{:S(2)}) collective-permute-start(f32[1288,128]{1,0:T(8,128)S(1)} %pad_add_fusion.1.inv), channel_id=1, source_target_pairs={{0,16},{1,9},{2,18},{3,11},{4,20},{5,13},{6,22},{7,15},{8,24},{9,1... | collective-permute-start | bytes 1978376 | tf_op jit(solution)/shard_map/ppermute | solution.py:359
  14.9 4.4 %copy-start.4 = (s32[2,4]{1,0:T(2,128)S(1)}, s32[2,4]{1,0:T(2,128)}, u32[]{:S(2)}) copy-start(s32[2,4]{1,0:T(2,128)} %param.16) | copy-start | bytes 100
  14.9 10.6 %collective-permute-start.5 = (f32[1280,128]{1,0:T(8,128)S(1)}, f32[1280,128]{1,0:T(8,128)S(1)}, u32[]{:S(2)}, u32[]{:S(2)}) collective-permute-start(f32[1280,128]{1,0:T(8,128)S(1)} %collective-permute-done.1.inv), channel_id=1, source_target_pairs={{0,16},{1,9},{2,18},{3,11},{4,20},{5,13},{6,22},{7,15},{8,24},{9,1... | collective-permute-start | bytes 1966088 | tf_op jit(solution)/shard_map/ppermute | solution.py:372
  16.9 2.4 %copy-start.7 = (s32[2]{0:T(128)S(1)}, s32[2]{0:T(128)}, u32[]{:S(2)}) copy-start(s32[2]{0:T(128)} %param.17) | copy-start | bytes 28
  16.9 4.1 %collective-permute-start.2 = (f32[8,128]{1,0:T(8,128)S(1)}, f32[8,128]{1,0:T(8,128)S(1)}, u32[]{:S(2)}, u32[]{:S(2)}) collective-permute-start(f32[8,128]{1,0:T(8,128)S(1)} %pad_add_fusion.2), channel_id=1, source_target_pairs={{0,8},{1,17},{2,10},{3,19},{4,12},{5,21},{6,14},{7,23},{8,0},{9,25... | collective-permute-start | bytes 12296 | tf_op jit(solution)/shard_map/ppermute | solution.py:373
  21.0 4.6 %collective-permute-start.6 = (f32[8,128]{1,0:T(8,128)S(1)}, f32[8,128]{1,0:T(8,128)S(1)}, u32[]{:S(2)}, u32[]{:S(2)}) collective-permute-start(f32[8,128]{1,0:T(8,128)S(1)} %collective-permute-done.2.tile), channel_id=1, source_target_pairs={{0,16},{1,9},{2,18},{3,11},{4,20},{5,13},{6,22},{7,15},{8,24},{9,1... | collective-permute-start | bytes 12296 | tf_op jit(solution)/shard_map/ppermute | solution.py:374

commit v6 on v5

--- a/solution.py
+++ b/solution.py
@@ -11,8 +11,6 @@
 BF16 = jnp.bfloat16
 VMEM = pl.BlockSpec(memory_space=pltpu.VMEM)
 SMEM = pl.BlockSpec(memory_space=pltpu.SMEM)
-PACK_LIMIT = 60 << 20
-PARTS = 4
 
 
 def halves(value):
@@ -68,49 +66,6 @@
                 block = sums[row * side : (row + 1) * side, other * side : (other + 1) * side]
                 result = jnp.where(code == other, block, result)
             out[row, slot] = result
-
-
-def fetch(sources, targets, sems):
-    copies = [pltpu.make_async_copy(x, y, sems.at[i]) for i, (x, y) in enumerate(zip(sources, targets))]
-    for copy in copies:
-        copy.start()
-    return copies
-
-
-def kernel_pack(inv, div, *refs):
-    tables, (inv_out, div_out, tile_out), scratch = refs[:7], refs[7:10], refs[10:]
-    small_refs, (inv_buf, div_buf, small_sem, in_sem, out_sem) = scratch[:7], scratch[7:]
-    small = fetch(tables, small_refs, small_sem)
-    parts = in_sem.shape[1]
-    arrays = ((inv, inv_buf, inv_out), (div, div_buf, div_out))
-    cuts = [[pl.ds(j * (x.shape[0] // parts), x.shape[0] // parts) for j in range(parts)] for x in (inv, div)]
-    reads, writes = [], []
-    for i, (blocks, buf, out) in enumerate(arrays):
-        reads += fetch([blocks.at[cut] for cut in cuts[i]], [buf.at[cut] for cut in cuts[i]], in_sem.at[i])
-    for copy in small:
-        copy.wait()
-    for i, tables in enumerate((small_refs[:2], small_refs[2:])):
-        _, buf, out = arrays[i]
-        at = rows = buf.shape[0] - 8
-        buf[pl.ds(rows, 8), :] = jnp.zeros((8, buf.shape[1]), F32)
-        for table in tables:
-            values = table[...].astype(F32)
-            height, length = (1, *values.shape)[-2:]
-            buf[pl.ds(at, height), pl.ds(0, length)] = values.reshape(height, length)
-            at += height
-        cuts[i].append(pl.ds(rows, 8))
-    tile = pltpu.make_async_copy(inv_buf.at[cuts[0][-1]], tile_out, small_sem.at[0])
-    tile.start()
-    writes.append(tile)
-    for i, (_, buf, out) in enumerate(arrays):
-        for j, cut in enumerate(cuts[i]):
-            if j < parts:
-                reads[i * parts + j].wait()
-            copy = pltpu.make_async_copy(buf.at[cut], out.at[cut], out_sem.at[i, j])
-            copy.start()
-            writes.append(copy)
-    for copy in writes:
-        copy.wait()
 
 
 def integers(packed):

time: 28.2 us -> 28.2 us (level)
  no operation moved by 1% of the time
where the time goes in v6:
time: 28.2 us; the launch traced here: 28.1 us
  starting transfers between devices  11.3 us (40%)
  waiting for transfers between devices  8.73 us (31%)
  Pallas kernels  6.38 us (23%)
  other arithmetic  1.34 us (5%)
    pallas_call x6, Pallas kernels, call(): pl.pallas_call(kernel, out_shape=outs if len(outs) > 1 else outs[0], in_s...  6.38 us
    ppermute x1, waiting for transfers between devices, local(): inv_1 = lax.ppermute(inv_flat, ('row', 'col'), swap(True))  5.19 us
    ppermute x1, starting transfers between devices, local(): inv_1 = lax.ppermute(inv_flat, ('row', 'col'), swap(True))  2.94 us
    ppermute x1, starting transfers between devices, local(): follow = lax.ppermute(div, 'col', backward)  2.84 us
    ppermute x1, starting transfers between devices, local(): tile_1 = lax.ppermute(tile, ('row', 'col'), swap(True))  2.38 us
    ppermute x1, starting transfers between devices, local(): inv_3 = lax.ppermute(inv_1, ('row', 'col'), swap(False))  1.98 us
    ppermute x1, waiting for transfers between devices, local(): tile_1 = lax.ppermute(tile, ('row', 'col'), swap(True))  1.67 us
    add x4, other arithmetic, noted(): out + jnp.pad(table.astype(F32), ((at, height - at - lines), (0, side - l...  1.32 us
  transfers between devices with their start and end apart: 7, of which 4 were waited for; matrix products, arithmetic and copies ran while one was open for 5% of the time, Pallas kernels for 17%

profile of v6, /device:TPU:0, one launch (start us, length us, event | category | flops | bytes accessed | tf_op | source)
XLA Modules:
  0.0 28.1 jit_solution(11871646442386593565)
XLA Ops:
  0.0 0.0 copy-start.1
  0.0 0.0 copy-start.2
  0.0 2.9 %collective-permute-start.1 = (f32[1280,128]{1,0:T(8,128)}, f32[1280,128]{1,0:T(8,128)S(1)}, u32[]{:S(2)}, u32[]{:S(2)}) collective-permute-start(f32[1280,128]{1,0:T(8,128)} %bitcast.9), channel_id=1, source_target_pairs={{0,8},{1,17},{2,10},{3,19},{4,12},{5,21},{6,14},{7,23},{8,0},{9,25... | collective-permute-start | bytes 1966088 | tf_op jit(solution)/shard_map/ppermute | solution.py:313
  2.9 0.0 copy-done.1
  2.9 0.0 copy-done.2
  3.0 0.0 copy-start.5
  3.0 0.0 copy-start
  3.0 1.3 %pad_add_fusion = f32[1544,128]{1,0:T(8,128)S(1)} fusion(f32[2,6]{1,0:T(2,128)S(1)} %convert_element_type.55, f32[2,6]{1,0:T(2,128)S(1)} %convert_element_type.54, f32[1536,128]{1,0:T(8,128)} %bitcast.8), kind=kLoop, calls=%fused_computation | loop fusion | flops 395264 | bytes 1577056 | tf_op jit(solution)/shard_map/add | solution.py:295
  4.2 0.0 copy-done.5
  4.3 0.0 copy-start.3
  4.3 0.2 dynamic_update_slice.3.div
  4.5 0.0 copy-start.6
  4.5 2.8 %collective-permute-start.4 = (f32[1544,128]{1,0:T(8,128)S(1)}, f32[1544,128]{1,0:T(8,128)S(1)}, u32[]{:S(2)}, u32[]{:S(2)}) collective-permute-start(f32[1544,128]{1,0:T(8,128)S(1)} %dynamic_update_slice.3.div), channel_id=1, source_target_pairs={{0,7},{1,0},{2,1},{3,2},{4,3},{5,4},{6,5},{7,6},{8,15},{9,8},{10,9... | collective-permute-start | bytes 2371592 | tf_op jit(solution)/shard_map/ppermute | solution.py:315
  7.3 0.0 collective-permute-start
  7.3 0.0 copy-done.3
  7.3 0.0 copy-done.6
  7.4 0.0 copy-done
  7.4 1.0 %collective-permute-start.3 = (f32[1288,128]{1,0:T(8,128)S(1)}, f32[1288,128]{1,0:T(8,128)S(1)}, u32[]{:S(2)}, u32[]{:S(2)}) collective-permute-start(f32[1288,128]{1,0:T(8,128)S(1)} %pad_add_fusion.1.inv), channel_id=1, source_target_pairs={{0,16},{1,9},{2,18},{3,11},{4,20},{5,13},{6,22},{7,15},{8,24},{9,1... | collective-permute-start | bytes 1978376 | tf_op jit(solution)/shard_map/ppermute | solution.py:314
  8.4 1.3 %shard_map.91 = (bf16[4,256,256]{2,1,0:T(8,128)(2,1)S(1)}, bf16[4,256,256]{2,1,0:T(8,128)(2,1)S(1)}, bf16[256,768]{1,0:T(8,128)(2,1)S(1)}, bf16[256,768]{1,0:T(8,128)(2,1)S(1)}, f32[256,256]{1,0:T(8,128)S(1)}) custom-call(f32[1544,128]{1,0:T(8,128)S(1)} %dynamic_update_slice.3.div, f32[1288,128]{1,0:T(8,128)S(1)} %pad_add_fusion.1.inv), custom_call_target="tpu_custom_call" | custom-call | flops 402653184 | bytes 3547136 | tf_op jit(solution)/shard_map/pallas_call | solution.py:227
  9.7 5.2 %collective-permute-done.1.inv = f32[1280,128]{1,0:T(8,128)S(1)} collective-permute-done((f32[1280,128]{1,0:T(8,128)}, f32[1280,128]{1,0:T(8,128)S(1)}, u32[]{:S(2)}, u32[]{:S(2)}) %collective-permute-start.1) | collective-permute-done | bytes 655392 | tf_op jit(solution)/shard_map/ppermute | solution.py:313
  14.9 0.0 copy-start.4
  14.9 2.0 %collective-permute-start.5 = (f32[1280,128]{1,0:T(8,128)S(1)}, f32[1280,128]{1,0:T(8,128)S(1)}, u32[]{:S(2)}, u32[]{:S(2)}) collective-permute-start(f32[1280,128]{1,0:T(8,128)S(1)} %collective-permute-done.1.inv), channel_id=1, source_target_pairs={{0,16},{1,9},{2,18},{3,11},{4,20},{5,13},{6,22},{7,15},{8,24},{9,1... | collective-permute-start | bytes 1966088 | tf_op jit(solution)/shard_map/ppermute | solution.py:327
  16.9 0.0 copy-start.7
  16.9 2.4 %collective-permute-start.2 = (f32[8,128]{1,0:T(8,128)S(1)}, f32[8,128]{1,0:T(8,128)S(1)}, u32[]{:S(2)}, u32[]{:S(2)}) collective-permute-start(f32[8,128]{1,0:T(8,128)S(1)} %pad_add_fusion.2), channel_id=1, source_target_pairs={{0,8},{1,17},{2,10},{3,19},{4,12},{5,21},{6,14},{7,23},{8,0},{9,25... | collective-permute-start | bytes 12296 | tf_op jit(solution)/shard_map/ppermute | solution.py:328
  19.3 0.0 copy-done.4
  19.3 0.0 copy-done.7
  19.3 1.7 %collective-permute-done.2.tile = f32[8,128]{1,0:T(8,128)S(1)} collective-permute-done((f32[8,128]{1,0:T(8,128)S(1)}, f32[8,128]{1,0:T(8,128)S(1)}, u32[]{:S(2)}, u32[]{:S(2)}) %collective-permute-start.2) | collective-permute-done | bytes 4128 | tf_op jit(solution)/shard_map/ppermute | solution.py:328
  21.0 0.1 collective-permute-start.6
  21.1 0.9 %shard_map.92 = (bf16[256,768]{1,0:T(8,128)(2,1)S(1)}, bf16[256,768]{1,0:T(8,128)(2,1)S(1)}, f32[256,256]{1,0:T(8,128)S(1)}) custom-call(f32[1280,128]{1,0:T(8,128)S(1)} %collective-permute-done.1.inv, f32[8,128]{1,0:T(8,128)S(1)} %collective-permute-done.2.tile, bf16[4,256,256]{2,1,0:T(8,128)(2,1)S(1)} %get-tuple-element.30.b_high, ...), custom_call_target="tpu_custom_call" | custom-call | flops 402653184 | bytes 3018752 | tf_op jit(solution)/shard_map/pallas_call | solution.py:227
  22.0 0.0 collective-permute-done.3.inv.tile
  22.0 0.9 %shard_map.93 = (bf16[256,768]{1,0:T(8,128)(2,1)S(1)}, bf16[256,768]{1,0:T(8,128)(2,1)S(1)}, f32[256,256]{1,0:T(8,128)S(1)}) custom-call(f32[1288,128]{1,0:T(8,128)S(1)} %collective-permute-done.3.inv.tile, f32[1288,128]{1,0:T(8,128)S(1)} %collective-permute-done.3.inv.tile, bf16[4,256,256]{2,1,0:T(8,128)(2,1)S(1)} %get-tuple-element.30.b_high, ...), custom_call_target="tpu_custom_call" | custom-call | flops 402653184 | bytes 3678208 | tf_op jit(solution)/shard_map/pallas_call | solution.py:227
  22.9 0.8 %collective-permute-done.4.div = f32[1544,128]{1,0:T(8,128)S(1)} collective-permute-done((f32[1544,128]{1,0:T(8,128)S(1)}, f32[1544,128]{1,0:T(8,128)S(1)}, u32[]{:S(2)}, u32[]{:S(2)}) %collective-permute-start.4) | collective-permute-done | bytes 790560 | tf_op jit(solution)/shard_map/ppermute | solution.py:315
  23.7 0.8 %shard_map.94 = (f32[256,256]{1,0:T(8,128)S(1)}, bf16[256,256]{1,0:T(8,128)(2,1)S(1)}, bf16[256,256]{1,0:T(8,128)(2,1)S(1)}, bf16[6,256,128]{2,1,0:T(8,128)(2,1)S(1)}, bf16[6,256,128]{2,1,0:T(8,128)(2,1)S(1)}) custom-call(bf16[256,768]{1,0:T(8,128)(2,1)S(1)} %get-tuple-element.26.y0_high, bf16[256,768]{1,0:T(8,128)(2,1)S(1)} %get-tuple-element.27.y0_low, ...), custom_call_target="tpu_custom_call" | custom-call | flops 301989888 | bytes 4460544 | tf_op jit(solution)/shard_map/pallas_call | solution.py:227
  24.5 1.1 %collective-permute-done.6.tile = f32[8,128]{1,0:T(8,128)S(1)} collective-permute-done((f32[8,128]{1,0:T(8,128)S(1)}, f32[8,128]{1,0:T(8,128)S(1)}, u32[]{:S(2)}, u32[]{:S(2)}) %collective-permute-start.6) | collective-permute-done | bytes 4128 | tf_op jit(solution)/shard_map/ppermute | solution.py:329
  25.6 0.0 collective-permute-done.5.inv
  25.6 1.0 %shard_map.95 = (f32[2,3,128,128]{3,2,1,0:T(8,128)S(1)}, bf16[2,256,128]{2,1,0:T(8,128)(2,1)S(1)}, bf16[2,256,128]{2,1,0:T(8,128)(2,1)S(1)}) custom-call(f32[1280,128]{1,0:T(8,128)S(1)} %collective-permute-done.5.inv, f32[8,128]{1,0:T(8,128)S(1)} %collective-permute-done.6.tile, f32[8,128]{1,0:T(8,128)S(1)} %pad_add_fusion.3.div.own, ...), custom_call_target="tpu_custom_call" | custom-call | flops 503316480 | bytes 3153920 | tf_op jit(solution)/shard_map/pallas_call | solution.py:227
  26.6 0.0 collective-permute-done.div
  26.6 1.5 %shard_map.96 = f32[2,4,128,128]{3,2,1,0:T(8,128)} custom-call(f32[1544,128]{1,0:T(8,128)S(1)} %collective-permute-done.div, f32[8,128]{1,0:T(8,128)S(1)} %pad_add_fusion.3.div.own, bf16[6,256,128]{2,1,0:T(8,128)(2,1)S(1)} %get-tuple-element.38.p_high, bf16[6,256,128]{2,1,0:T(8,128)(2,1)S(1)} %get-tuple-element.39.p_low, ...), custom_call_target="tpu_custom_call" | custom-call | flops 301989888 | bytes 2760704 | tf_op jit(solution)/shard_map/pallas_call | solution.py:227
  (10 shorter events, 0.1 us)
Async XLA Ops:
  0.0 2.9 %copy-start.1 = (s32[2,6]{1,0:T(2,128)S(1)}, s32[2,6]{1,0:T(2,128)}, u32[]{:S(2)}) copy-start(s32[2,6]{1,0:T(2,128)} %param.10) | copy-start | bytes 148
  0.0 2.9 %copy-start.2 = (s32[2,6]{1,0:T(2,128)S(1)}, s32[2,6]{1,0:T(2,128)}, u32[]{:S(2)}) copy-start(s32[2,6]{1,0:T(2,128)} %param.11) | copy-start | bytes 148
  0.0 14.9 %collective-permute-start.1 = (f32[1280,128]{1,0:T(8,128)}, f32[1280,128]{1,0:T(8,128)S(1)}, u32[]{:S(2)}, u32[]{:S(2)}) collective-permute-start(f32[1280,128]{1,0:T(8,128)} %bitcast.9), channel_id=1, source_target_pairs={{0,8},{1,17},{2,10},{3,19},{4,12},{5,21},{6,14},{7,23},{8,0},{9,25... | collective-permute-start | bytes 1966088 | tf_op jit(solution)/shard_map/ppermute | solution.py:313
  3.0 1.3 %copy-start.5 = (s32[2]{0:T(128)S(1)}, s32[2]{0:T(128)}, u32[]{:S(2)}) copy-start(s32[2]{0:T(128)} %param.12) | copy-start | bytes 28
  3.0 4.4 %copy-start = (f32[2,5,128,128]{3,2,1,0:T(8,128)S(1)}, f32[2,5,128,128]{3,2,1,0:T(8,128)}, u32[]{:S(2)}) copy-start(f32[2,5,128,128]{3,2,1,0:T(8,128)} %param.13) | copy-start | bytes 1966084
  4.3 3.1 %copy-start.3 = (s32[2,5]{1,0:T(2,128)S(1)}, s32[2,5]{1,0:T(2,128)}, u32[]{:S(2)}) copy-start(s32[2,5]{1,0:T(2,128)} %param.14) | copy-start | bytes 124
  4.5 2.9 %copy-start.6 = (s32[2]{0:T(128)S(1)}, s32[2]{0:T(128)}, u32[]{:S(2)}) copy-start(s32[2]{0:T(128)} %param.15) | copy-start | bytes 28
  4.5 19.2 %collective-permute-start.4 = (f32[1544,128]{1,0:T(8,128)S(1)}, f32[1544,128]{1,0:T(8,128)S(1)}, u32[]{:S(2)}, u32[]{:S(2)}) collective-permute-start(f32[1544,128]{1,0:T(8,128)S(1)} %dynamic_update_slice.3.div), channel_id=1, source_target_pairs={{0,7},{1,0},{2,1},{3,2},{4,3},{5,4},{6,5},{7,6},{8,15},{9,8},{10,9... | collective-permute-start | bytes 2371592 | tf_op jit(solution)/shard_map/ppermute | solution.py:315
  7.3 19.3 %collective-permute-start = (f32[1544,128]{1,0:T(8,128)S(1)}, f32[1544,128]{1,0:T(8,128)S(1)}, u32[]{:S(2)}, u32[]{:S(2)}) collective-permute-start(f32[1544,128]{1,0:T(8,128)S(1)} %dynamic_update_slice.3.div), channel_id=1, source_target_pairs={{0,1},{1,2},{2,3},{3,4},{4,5},{5,6},{6,7},{7,0},{8,9},{9,10},{10,1... | collective-permute-start | bytes 2371592 | tf_op jit(solution)/shard_map/ppermute | solution.py:316
  7.4 14.6 %collective-permute-start.3 = (f32[1288,128]{1,0:T(8,128)S(1)}, f32[1288,128]{1,0:T(8,128)S(1)}, u32[]{:S(2)}, u32[]{:S(2)}) collective-permute-start(f32[1288,128]{1,0:T(8,128)S(1)} %pad_add_fusion.1.inv), channel_id=1, source_target_pairs={{0,16},{1,9},{2,18},{3,11},{4,20},{5,13},{6,22},{7,15},{8,24},{9,1... | collective-permute-start | bytes 1978376 | tf_op jit(solution)/shard_map/ppermute | solution.py:314
  14.9 4.4 %copy-start.4 = (s32[2,4]{1,0:T(2,128)S(1)}, s32[2,4]{1,0:T(2,128)}, u32[]{:S(2)}) copy-start(s32[2,4]{1,0:T(2,128)} %param.16) | copy-start | bytes 100
  14.9 10.6 %collective-permute-start.5 = (f32[1280,128]{1,0:T(8,128)S(1)}, f32[1280,128]{1,0:T(8,128)S(1)}, u32[]{:S(2)}, u32[]{:S(2)}) collective-permute-start(f32[1280,128]{1,0:T(8,128)S(1)} %collective-permute-done.1.inv), channel_id=1, source_target_pairs={{0,16},{1,9},{2,18},{3,11},{4,20},{5,13},{6,22},{7,15},{8,24},{9,1... | collective-permute-start | bytes 1966088 | tf_op jit(solution)/shard_map/ppermute | solution.py:327
  16.9 2.4 %copy-start.7 = (s32[2]{0:T(128)S(1)}, s32[2]{0:T(128)}, u32[]{:S(2)}) copy-start(s32[2]{0:T(128)} %param.17) | copy-start | bytes 28
  16.9 4.1 %collective-permute-start.2 = (f32[8,128]{1,0:T(8,128)S(1)}, f32[8,128]{1,0:T(8,128)S(1)}, u32[]{:S(2)}, u32[]{:S(2)}) collective-permute-start(f32[8,128]{1,0:T(8,128)S(1)} %pad_add_fusion.2), channel_id=1, source_target_pairs={{0,8},{1,17},{2,10},{3,19},{4,12},{5,21},{6,14},{7,23},{8,0},{9,25... | collective-permute-start | bytes 12296 | tf_op jit(solution)/shard_map/ppermute | solution.py:328
  21.0 4.6 %collective-permute-start.6 = (f32[8,128]{1,0:T(8,128)S(1)}, f32[8,128]{1,0:T(8,128)S(1)}, u32[]{:S(2)}, u32[]{:S(2)}) collective-permute-start(f32[8,128]{1,0:T(8,128)S(1)} %collective-permute-done.2.tile), channel_id=1, source_target_pairs={{0,16},{1,9},{2,18},{3,11},{4,20},{5,13},{6,22},{7,15},{8,24},{9,1... | collective-permute-start | bytes 12296 | tf_op jit(solution)/shard_map/ppermute | solution.py:329

commit v7 on v6

--- a/solution.py
+++ b/solution.py
@@ -175,6 +175,7 @@
         copies[-1].start()
     codes = div_codes(integers(div), sizes)
     targets = target_codes(integers(own), rows, pattern)
+    factors = []
     for row in range(rows):
         target = targets[row * pattern + pattern - 1]
         place = pl.ds(row * side, side)
@@ -186,11 +187,13 @@
                 code = jnp.where(other == i, codes[i * slots + slot], code)
             source = pl.multiple_of((other * slots + slot) * side, side)
             live = jnp.where((code >= 0) & (target >= 0), 1.0, 0.0)
-            right.append(div[pl.ds(source, side), :] * live)
+            right.append(halves(div[pl.ds(source, side), :] * live))
             at, late = jnp.clip(code, 0, known - 1), jnp.maximum(code - known, 0)
             for part, early, last in zip(left, (p_high, p_low), (q_high, q_low)):
                 part.append(jnp.where(code < known, early[at, place, :], last[late, place, :]))
-        buf[row] = product([jnp.concatenate(x, axis=1) for x in left], halves(jnp.concatenate(right, axis=1)), True)
+        factors.append([[jnp.concatenate(x, axis=1) for x in pair] for pair in (left, zip(*right))])
+    for row, (left, right) in enumerate(factors):
+        buf[row] = product(left, right, True)
         copies.append(pltpu.make_async_copy(buf.at[row], out.at[row, pattern - 1], sems.at[1, row]))
         copies[-1].start()
     for copy in copies:

time: 28.2 us -> 28.2 us (level)
  no operation moved by 1% of the time
where the time goes in v7:
time: 28.2 us; the launch traced here: 28.1 us
  starting transfers between devices  11.3 us (40%)
  waiting for transfers between devices  8.77 us (31%)
  Pallas kernels  6.34 us (22%)
  other arithmetic  1.34 us (5%)
    pallas_call x6, Pallas kernels, call(): pl.pallas_call(kernel, out_shape=outs if len(outs) > 1 else outs[0], in_s...  6.34 us
    ppermute x1, waiting for transfers between devices, local(): inv_1 = lax.ppermute(inv_flat, ('row', 'col'), swap(True))  5.21 us
    ppermute x1, starting transfers between devices, local(): inv_1 = lax.ppermute(inv_flat, ('row', 'col'), swap(True))  2.94 us
    ppermute x1, starting transfers between devices, local(): follow = lax.ppermute(div, 'col', backward)  2.84 us
    ppermute x1, starting transfers between devices, local(): tile_1 = lax.ppermute(tile, ('row', 'col'), swap(True))  2.38 us
    ppermute x1, starting transfers between devices, local(): inv_3 = lax.ppermute(inv_1, ('row', 'col'), swap(False))  1.98 us
    ppermute x1, waiting for transfers between devices, local(): tile_1 = lax.ppermute(tile, ('row', 'col'), swap(True))  1.67 us
    add x4, other arithmetic, noted(): out + jnp.pad(table.astype(F32), ((at, height - at - lines), (0, side - l...  1.32 us
  transfers between devices with their start and end apart: 7, of which 4 were waited for; matrix products, arithmetic and copies ran while one was open for 5% of the time, Pallas kernels for 17%

profile of v7, /device:TPU:0, one launch (start us, length us, event | category | flops | bytes accessed | tf_op | source)
XLA Modules:
  0.0 28.1 jit_solution(11871646442386593565)
XLA Ops:
  0.0 0.0 copy-start.1
  0.0 0.0 copy-start.2
  0.0 2.9 %collective-permute-start.1 = (f32[1280,128]{1,0:T(8,128)}, f32[1280,128]{1,0:T(8,128)S(1)}, u32[]{:S(2)}, u32[]{:S(2)}) collective-permute-start(f32[1280,128]{1,0:T(8,128)} %bitcast.9), channel_id=1, source_target_pairs={{0,8},{1,17},{2,10},{3,19},{4,12},{5,21},{6,14},{7,23},{8,0},{9,25... | collective-permute-start | bytes 1966088 | tf_op jit(solution)/shard_map/ppermute | solution.py:316
  2.9 0.0 copy-done.1
  2.9 0.0 copy-done.2
  3.0 0.0 copy-start.5
  3.0 0.0 copy-start
  3.0 1.3 %pad_add_fusion = f32[1544,128]{1,0:T(8,128)S(1)} fusion(f32[2,6]{1,0:T(2,128)S(1)} %convert_element_type.55, f32[2,6]{1,0:T(2,128)S(1)} %convert_element_type.54, f32[1536,128]{1,0:T(8,128)} %bitcast.8), kind=kLoop, calls=%fused_computation | loop fusion | flops 395264 | bytes 1577056 | tf_op jit(solution)/shard_map/add | solution.py:298
  4.2 0.0 copy-done.5
  4.3 0.0 copy-start.3
  4.3 0.2 dynamic_update_slice.3.div
  4.5 0.0 copy-start.6
  4.5 2.8 %collective-permute-start.4 = (f32[1544,128]{1,0:T(8,128)S(1)}, f32[1544,128]{1,0:T(8,128)S(1)}, u32[]{:S(2)}, u32[]{:S(2)}) collective-permute-start(f32[1544,128]{1,0:T(8,128)S(1)} %dynamic_update_slice.3.div), channel_id=1, source_target_pairs={{0,7},{1,0},{2,1},{3,2},{4,3},{5,4},{6,5},{7,6},{8,15},{9,8},{10,9... | collective-permute-start | bytes 2371592 | tf_op jit(solution)/shard_map/ppermute | solution.py:318
  7.3 0.0 collective-permute-start
  7.3 0.0 copy-done.3
  7.3 0.0 copy-done.6
  7.4 0.0 copy-done
  7.4 1.0 %collective-permute-start.3 = (f32[1288,128]{1,0:T(8,128)S(1)}, f32[1288,128]{1,0:T(8,128)S(1)}, u32[]{:S(2)}, u32[]{:S(2)}) collective-permute-start(f32[1288,128]{1,0:T(8,128)S(1)} %pad_add_fusion.1.inv), channel_id=1, source_target_pairs={{0,16},{1,9},{2,18},{3,11},{4,20},{5,13},{6,22},{7,15},{8,24},{9,1... | collective-permute-start | bytes 1978376 | tf_op jit(solution)/shard_map/ppermute | solution.py:317
  8.4 1.3 %shard_map.91 = (bf16[4,256,256]{2,1,0:T(8,128)(2,1)S(1)}, bf16[4,256,256]{2,1,0:T(8,128)(2,1)S(1)}, bf16[256,768]{1,0:T(8,128)(2,1)S(1)}, bf16[256,768]{1,0:T(8,128)(2,1)S(1)}, f32[256,256]{1,0:T(8,128)S(1)}) custom-call(f32[1544,128]{1,0:T(8,128)S(1)} %dynamic_update_slice.3.div, f32[1288,128]{1,0:T(8,128)S(1)} %pad_add_fusion.1.inv), custom_call_target="tpu_custom_call" | custom-call | flops 402653184 | bytes 3547136 | tf_op jit(solution)/shard_map/pallas_call | solution.py:230
  9.7 5.2 %collective-permute-done.1.inv = f32[1280,128]{1,0:T(8,128)S(1)} collective-permute-done((f32[1280,128]{1,0:T(8,128)}, f32[1280,128]{1,0:T(8,128)S(1)}, u32[]{:S(2)}, u32[]{:S(2)}) %collective-permute-start.1) | collective-permute-done | bytes 655392 | tf_op jit(solution)/shard_map/ppermute | solution.py:316
  14.9 0.0 copy-start.4
  14.9 2.0 %collective-permute-start.5 = (f32[1280,128]{1,0:T(8,128)S(1)}, f32[1280,128]{1,0:T(8,128)S(1)}, u32[]{:S(2)}, u32[]{:S(2)}) collective-permute-start(f32[1280,128]{1,0:T(8,128)S(1)} %collective-permute-done.1.inv), channel_id=1, source_target_pairs={{0,16},{1,9},{2,18},{3,11},{4,20},{5,13},{6,22},{7,15},{8,24},{9,1... | collective-permute-start | bytes 1966088 | tf_op jit(solution)/shard_map/ppermute | solution.py:330
  16.9 0.0 copy-start.7
  16.9 2.4 %collective-permute-start.2 = (f32[8,128]{1,0:T(8,128)S(1)}, f32[8,128]{1,0:T(8,128)S(1)}, u32[]{:S(2)}, u32[]{:S(2)}) collective-permute-start(f32[8,128]{1,0:T(8,128)S(1)} %pad_add_fusion.2), channel_id=1, source_target_pairs={{0,8},{1,17},{2,10},{3,19},{4,12},{5,21},{6,14},{7,23},{8,0},{9,25... | collective-permute-start | bytes 12296 | tf_op jit(solution)/shard_map/ppermute | solution.py:331
  19.3 0.0 copy-done.4
  19.3 0.0 copy-done.7
  19.3 1.7 %collective-permute-done.2.tile = f32[8,128]{1,0:T(8,128)S(1)} collective-permute-done((f32[8,128]{1,0:T(8,128)S(1)}, f32[8,128]{1,0:T(8,128)S(1)}, u32[]{:S(2)}, u32[]{:S(2)}) %collective-permute-start.2) | collective-permute-done | bytes 4128 | tf_op jit(solution)/shard_map/ppermute | solution.py:331
  21.0 0.1 collective-permute-start.6
  21.1 0.9 %shard_map.92 = (bf16[256,768]{1,0:T(8,128)(2,1)S(1)}, bf16[256,768]{1,0:T(8,128)(2,1)S(1)}, f32[256,256]{1,0:T(8,128)S(1)}) custom-call(f32[1280,128]{1,0:T(8,128)S(1)} %collective-permute-done.1.inv, f32[8,128]{1,0:T(8,128)S(1)} %collective-permute-done.2.tile, bf16[4,256,256]{2,1,0:T(8,128)(2,1)S(1)} %get-tuple-element.30.b_high, ...), custom_call_target="tpu_custom_call" | custom-call | flops 402653184 | bytes 3018752 | tf_op jit(solution)/shard_map/pallas_call | solution.py:230
  22.0 0.0 collective-permute-done.3.inv.tile
  22.0 0.9 %shard_map.93 = (bf16[256,768]{1,0:T(8,128)(2,1)S(1)}, bf16[256,768]{1,0:T(8,128)(2,1)S(1)}, f32[256,256]{1,0:T(8,128)S(1)}) custom-call(f32[1288,128]{1,0:T(8,128)S(1)} %collective-permute-done.3.inv.tile, f32[1288,128]{1,0:T(8,128)S(1)} %collective-permute-done.3.inv.tile, bf16[4,256,256]{2,1,0:T(8,128)(2,1)S(1)} %get-tuple-element.30.b_high, ...), custom_call_target="tpu_custom_call" | custom-call | flops 402653184 | bytes 3678208 | tf_op jit(solution)/shard_map/pallas_call | solution.py:230
  22.9 0.8 %collective-permute-done.4.div = f32[1544,128]{1,0:T(8,128)S(1)} collective-permute-done((f32[1544,128]{1,0:T(8,128)S(1)}, f32[1544,128]{1,0:T(8,128)S(1)}, u32[]{:S(2)}, u32[]{:S(2)}) %collective-permute-start.4) | collective-permute-done | bytes 790560 | tf_op jit(solution)/shard_map/ppermute | solution.py:318
  23.7 0.8 %shard_map.94 = (f32[256,256]{1,0:T(8,128)S(1)}, bf16[256,256]{1,0:T(8,128)(2,1)S(1)}, bf16[256,256]{1,0:T(8,128)(2,1)S(1)}, bf16[6,256,128]{2,1,0:T(8,128)(2,1)S(1)}, bf16[6,256,128]{2,1,0:T(8,128)(2,1)S(1)}) custom-call(bf16[256,768]{1,0:T(8,128)(2,1)S(1)} %get-tuple-element.26.y0_high, bf16[256,768]{1,0:T(8,128)(2,1)S(1)} %get-tuple-element.27.y0_low, ...), custom_call_target="tpu_custom_call" | custom-call | flops 301989888 | bytes 4460544 | tf_op jit(solution)/shard_map/pallas_call | solution.py:230
  24.5 1.1 %collective-permute-done.6.tile = f32[8,128]{1,0:T(8,128)S(1)} collective-permute-done((f32[8,128]{1,0:T(8,128)S(1)}, f32[8,128]{1,0:T(8,128)S(1)}, u32[]{:S(2)}, u32[]{:S(2)}) %collective-permute-start.6) | collective-permute-done | bytes 4128 | tf_op jit(solution)/shard_map/ppermute | solution.py:332
  25.6 0.0 collective-permute-done.5.inv
  25.6 1.0 %shard_map.95 = (f32[2,3,128,128]{3,2,1,0:T(8,128)S(1)}, bf16[2,256,128]{2,1,0:T(8,128)(2,1)S(1)}, bf16[2,256,128]{2,1,0:T(8,128)(2,1)S(1)}) custom-call(f32[1280,128]{1,0:T(8,128)S(1)} %collective-permute-done.5.inv, f32[8,128]{1,0:T(8,128)S(1)} %collective-permute-done.6.tile, f32[8,128]{1,0:T(8,128)S(1)} %pad_add_fusion.3.div.own, ...), custom_call_target="tpu_custom_call" | custom-call | flops 503316480 | bytes 3153920 | tf_op jit(solution)/shard_map/pallas_call | solution.py:230
  26.6 0.0 collective-permute-done.div
  26.6 1.5 %shard_map.96 = f32[2,4,128,128]{3,2,1,0:T(8,128)} custom-call(f32[1544,128]{1,0:T(8,128)S(1)} %collective-permute-done.div, f32[8,128]{1,0:T(8,128)S(1)} %pad_add_fusion.3.div.own, bf16[6,256,128]{2,1,0:T(8,128)(2,1)S(1)} %get-tuple-element.38.p_high, bf16[6,256,128]{2,1,0:T(8,128)(2,1)S(1)} %get-tuple-element.39.p_low, ...), custom_call_target="tpu_custom_call" | custom-call | flops 301989888 | bytes 2760704 | tf_op jit(solution)/shard_map/pallas_call | solution.py:230
  (10 shorter events, 0.1 us)
Async XLA Ops:
  0.0 2.9 %copy-start.1 = (s32[2,6]{1,0:T(2,128)S(1)}, s32[2,6]{1,0:T(2,128)}, u32[]{:S(2)}) copy-start(s32[2,6]{1,0:T(2,128)} %param.10) | copy-start | bytes 148
  0.0 2.9 %copy-start.2 = (s32[2,6]{1,0:T(2,128)S(1)}, s32[2,6]{1,0:T(2,128)}, u32[]{:S(2)}) copy-start(s32[2,6]{1,0:T(2,128)} %param.11) | copy-start | bytes 148
  0.0 14.9 %collective-permute-start.1 = (f32[1280,128]{1,0:T(8,128)}, f32[1280,128]{1,0:T(8,128)S(1)}, u32[]{:S(2)}, u32[]{:S(2)}) collective-permute-start(f32[1280,128]{1,0:T(8,128)} %bitcast.9), channel_id=1, source_target_pairs={{0,8},{1,17},{2,10},{3,19},{4,12},{5,21},{6,14},{7,23},{8,0},{9,25... | collective-permute-start | bytes 1966088 | tf_op jit(solution)/shard_map/ppermute | solution.py:316
  3.0 1.3 %copy-start.5 = (s32[2]{0:T(128)S(1)}, s32[2]{0:T(128)}, u32[]{:S(2)}) copy-start(s32[2]{0:T(128)} %param.12) | copy-start | bytes 28
  3.0 4.4 %copy-start = (f32[2,5,128,128]{3,2,1,0:T(8,128)S(1)}, f32[2,5,128,128]{3,2,1,0:T(8,128)}, u32[]{:S(2)}) copy-start(f32[2,5,128,128]{3,2,1,0:T(8,128)} %param.13) | copy-start | bytes 1966084
  4.3 3.1 %copy-start.3 = (s32[2,5]{1,0:T(2,128)S(1)}, s32[2,5]{1,0:T(2,128)}, u32[]{:S(2)}) copy-start(s32[2,5]{1,0:T(2,128)} %param.14) | copy-start | bytes 124
  4.5 2.9 %copy-start.6 = (s32[2]{0:T(128)S(1)}, s32[2]{0:T(128)}, u32[]{:S(2)}) copy-start(s32[2]{0:T(128)} %param.15) | copy-start | bytes 28
  4.5 19.2 %collective-permute-start.4 = (f32[1544,128]{1,0:T(8,128)S(1)}, f32[1544,128]{1,0:T(8,128)S(1)}, u32[]{:S(2)}, u32[]{:S(2)}) collective-permute-start(f32[1544,128]{1,0:T(8,128)S(1)} %dynamic_update_slice.3.div), channel_id=1, source_target_pairs={{0,7},{1,0},{2,1},{3,2},{4,3},{5,4},{6,5},{7,6},{8,15},{9,8},{10,9... | collective-permute-start | bytes 2371592 | tf_op jit(solution)/shard_map/ppermute | solution.py:318
  7.3 19.3 %collective-permute-start = (f32[1544,128]{1,0:T(8,128)S(1)}, f32[1544,128]{1,0:T(8,128)S(1)}, u32[]{:S(2)}, u32[]{:S(2)}) collective-permute-start(f32[1544,128]{1,0:T(8,128)S(1)} %dynamic_update_slice.3.div), channel_id=1, source_target_pairs={{0,1},{1,2},{2,3},{3,4},{4,5},{5,6},{6,7},{7,0},{8,9},{9,10},{10,1... | collective-permute-start | bytes 2371592 | tf_op jit(solution)/shard_map/ppermute | solution.py:319
  7.4 14.6 %collective-permute-start.3 = (f32[1288,128]{1,0:T(8,128)S(1)}, f32[1288,128]{1,0:T(8,128)S(1)}, u32[]{:S(2)}, u32[]{:S(2)}) collective-permute-start(f32[1288,128]{1,0:T(8,128)S(1)} %pad_add_fusion.1.inv), channel_id=1, source_target_pairs={{0,16},{1,9},{2,18},{3,11},{4,20},{5,13},{6,22},{7,15},{8,24},{9,1... | collective-permute-start | bytes 1978376 | tf_op jit(solution)/shard_map/ppermute | solution.py:317
  14.9 4.4 %copy-start.4 = (s32[2,4]{1,0:T(2,128)S(1)}, s32[2,4]{1,0:T(2,128)}, u32[]{:S(2)}) copy-start(s32[2,4]{1,0:T(2,128)} %param.16) | copy-start | bytes 100
  14.9 10.6 %collective-permute-start.5 = (f32[1280,128]{1,0:T(8,128)S(1)}, f32[1280,128]{1,0:T(8,128)S(1)}, u32[]{:S(2)}, u32[]{:S(2)}) collective-permute-start(f32[1280,128]{1,0:T(8,128)S(1)} %collective-permute-done.1.inv), channel_id=1, source_target_pairs={{0,16},{1,9},{2,18},{3,11},{4,20},{5,13},{6,22},{7,15},{8,24},{9,1... | collective-permute-start | bytes 1966088 | tf_op jit(solution)/shard_map/ppermute | solution.py:330
  16.9 2.4 %copy-start.7 = (s32[2]{0:T(128)S(1)}, s32[2]{0:T(128)}, u32[]{:S(2)}) copy-start(s32[2]{0:T(128)} %param.17) | copy-start | bytes 28
  16.9 4.1 %collective-permute-start.2 = (f32[8,128]{1,0:T(8,128)S(1)}, f32[8,128]{1,0:T(8,128)S(1)}, u32[]{:S(2)}, u32[]{:S(2)}) collective-permute-start(f32[8,128]{1,0:T(8,128)S(1)} %pad_add_fusion.2), channel_id=1, source_target_pairs={{0,8},{1,17},{2,10},{3,19},{4,12},{5,21},{6,14},{7,23},{8,0},{9,25... | collective-permute-start | bytes 12296 | tf_op jit(solution)/shard_map/ppermute | solution.py:331
  21.0 4.6 %collective-permute-start.6 = (f32[8,128]{1,0:T(8,128)S(1)}, f32[8,128]{1,0:T(8,128)S(1)}, u32[]{:S(2)}, u32[]{:S(2)}) collective-permute-start(f32[8,128]{1,0:T(8,128)S(1)} %collective-permute-done.2.tile), channel_id=1, source_target_pairs={{0,16},{1,9},{2,18},{3,11},{4,20},{5,13},{6,22},{7,15},{8,24},{9,1... | collective-permute-start | bytes 12296 | tf_op jit(solution)/shard_map/ppermute | solution.py:332

commit v8 on v5

--- a/solution.py
+++ b/solution.py
@@ -368,7 +368,6 @@
         [pltpu.VMEM((owners * width, rows * side, side), F32), *m_scratch],
         one * 4 // 3,
     )
-    inv_1, s_own = lax.optimization_barrier((inv_1, s_own))
     inv_3 = lax.ppermute(inv_1, ("row", "col"), swap(False))
     tile_1 = lax.ppermute(tile, ("row", "col"), swap(True))
     tile_3 = lax.ppermute(tile_1, ("row", "col"), swap(False))

time: 28.2 us -> 28.2 us (level)
    ppermute x1, waiting for transfers between devices: 1.67 us -> 0.36 us  [local(): tile_1 = lax.ppermute(tile, ('row', 'col'), swap(True))]
    ppermute x1, waiting for transfers between devices: 5.18 us -> 6.48 us  [local(): inv_1 = lax.ppermute(inv_flat, ('row', 'col'), swap(True))]
where the time goes in v8:
time: 28.2 us; the launch traced here: 28.1 us
  starting transfers between devices  11.3 us (40%)
  waiting for transfers between devices  8.75 us (31%)
  Pallas kernels  6.34 us (22%)
  other arithmetic  1.34 us (5%)
    ppermute x1, waiting for transfers between devices, local(): inv_1 = lax.ppermute(inv_flat, ('row', 'col'), swap(True))  6.48 us
    pallas_call x6, Pallas kernels, call(): pl.pallas_call(kernel, out_shape=outs if len(outs) > 1 else outs[0], in_s...  6.34 us
    ppermute x1, starting transfers between devices, local(): inv_1 = lax.ppermute(inv_flat, ('row', 'col'), swap(True))  2.94 us
    ppermute x1, starting transfers between devices, local(): follow = lax.ppermute(div, 'col', backward)  2.84 us
    ppermute x1, starting transfers between devices, local(): tile_1 = lax.ppermute(tile, ('row', 'col'), swap(True))  2.38 us
    ppermute x1, starting transfers between devices, local(): inv_3 = lax.ppermute(inv_1, ('row', 'col'), swap(False))  1.98 us
    add x4, other arithmetic, noted(): out + jnp.pad(table.astype(F32), ((at, height - at - lines), (0, side - l...  1.32 us
    ppermute x1, waiting for transfers between devices, local(): tile_3 = lax.ppermute(tile_1, ('row', 'col'), swap(False))  1.08 us
  transfers between devices with their start and end apart: 7, of which 4 were waited for; matrix products, arithmetic and copies ran while one was open for 5% of the time, Pallas kernels for 17%

profile of v8, /device:TPU:0, one launch (start us, length us, event | category | flops | bytes accessed | tf_op | source)
XLA Modules:
  0.0 28.1 jit_solution(1482041521747324345)
XLA Ops:
  0.0 0.0 copy-start.1
  0.0 0.0 copy-start.2
  0.0 2.9 %collective-permute-start.1 = (f32[1280,128]{1,0:T(8,128)}, f32[1280,128]{1,0:T(8,128)S(1)}, u32[]{:S(2)}, u32[]{:S(2)}) collective-permute-start(f32[1280,128]{1,0:T(8,128)} %bitcast.9), channel_id=1, source_target_pairs={{0,8},{1,17},{2,10},{3,19},{4,12},{5,21},{6,14},{7,23},{8,0},{9,25... | collective-permute-start | bytes 1966088 | tf_op jit(solution)/shard_map/ppermute | solution.py:358
  2.9 0.0 copy-done.1
  2.9 0.0 copy-done.2
  3.0 0.0 copy-start.5
  3.0 0.0 copy-start
  3.0 1.3 %pad_add_fusion = f32[1544,128]{1,0:T(8,128)S(1)} fusion(f32[2,6]{1,0:T(2,128)S(1)} %convert_element_type.55, f32[2,6]{1,0:T(2,128)S(1)} %convert_element_type.54, f32[1536,128]{1,0:T(8,128)} %bitcast.8), kind=kLoop, calls=%fused_computation | loop fusion | flops 395264 | bytes 1577056 | tf_op jit(solution)/shard_map/add | solution.py:340
  4.2 0.0 copy-done.5
  4.3 0.0 copy-start.3
  4.3 0.2 dynamic_update_slice.3.div
  4.5 0.0 copy-start.6
  4.5 2.8 %collective-permute-start.4 = (f32[1544,128]{1,0:T(8,128)S(1)}, f32[1544,128]{1,0:T(8,128)S(1)}, u32[]{:S(2)}, u32[]{:S(2)}) collective-permute-start(f32[1544,128]{1,0:T(8,128)S(1)} %dynamic_update_slice.3.div), channel_id=1, source_target_pairs={{0,7},{1,0},{2,1},{3,2},{4,3},{5,4},{6,5},{7,6},{8,15},{9,8},{10,9... | collective-permute-start | bytes 2371592 | tf_op jit(solution)/shard_map/ppermute | solution.py:360
  7.3 0.0 collective-permute-start
  7.3 0.0 copy-done.3
  7.3 0.0 copy-done.6
  7.4 0.0 copy-done
  7.4 0.0 copy-start.4
  7.4 1.0 %collective-permute-start.3 = (f32[1288,128]{1,0:T(8,128)S(1)}, f32[1288,128]{1,0:T(8,128)S(1)}, u32[]{:S(2)}, u32[]{:S(2)}) collective-permute-start(f32[1288,128]{1,0:T(8,128)S(1)} %pad_add_fusion.1.inv), channel_id=1, source_target_pairs={{0,16},{1,9},{2,18},{3,11},{4,20},{5,13},{6,22},{7,15},{8,24},{9,1... | collective-permute-start | bytes 1978376 | tf_op jit(solution)/shard_map/ppermute | solution.py:359
  8.4 6.5 %collective-permute-done.1.inv = f32[1280,128]{1,0:T(8,128)S(1)} collective-permute-done((f32[1280,128]{1,0:T(8,128)}, f32[1280,128]{1,0:T(8,128)S(1)}, u32[]{:S(2)}, u32[]{:S(2)}) %collective-permute-start.1) | collective-permute-done | bytes 655392 | tf_op jit(solution)/shard_map/ppermute | solution.py:358
  14.9 2.0 %collective-permute-start.5 = (f32[1280,128]{1,0:T(8,128)S(1)}, f32[1280,128]{1,0:T(8,128)S(1)}, u32[]{:S(2)}, u32[]{:S(2)}) collective-permute-start(f32[1280,128]{1,0:T(8,128)S(1)} %collective-permute-done.1.inv), channel_id=1, source_target_pairs={{0,16},{1,9},{2,18},{3,11},{4,20},{5,13},{6,22},{7,15},{8,24},{9,1... | collective-permute-start | bytes 1966088 | tf_op jit(solution)/shard_map/ppermute | solution.py:371
  16.9 0.0 copy-start.7
  16.9 2.4 %collective-permute-start.2 = (f32[8,128]{1,0:T(8,128)S(1)}, f32[8,128]{1,0:T(8,128)S(1)}, u32[]{:S(2)}, u32[]{:S(2)}) collective-permute-start(f32[8,128]{1,0:T(8,128)S(1)} %pad_add_fusion.2), channel_id=1, source_target_pairs={{0,8},{1,17},{2,10},{3,19},{4,12},{5,21},{6,14},{7,23},{8,0},{9,25... | collective-permute-start | bytes 12296 | tf_op jit(solution)/shard_map/ppermute | solution.py:372
  19.3 0.0 copy-done.4
  19.3 0.0 copy-done.7
  19.3 1.3 %shard_map.91 = (bf16[4,256,256]{2,1,0:T(8,128)(2,1)S(1)}, bf16[4,256,256]{2,1,0:T(8,128)(2,1)S(1)}, bf16[256,768]{1,0:T(8,128)(2,1)S(1)}, bf16[256,768]{1,0:T(8,128)(2,1)S(1)}, f32[256,256]{1,0:T(8,128)S(1)}) custom-call(f32[1544,128]{1,0:T(8,128)S(1)} %dynamic_update_slice.3.div, f32[1288,128]{1,0:T(8,128)S(1)} %pad_add_fusion.1.inv), custom_call_target="tpu_custom_call" | custom-call | flops 402653184 | bytes 3547136 | tf_op jit(solution)/shard_map/pallas_call | solution.py:272
  20.6 0.4 %collective-permute-done.2.tile = f32[8,128]{1,0:T(8,128)S(1)} collective-permute-done((f32[8,128]{1,0:T(8,128)S(1)}, f32[8,128]{1,0:T(8,128)S(1)}, u32[]{:S(2)}, u32[]{:S(2)}) %collective-permute-start.2) | collective-permute-done | bytes 4128 | tf_op jit(solution)/shard_map/ppermute | solution.py:372
  21.0 0.1 collective-permute-start.6
  21.1 0.9 %shard_map.92 = (bf16[256,768]{1,0:T(8,128)(2,1)S(1)}, bf16[256,768]{1,0:T(8,128)(2,1)S(1)}, f32[256,256]{1,0:T(8,128)S(1)}) custom-call(f32[1280,128]{1,0:T(8,128)S(1)} %collective-permute-done.1.inv, f32[8,128]{1,0:T(8,128)S(1)} %collective-permute-done.2.tile, bf16[4,256,256]{2,1,0:T(8,128)(2,1)S(1)} %get-tuple-element.26.b_high, ...), custom_call_target="tpu_custom_call" | custom-call | flops 402653184 | bytes 3018752 | tf_op jit(solution)/shard_map/pallas_call | solution.py:272
  22.0 0.0 collective-permute-done.3.inv.tile
  22.0 0.9 %shard_map.93 = (bf16[256,768]{1,0:T(8,128)(2,1)S(1)}, bf16[256,768]{1,0:T(8,128)(2,1)S(1)}, f32[256,256]{1,0:T(8,128)S(1)}) custom-call(f32[1288,128]{1,0:T(8,128)S(1)} %collective-permute-done.3.inv.tile, f32[1288,128]{1,0:T(8,128)S(1)} %collective-permute-done.3.inv.tile, bf16[4,256,256]{2,1,0:T(8,128)(2,1)S(1)} %get-tuple-element.26.b_high, ...), custom_call_target="tpu_custom_call" | custom-call | flops 402653184 | bytes 3678208 | tf_op jit(solution)/shard_map/pallas_call | solution.py:272
  22.9 0.8 %collective-permute-done.4.div = f32[1544,128]{1,0:T(8,128)S(1)} collective-permute-done((f32[1544,128]{1,0:T(8,128)S(1)}, f32[1544,128]{1,0:T(8,128)S(1)}, u32[]{:S(2)}, u32[]{:S(2)}) %collective-permute-start.4) | collective-permute-done | bytes 790560 | tf_op jit(solution)/shard_map/ppermute | solution.py:360
  23.7 0.8 %shard_map.94 = (f32[256,256]{1,0:T(8,128)S(1)}, bf16[256,256]{1,0:T(8,128)(2,1)S(1)}, bf16[256,256]{1,0:T(8,128)(2,1)S(1)}, bf16[6,256,128]{2,1,0:T(8,128)(2,1)S(1)}, bf16[6,256,128]{2,1,0:T(8,128)(2,1)S(1)}) custom-call(bf16[256,768]{1,0:T(8,128)(2,1)S(1)} %get-tuple-element.24.y0_high, bf16[256,768]{1,0:T(8,128)(2,1)S(1)} %get-tuple-element.25.y0_low, ...), custom_call_target="tpu_custom_call" | custom-call | flops 301989888 | bytes 4460544 | tf_op jit(solution)/shard_map/pallas_call | solution.py:272
  24.5 1.1 %collective-permute-done.6.tile = f32[8,128]{1,0:T(8,128)S(1)} collective-permute-done((f32[8,128]{1,0:T(8,128)S(1)}, f32[8,128]{1,0:T(8,128)S(1)}, u32[]{:S(2)}, u32[]{:S(2)}) %collective-permute-start.6) | collective-permute-done | bytes 4128 | tf_op jit(solution)/shard_map/ppermute | solution.py:373
  25.6 0.0 collective-permute-done.5.inv
  25.6 1.0 %shard_map.95 = (f32[2,3,128,128]{3,2,1,0:T(8,128)S(1)}, bf16[2,256,128]{2,1,0:T(8,128)(2,1)S(1)}, bf16[2,256,128]{2,1,0:T(8,128)(2,1)S(1)}) custom-call(f32[1280,128]{1,0:T(8,128)S(1)} %collective-permute-done.5.inv, f32[8,128]{1,0:T(8,128)S(1)} %collective-permute-done.6.tile, f32[8,128]{1,0:T(8,128)S(1)} %pad_add_fusion.3.div.own, ...), custom_call_target="tpu_custom_call" | custom-call | flops 503316480 | bytes 3153920 | tf_op jit(solution)/shard_map/pallas_call | solution.py:272
  26.6 0.0 collective-permute-done.div
  26.6 1.5 %shard_map.96 = f32[2,4,128,128]{3,2,1,0:T(8,128)} custom-call(f32[1544,128]{1,0:T(8,128)S(1)} %collective-permute-done.div, f32[8,128]{1,0:T(8,128)S(1)} %pad_add_fusion.3.div.own, bf16[6,256,128]{2,1,0:T(8,128)(2,1)S(1)} %get-tuple-element.34.p_high, bf16[6,256,128]{2,1,0:T(8,128)(2,1)S(1)} %get-tuple-element.35.p_low, ...), custom_call_target="tpu_custom_call" | custom-call | flops 301989888 | bytes 2760704 | tf_op jit(solution)/shard_map/pallas_call | solution.py:272
  (10 shorter events, 0.1 us)
Async XLA Ops:
  0.0 2.9 %copy-start.1 = (s32[2,6]{1,0:T(2,128)S(1)}, s32[2,6]{1,0:T(2,128)}, u32[]{:S(2)}) copy-start(s32[2,6]{1,0:T(2,128)} %param.10) | copy-start | bytes 148
  0.0 2.9 %copy-start.2 = (s32[2,6]{1,0:T(2,128)S(1)}, s32[2,6]{1,0:T(2,128)}, u32[]{:S(2)}) copy-start(s32[2,6]{1,0:T(2,128)} %param.11) | copy-start | bytes 148
  0.0 14.9 %collective-permute-start.1 = (f32[1280,128]{1,0:T(8,128)}, f32[1280,128]{1,0:T(8,128)S(1)}, u32[]{:S(2)}, u32[]{:S(2)}) collective-permute-start(f32[1280,128]{1,0:T(8,128)} %bitcast.9), channel_id=1, source_target_pairs={{0,8},{1,17},{2,10},{3,19},{4,12},{5,21},{6,14},{7,23},{8,0},{9,25... | collective-permute-start | bytes 1966088 | tf_op jit(solution)/shard_map/ppermute | solution.py:358
  3.0 1.3 %copy-start.5 = (s32[2]{0:T(128)S(1)}, s32[2]{0:T(128)}, u32[]{:S(2)}) copy-start(s32[2]{0:T(128)} %param.12) | copy-start | bytes 28
  3.0 4.4 %copy-start = (f32[2,5,128,128]{3,2,1,0:T(8,128)S(1)}, f32[2,5,128,128]{3,2,1,0:T(8,128)}, u32[]{:S(2)}) copy-start(f32[2,5,128,128]{3,2,1,0:T(8,128)} %param.13) | copy-start | bytes 1966084
  4.3 3.1 %copy-start.3 = (s32[2,5]{1,0:T(2,128)S(1)}, s32[2,5]{1,0:T(2,128)}, u32[]{:S(2)}) copy-start(s32[2,5]{1,0:T(2,128)} %param.14) | copy-start | bytes 124
  4.5 2.9 %copy-start.6 = (s32[2]{0:T(128)S(1)}, s32[2]{0:T(128)}, u32[]{:S(2)}) copy-start(s32[2]{0:T(128)} %param.15) | copy-start | bytes 28
  4.5 19.2 %collective-permute-start.4 = (f32[1544,128]{1,0:T(8,128)S(1)}, f32[1544,128]{1,0:T(8,128)S(1)}, u32[]{:S(2)}, u32[]{:S(2)}) collective-permute-start(f32[1544,128]{1,0:T(8,128)S(1)} %dynamic_update_slice.3.div), channel_id=1, source_target_pairs={{0,7},{1,0},{2,1},{3,2},{4,3},{5,4},{6,5},{7,6},{8,15},{9,8},{10,9... | collective-permute-start | bytes 2371592 | tf_op jit(solution)/shard_map/ppermute | solution.py:360
  7.3 19.3 %collective-permute-start = (f32[1544,128]{1,0:T(8,128)S(1)}, f32[1544,128]{1,0:T(8,128)S(1)}, u32[]{:S(2)}, u32[]{:S(2)}) collective-permute-start(f32[1544,128]{1,0:T(8,128)S(1)} %dynamic_update_slice.3.div), channel_id=1, source_target_pairs={{0,1},{1,2},{2,3},{3,4},{4,5},{5,6},{6,7},{7,0},{8,9},{9,10},{10,1... | collective-permute-start | bytes 2371592 | tf_op jit(solution)/shard_map/ppermute | solution.py:361
  7.4 11.9 %copy-start.4 = (s32[2,4]{1,0:T(2,128)S(1)}, s32[2,4]{1,0:T(2,128)}, u32[]{:S(2)}) copy-start(s32[2,4]{1,0:T(2,128)} %param.16) | copy-start | bytes 100
  7.4 14.6 %collective-permute-start.3 = (f32[1288,128]{1,0:T(8,128)S(1)}, f32[1288,128]{1,0:T(8,128)S(1)}, u32[]{:S(2)}, u32[]{:S(2)}) collective-permute-start(f32[1288,128]{1,0:T(8,128)S(1)} %pad_add_fusion.1.inv), channel_id=1, source_target_pairs={{0,16},{1,9},{2,18},{3,11},{4,20},{5,13},{6,22},{7,15},{8,24},{9,1... | collective-permute-start | bytes 1978376 | tf_op jit(solution)/shard_map/ppermute | solution.py:359
  14.9 10.6 %collective-permute-start.5 = (f32[1280,128]{1,0:T(8,128)S(1)}, f32[1280,128]{1,0:T(8,128)S(1)}, u32[]{:S(2)}, u32[]{:S(2)}) collective-permute-start(f32[1280,128]{1,0:T(8,128)S(1)} %collective-permute-done.1.inv), channel_id=1, source_target_pairs={{0,16},{1,9},{2,18},{3,11},{4,20},{5,13},{6,22},{7,15},{8,24},{9,1... | collective-permute-start | bytes 1966088 | tf_op jit(solution)/shard_map/ppermute | solution.py:371
  16.9 2.4 %copy-start.7 = (s32[2]{0:T(128)S(1)}, s32[2]{0:T(128)}, u32[]{:S(2)}) copy-start(s32[2]{0:T(128)} %param.17) | copy-start | bytes 28
  16.9 4.1 %collective-permute-start.2 = (f32[8,128]{1,0:T(8,128)S(1)}, f32[8,128]{1,0:T(8,128)S(1)}, u32[]{:S(2)}, u32[]{:S(2)}) collective-permute-start(f32[8,128]{1,0:T(8,128)S(1)} %pad_add_fusion.2), channel_id=1, source_target_pairs={{0,8},{1,17},{2,10},{3,19},{4,12},{5,21},{6,14},{7,23},{8,0},{9,25... | collective-permute-start | bytes 12296 | tf_op jit(solution)/shard_map/ppermute | solution.py:372
  21.0 4.6 %collective-permute-start.6 = (f32[8,128]{1,0:T(8,128)S(1)}, f32[8,128]{1,0:T(8,128)S(1)}, u32[]{:S(2)}, u32[]{:S(2)}) collective-permute-start(f32[8,128]{1,0:T(8,128)S(1)} %collective-permute-done.2.tile), channel_id=1, source_target_pairs={{0,16},{1,9},{2,18},{3,11},{4,20},{5,13},{6,22},{7,15},{8,24},{9,1... | collective-permute-start | bytes 12296 | tf_op jit(solution)/shard_map/ppermute | solution.py:373
